TPU v7x, 32 devices: a whole 2x2x4 slice. The times are simulated.
32 devices in a mesh: pix: 16 (over z, x, core), col: 2 (over y).
Axes of the slice: x: 2, y: 2, z: 4, core: 2. Of those that a mesh axis runs over, the one named last changes fastest.
Arguments:
- observed: float32 [4096, 4096], P('pix', 'col'), may hold values from -40 to 40
- valid_mask: int32 [4096, 512], P('pix', 'col'), may hold values 0 or 1
- pix_factor: float32 [4096, 256], P('pix'), may hold values from -6 to 6
- col_factor: float32 [4096, 256], P('col'), may hold values from -0.375 to 0.375
Outputs:
- pix_next: float32 [4096, 256], P('pix')
- col_next: float32 [4096, 256], P('col')
- cloud: float32 [4096, 4096], P('pix', 'col')
All inputs are finite; a program needn't handle non-finite values. No bound on the sum of `valid_mask` on one device may be relied on, other than what follows from the above.
Results may differ from a plain program's by a relative error of at most 0.0003.
Values sent between devices are 32-bit elements; how exact they have to be, the bound alone decides.
No kernel may reach another device: no remote copies, remote signals or barrier semaphores. Data moves between devices by JAX's collectives and lax.ppermute only.
A program may use at most 64 MiB of HBM per device.

v0:
```python
import jax
import jax.numpy as jnp
from jax import lax
from jax.sharding import PartitionSpec as P

BANDS = 8
WIDTH = 256
ITERS = 2
PASSES = 2


highest = lax.Precision.HIGHEST
threshold_scale = 1.0
diffusion = 0.2


def passed_along(block, axis, distance):
    devices = range(lax.axis_size(axis))
    route = [(i - distance, i) for i in devices if i - distance in devices]
    return lax.ppermute(block, axis, route)


def soft_cut(values, level):
    return jnp.sign(values) * jnp.maximum(jnp.abs(values) - level, 0.0)


def flux_of(diff, level):
    return diff / (1.0 + (diff / level) ** 2)


def level_of(residual, weight, total):
    spread = lax.psum(jnp.sum(weight * residual * residual), ("pix", "col"))
    return threshold_scale * jnp.sqrt(spread / total + 1e-06)


def smooth_pass(grid, level, strip_index, pix_count):
    has_north = strip_index > 0
    has_south = strip_index < pix_count - 1
    top_row = grid[0]
    bottom_row = grid[-1]
    north_rim = passed_along(bottom_row, "pix", 1)
    south_rim = passed_along(top_row, "pix", -1)
    north_rim = jnp.where(has_north, north_rim, top_row)
    south_rim = jnp.where(has_south, south_rim, bottom_row)
    north = jnp.concatenate([north_rim[None], grid[:-1]], axis=0)
    south = jnp.concatenate([grid[1:], south_rim[None]], axis=0)
    west = jnp.concatenate([grid[:, :1], grid[:, :-1]], axis=1)
    east = jnp.concatenate([grid[:, 1:], grid[:, -1:]], axis=1)
    summed = flux_of(north - grid, level) + flux_of(south - grid, level)
    summed = summed + flux_of(west - grid, level) + flux_of(east - grid, level)
    return grid + diffusion * summed


def per_device(observed, valid_mask, pix_factor, col_factor):
    pix_count = lax.axis_size("pix")
    col_count = lax.axis_size("col")
    pixels, columns = observed.shape
    dates = valid_mask.shape[1]
    weight = jnp.broadcast_to(
        valid_mask.astype(jnp.float32)[:, :, None], (pixels, dates, BANDS)
    ).reshape(pixels, columns)
    total = float(pixels * columns * pix_count * col_count)
    pix_fac = pix_factor
    col_fac = col_factor
    low_rank = jnp.dot(pix_fac, col_fac.T, precision=highest)
    for iteration in range(ITERS):
        residual = observed - low_rank
        level = level_of(residual, weight, total)
        sparse = weight * soft_cut(residual, level)
        misfit = weight * (sparse - residual)
        pix_grad = lax.psum(jnp.dot(misfit, col_fac, precision=highest), "col")
        change = jnp.dot(pix_grad, col_fac.T, precision=highest)
        norm_local = jnp.sum(pix_grad * pix_grad)
        curve_local = jnp.sum(weight * change * change)
        top_sum, bottom_sum = lax.psum((norm_local / col_count, curve_local), ("pix", "col"))
        step_pix = top_sum / bottom_sum
        pix_fac = pix_fac - step_pix * pix_grad
        low_rank = low_rank - step_pix * change
        misfit = weight * (sparse - (observed - low_rank))
        local_grad = lax.dot_general(
            misfit,
            pix_fac,
            (((0,), (0,)), ((), ())),
            precision=highest,
            preferred_element_type=jnp.float32,
        )
        col_grad = lax.psum(local_grad, "pix")
        shifted = jnp.dot(pix_fac, col_grad.T, precision=highest)
        norm_local = jnp.sum(col_grad * col_grad)
        curve_local = jnp.sum(weight * shifted * shifted)
        top_sum, bottom_sum = lax.psum((norm_local / pix_count, curve_local), ("pix", "col"))
        step_col = top_sum / bottom_sum
        col_fac = col_fac - step_col * col_grad
        low_rank = low_rank - step_col * shifted
    residual = observed - low_rank
    level = level_of(residual, weight, total)
    layer = weight * soft_cut(residual, level)
    strip_index = lax.axis_index("pix")
    grid = layer.reshape(pixels // WIDTH, WIDTH, columns)
    for sweep_index in range(PASSES):
        grid = smooth_pass(grid, level, strip_index, pix_count)
    return (pix_fac, col_fac, grid.reshape(pixels, columns))


def solution(mesh):
    in_specs = (P("pix", "col"), P("pix", "col"), P("pix", None), P("col", None))
    out_specs = (P("pix", None), P("col", None), P("pix", "col"))
    return jax.shard_map(
        per_device, mesh=mesh, in_specs=in_specs, out_specs=out_specs, check_vma=False
    )
```

profile of v0, /device:TPU:13, one launch (start us, length us, event | category | flops | bytes accessed | tf_op | source)
XLA Modules:
  0.0 770.9 jit_solution(11350688591858291630)
XLA Ops:
  11.8 7.0 fusion
  18.7 39.9 %psum.105 = f32[]{:T(128)} all-reduce(f32[]{:T(128)} %get-tuple-element.16), channel_id=1, replica_groups=mesh['pix'=16,'col'=2] {'pix','col'}, use_global_device_ids=true, to_apply=%region_1.0 | all-reduce | flops 1 | bytes 8 | tf_op jit(solution)/shard_map/psum | solution.py:32
  59.3 5.7 fusion.20
  65.1 22.6 %all-reduce.9.cloned.1.call-done = f32[256,256]{1,0:T(8,128)} async-done(((f32[256,256]{1,0:T(8,128)}), f32[256,256]{1,0:T(8,128)}) %all-reduce.9.cloned.1.call-update) | async-done | bytes 262160 | tf_op jit(solution)/shard_map/psum | solution.py:71
  90.0 5.6 fusion.1
  95.6 41.3 %all-reduce.3 = (f32[]{:T(128)}, f32[]{:T(128)}) all-reduce(f32[]{:T(128)S(6)} %div.106, f32[]{:T(128)} %get-tuple-element.27), channel_id=1, replica_groups=mesh['pix'=16,'col'=2] {'pix','col'}, use_global_device_ids=true, to_apply=%region_4.0 | all-reduce | flops 2 | bytes 16 | tf_op jit(solution)/shard_map/psum | solution.py:75
  138.3 9.0 %fusion.16 = f32[2048,256]{1,0:T(8,128)} fusion(f32[256,256]{1,0:T(8,128)S(1)} %multiply_subtract_fusion.8, f32[256,2048]{1,0:T(8,128)S(1)} %copy.10, f32[256,2048]{1,0:T(8,128)} %param.4, f32[256,2048]{1,0:T(8,128)} %get-tuple-element.17, f32[]{:T(128)S(6)} %sqrt.9, f32[256,2048]{1,0:T(8,128)} %get-tuple-element.26, f32[256,2048]{1,0:T(8,128)} %get-tuple-element.28, ...), kind=kOutput, calls=%fused_computation.46 | convolution fusion | flops 1616379904 | bytes 12845064 | tf_op jit(solution)/shard_map/dot_general | solution.py:80
  147.3 97.4 %all-reduce.11.cloned.1.call-done = f32[2048,256]{1,0:T(8,128)} async-done(((f32[2048,256]{1,0:T(8,128)}), f32[2048,256]{1,0:T(8,128)}) %all-reduce.11.cloned.1.call-update) | async-done | bytes 2097168 | tf_op jit(solution)/shard_map/psum | solution.py:87
  248.1 5.5 fusion.2
  253.5 40.1 %all-reduce.2 = (f32[]{:T(128)}, f32[]{:T(128)}) all-reduce(f32[]{:T(128)S(6)} %div.108, f32[]{:T(128)} %get-tuple-element.29), channel_id=1, replica_groups=mesh['pix'=16,'col'=2] {'pix','col'}, use_global_device_ids=true, to_apply=%region_9.0 | all-reduce | flops 2 | bytes 16 | tf_op jit(solution)/shard_map/psum | solution.py:91
  294.9 7.4 fusion.3
  302.4 40.6 %psum.112 = f32[]{:T(128)} all-reduce(f32[]{:T(128)} %get-tuple-element.13), channel_id=1, replica_groups=mesh['pix'=16,'col'=2] {'pix','col'}, use_global_device_ids=true, to_apply=%region_13.0 | all-reduce | flops 1 | bytes 8 | tf_op jit(solution)/shard_map/psum | solution.py:32
  351.3 22.7 %all-reduce.13.cloned.1.call-done = f32[256,256]{1,0:T(8,128)} async-done(((f32[256,256]{1,0:T(8,128)}), f32[256,256]{1,0:T(8,128)}) %all-reduce.13.cloned.1.call-update) | async-done | bytes 262160 | tf_op jit(solution)/shard_map/psum | solution.py:71
  376.2 5.6 fusion.4
  381.8 41.4 %all-reduce.1 = (f32[]{:T(128)}, f32[]{:T(128)}) all-reduce(f32[]{:T(128)S(6)} %div.111, f32[]{:T(128)} %get-tuple-element.31), channel_id=1, replica_groups=mesh['pix'=16,'col'=2] {'pix','col'}, use_global_device_ids=true, to_apply=%region_16.0 | all-reduce | flops 2 | bytes 16 | tf_op jit(solution)/shard_map/psum | solution.py:75
  424.5 9.1 %fusion.7 = f32[2048,256]{1,0:T(8,128)} fusion(f32[256,256]{1,0:T(8,128)S(1)} %multiply_subtract_fusion.7, f32[256,2048]{1,0:T(8,128)S(1)} %copy.10, f32[256,2048]{1,0:T(8,128)} %param.4, f32[256,2048]{1,0:T(8,128)} %get-tuple-element.14, f32[]{:T(128)S(6)} %sqrt.10, f32[256,2048]{1,0:T(8,128)} %get-tuple-element.15, f32[256,2048]{1,0:T(8,128)} %get-tuple-element.32, ...), kind=kOutput, calls=%fused_computation.32 | convolution fusion | flops 1616379904 | bytes 12845064 | tf_op jit(solution)/shard_map/dot_general | solution.py:80
  433.7 97.4 %all-reduce.15.cloned.1.call-done = f32[2048,256]{1,0:T(8,128)} async-done(((f32[2048,256]{1,0:T(8,128)}), f32[2048,256]{1,0:T(8,128)}) %all-reduce.15.cloned.1.call-update) | async-done | bytes 2097168 | tf_op jit(solution)/shard_map/psum | solution.py:87
  534.4 5.5 fusion.5
  539.9 40.1 %all-reduce = (f32[]{:T(128)}, f32[]{:T(128)}) all-reduce(f32[]{:T(128)S(6)} %div.113, f32[]{:T(128)} %get-tuple-element.33), channel_id=1, replica_groups=mesh['pix'=16,'col'=2] {'pix','col'}, use_global_device_ids=true, to_apply=%region_21.0 | all-reduce | flops 2 | bytes 16 | tf_op jit(solution)/shard_map/psum | solution.py:91
  581.3 6.5 fusion.6
  587.8 40.4 %psum.119 = f32[]{:T(128)} all-reduce(f32[]{:T(128)} %get-tuple-element.11), channel_id=1, replica_groups=mesh['pix'=16,'col'=2] {'pix','col'}, use_global_device_ids=true, to_apply=%region_25.0 | all-reduce | flops 1 | bytes 8 | tf_op jit(solution)/shard_map/psum | solution.py:32
  642.7 40.7 %collective-permute-done.1 = f32[256,2048]{1,0:T(8,128)S(1)} collective-permute-done((f32[256,2048]{1,0:T(8,128)}, f32[256,2048]{1,0:T(8,128)S(1)}, u32[]{:S(2)}, u32[]{:S(2)}) %collective-permute-start.1) | collective-permute-done | bytes 2097184 | tf_op jit(solution)/shard_map/ppermute | solution.py:20
  683.4 22.2 %collective-permute-done = f32[256,2048]{1,0:T(8,128)} collective-permute-done((f32[256,2048]{1,0:T(8,128)}, f32[256,2048]{1,0:T(8,128)}, u32[]{:S(2)}, u32[]{:S(2)}) %collective-permute-start) | collective-permute-done | bytes 2097184 | tf_op jit(solution)/shard_map/ppermute | solution.py:20
  718.4 42.2 %collective-permute-done.3 = f32[256,2048]{1,0:T(8,128)S(1)} collective-permute-done((f32[256,2048]{1,0:T(8,128)S(1)}, f32[256,2048]{1,0:T(8,128)S(1)}, u32[]{:S(2)}, u32[]{:S(2)}) %collective-permute-start.3) | collective-permute-done | bytes 2097184 | tf_op jit(solution)/shard_map/ppermute | solution.py:20
  (51 shorter events, 50.9 us)
Async XLA Ops:
  7.2 80.6 %all-reduce.9.cloned.1.call-start = ((), (), s32[]{:S(2)}) async-start(), calls=%async_computation | async-start | bytes 524288 | tf_op jit(solution)/shard_map/psum | solution.py:71
  9.8 2.0 copy-start.8
  65.0 179.6 %all-reduce.11.cloned.1.call-start = ((), (), s32[]{:S(2)}) async-start(), calls=%async_computation.1 | async-start | bytes 4194304 | tf_op jit(solution)/shard_map/psum | solution.py:87
  90.0 48.2 %copy-start.6 = (f32[256,256]{1,0:T(8,128)S(1)}, f32[256,256]{1,0:T(8,128)}, u32[]{:S(2)}) copy-start(f32[256,256]{1,0:T(8,128)} %all-reduce.9.cloned.1.call-done) | copy-start | bytes 786436
  147.3 226.7 %all-reduce.13.cloned.1.call-start = ((), (), s32[]{:S(2)}) async-start(), calls=%async_computation.2 | async-start | bytes 524288 | tf_op jit(solution)/shard_map/psum | solution.py:71
  343.7 4.0 copy-start.3
  346.3 1.4 copy-start
  351.2 179.8 %all-reduce.15.cloned.1.call-start = ((), (), s32[]{:S(2)}) async-start(), calls=%async_computation.3 | async-start | bytes 4194304 | tf_op jit(solution)/shard_map/psum | solution.py:87
  376.2 48.3 %copy-start.5 = (f32[256,256]{1,0:T(8,128)S(1)}, f32[256,256]{1,0:T(8,128)}, u32[]{:S(2)}) copy-start(f32[256,256]{1,0:T(8,128)} %all-reduce.13.cloned.1.call-done) | copy-start | bytes 786436
  424.5 109.9 %copy-start.4 = (f32[256,256]{1,0:T(8,128)}, f32[256,256]{1,0:T(8,128)S(1)}, u32[]{:S(2)}) copy-start(f32[256,256]{1,0:T(8,128)S(1)} %multiply_subtract_fusion.7) | copy-start | bytes 786436
  632.6 50.8 %collective-permute-start.1 = (f32[256,2048]{1,0:T(8,128)}, f32[256,2048]{1,0:T(8,128)S(1)}, u32[]{:S(2)}, u32[]{:S(2)}) collective-permute-start(f32[256,2048]{1,0:T(8,128)} %multiply_multiply_fusion.7), channel_id=1, source_target_pairs={{2,0},{4,2},{6,4},{8,6},{10,8},{12,10},{14,12},{16,14},{18,16},{20... | collective-permute-start | bytes 6291464 | tf_op jit(solution)/shard_map/ppermute | solution.py:20
  636.8 68.8 %collective-permute-start = (f32[256,2048]{1,0:T(8,128)}, f32[256,2048]{1,0:T(8,128)}, u32[]{:S(2)}, u32[]{:S(2)}) collective-permute-start(f32[256,2048]{1,0:T(8,128)} %multiply_multiply_fusion.7), channel_id=1, source_target_pairs={{0,2},{2,4},{4,6},{6,8},{8,10},{10,12},{12,14},{14,16},{16,18},{18... | collective-permute-start | bytes 6291464 | tf_op jit(solution)/shard_map/ppermute | solution.py:20
  683.4 22.2 %copy-start.7 = (f32[256,2048]{1,0:T(8,128)}, f32[256,2048]{1,0:T(8,128)S(1)}, u32[]{:S(2)}) copy-start(f32[256,2048]{1,0:T(8,128)S(1)} %collective-permute-done.1) | copy-start | bytes 6291460
  705.6 10.7 %copy-start.1 = (f32[2048,256]{1,0:T(8,128)S(1)}, f32[2048,256]{1,0:T(8,128)}, u32[]{:S(2)}) copy-start(f32[2048,256]{1,0:T(8,128)} %copy-done) | copy-start | bytes 6291460
  705.6 10.7 %copy-start.2 = (f32[2048,256]{1,0:T(8,128)S(1)}, f32[2048,256]{1,0:T(8,128)}, u32[]{:S(2)}) copy-start(f32[2048,256]{1,0:T(8,128)} %all-reduce.15.cloned.1.call-done) | copy-start | bytes 6291460
  710.0 50.6 %collective-permute-start.3 = (f32[256,2048]{1,0:T(8,128)S(1)}, f32[256,2048]{1,0:T(8,128)S(1)}, u32[]{:S(2)}, u32[]{:S(2)}) collective-permute-start(f32[256,2048]{1,0:T(8,128)S(1)} %multiply_add_fusion.1), channel_id=1, source_target_pairs={{2,0},{4,2},{6,4},{8,6},{10,8},{12,10},{14,12},{16,14},{18,16},{20... | collective-permute-start | bytes 6291464 | tf_op jit(solution)/shard_map/ppermute | solution.py:20
  711.9 48.6 %collective-permute-start.2 = (f32[256,2048]{1,0:T(8,128)S(1)}, f32[256,2048]{1,0:T(8,128)S(1)}, u32[]{:S(2)}, u32[]{:S(2)}) collective-permute-start(f32[256,2048]{1,0:T(8,128)S(1)} %multiply_add_fusion.1), channel_id=1, source_target_pairs={{0,2},{2,4},{4,6},{6,8},{8,10},{10,12},{12,14},{14,16},{16,18},{18... | collective-permute-start | bytes 6291464 | tf_op jit(solution)/shard_map/ppermute | solution.py:20
Sparse Core Ops, SparseCore 0:
  65.2 22.5 all-reduce.8
  147.4 97.2 all-reduce.10
  351.3 22.5 all-reduce.12
  433.8 97.2 all-reduce.14
where the time goes:
time: 779 us; the launch traced here: 771 us
  waiting for transfers between devices  345 us (44%)
  blocking collectives  284 us (36%)
  matrix products  56.5 us (7%)
  other arithmetic  39.3 us (5%)
  between operations  24.3 us (3%)
  starting transfers between devices  13.1 us (2%)
  local copies, waits for them, and re-layouts  8.81 us (1%)
    psum x2, waiting for transfers between devices, per_device(): col_grad = lax.psum(local_grad, 'pix')  195 us
    psum x3, blocking collectives, level_of(): spread = lax.psum(jnp.sum(weight * residual * residual), ('pix', 'col'))  121 us
    ppermute x4, waiting for transfers between devices, passed_along(): return lax.ppermute(block, axis, route)  105 us
    psum x2, blocking collectives, per_device(): lax.psum((norm_local / col_count, curve_local), ('pix', 'col'))  82.7 us
    psum x2, blocking collectives, per_device(): lax.psum((norm_local / pix_count, curve_local), ('pix', 'col'))  80.2 us
    psum x2, waiting for transfers between devices, per_device(): pix_grad = lax.psum(jnp.dot(misfit, col_fac, precision=highest), 'col')  45.3 us
    dot_general x2, matrix products, per_device(): lax.dot_general(misfit, pix_fac, (((0,), (0,)), ((), ())), precision=high...  18.1 us
  transfers between devices with their start and end apart: 8, of which 7 were waited for; matrix products, arithmetic and copies ran while one was open for 1% of the time, Pallas kernels for 0%

commit v1 on v0

v1 whole, which is shorter than its diff:
```python
import functools

import jax
import jax.numpy as jnp
from jax import lax
from jax.experimental import pallas as pl
from jax.experimental.pallas import tpu as pltpu
from jax.sharding import PartitionSpec as P

BANDS = 8
WIDTH = 256
ITERS = 2
PASSES = 2
LANES = 128
GROUP = 8

threshold_scale = 1.0
diffusion = 0.2
f32 = jnp.float32
bf16 = jnp.bfloat16


def along_pix(block, distance):
    count = lax.axis_size("pix")
    return lax.ppermute(block, "pix", [(i, i ^ distance) for i in range(count)])


def to_chip(block, distance, crossed):
    count = lax.axis_size("pix")
    route = [(i, (i ^ crossed) + 2 * distance) for i in range(count)]
    route = [(a, b) for a, b in route if 0 <= b < count]
    return lax.ppermute(block, "pix", route)


def summed_over_col(block):
    count = lax.axis_size("col")
    step = 1
    while step < count:
        block = block + lax.ppermute(block, "col", [(i, i ^ step) for i in range(count)])
        step *= 2
    return block


def everywhere(rows):
    return lax.all_to_all(rows, ("pix", "col"), 0, 0, tiled=True)


def halves(x):
    high = x.astype(bf16)
    return high, (x - high.astype(f32)).astype(bf16)


def product(a, b, dims=((1,), (0,))):
    def part(x, y):
        return lax.dot_general(x, y, (dims, ((), ())), preferred_element_type=f32)

    return part(a[0], b[0]) + (part(a[0], b[1]) + part(a[1], b[0]))


def rows_folded(x):
    return jnp.sum(x.reshape(x.shape[0] // 8, 8, x.shape[1]), axis=0)


def whole_sum(x):
    return jnp.sum(jnp.sum(x, axis=0, keepdims=True), axis=1, keepdims=True)


def packed_sums(shape, sums):
    lane = lax.broadcasted_iota(jnp.int32, shape, 1)
    packed = jnp.zeros(shape, f32)
    for place, value in enumerate(sums):
        packed = packed + jnp.where(lane == place, value, 0.0)
    return packed


def read_sums(ref, count):
    total = jnp.sum(ref[...], axis=0, keepdims=True)
    return [total[:, k : k + 1] for k in range(count)]


def spread_mask(mask, chunk):
    dates = mask.shape[1]
    date = lax.broadcasted_iota(jnp.int32, (dates, LANES), 0)
    lane = lax.broadcasted_iota(jnp.int32, (dates, LANES), 1)
    pick = (date == chunk * (LANES // BANDS) + lane // BANDS).astype(bf16)
    return jnp.dot(mask.astype(bf16), pick, preferred_element_type=f32)


def call(kernel, grid, in_specs, out_specs, out_shape, scratch, place, *args):
    return pl.pallas_call(
        kernel,
        grid_spec=pltpu.PrefetchScalarGridSpec(
            num_scalar_prefetch=1,
            grid=grid,
            in_specs=in_specs,
            out_specs=out_specs,
            scratch_shapes=scratch,
        ),
        out_shape=out_shape,
        compiler_params=pltpu.CompilerParams(vmem_limit_bytes=48 * 2**20),
    )(place, *args)


def whole(shape):
    return pl.BlockSpec(shape, lambda t, s: (0,) * len(shape))


def tile(rows, cols):
    return pl.BlockSpec((rows, cols), lambda t, s: (0, t))


def shaped(*shape):
    return jax.ShapeDtypeStruct(shape, f32)


def start_kernel(place, own_obs, own_mask, other_obs, other_mask, own_u, other_u, v_ref,
                 res_ref, weight_ref, vt_ref, sums_ref, u_high, u_low, acc):
    step = pl.program_id(0)
    chunk = place[1] ^ step
    pixels = own_u.shape[0]

    @pl.when(step == 0)
    def _():
        for part, ref in enumerate((own_u, other_u)):
            high, low = halves(ref[...])
            u_high[part * pixels : (part + 1) * pixels] = high
            u_low[part * pixels : (part + 1) * pixels] = low
        acc[...] = jnp.zeros_like(acc)

    vt = v_ref[...].T
    vt_ref[...] = vt
    low_rank = product((u_high[...], u_low[...]), halves(vt))
    for part, (obs, mask) in enumerate(((own_obs, own_mask), (other_obs, other_mask))):
        rows = slice(part * pixels, (part + 1) * pixels)
        weight = spread_mask(mask[...], chunk)
        res = weight * (obs[...] - low_rank[rows])
        weight_ref[rows] = weight
        res_ref[rows] = res
        acc[...] += rows_folded(res * res)

    @pl.when(step == pl.num_programs(0) - 1)
    def _():
        sums_ref[...] = packed_sums(sums_ref.shape, [whole_sum(acc[...])])


def level_from(spread, total):
    return threshold_scale * jnp.sqrt(jnp.maximum(spread, 0.0) / total + 1e-06)


def first_grad_kernel(total, place, sums_ref, res_ref, vt_ref, grad_ref):
    step = pl.program_id(0)
    (spread,) = read_sums(sums_ref, 1)
    level = level_from(spread, total)
    misfit = -jnp.clip(res_ref[...], -level, level)
    part = product(halves(misfit), halves(vt_ref[...]), ((1,), (1,)))

    @pl.when(step == 0)
    def _():
        grad_ref[...] = part

    @pl.when(step > 0)
    def _():
        grad_ref[...] += part


def column_sums(sums):
    top, curve, cross, before = sums
    step = top / curve
    return step, before + 2.0 * step * cross + step * step * curve


def next_grad_kernel(total, place, sums_ref, res_ref, shift_ref, vt_ref, even_ref, odd_ref,
                     res_out, vt_out, grad_ref):
    step = pl.program_id(0)
    size, spread = column_sums(read_sums(sums_ref, 4))
    level = level_from(spread, total)
    grad = jnp.concatenate([even_ref[0], odd_ref[0]], axis=1)
    vt = vt_ref[...] - size * grad
    vt_out[...] = vt
    res = res_ref[...] + size * shift_ref[...]
    res_out[...] = res
    misfit = -jnp.clip(res, -level, level)
    part = product(halves(misfit), halves(vt), ((1,), (1,)))

    @pl.when(step == 0)
    def _():
        grad_ref[...] = part

    @pl.when(step > 0)
    def _():
        grad_ref[...] += part


def change_kernel(col_count, place, own_grad, other_grad, vt_ref, weight_ref,
                  change_ref, sums_ref, g_high, g_low, acc):
    step = pl.program_id(0)
    pixels = own_grad.shape[0]

    @pl.when(step == 0)
    def _():
        for part, ref in enumerate((own_grad, other_grad)):
            high, low = halves(ref[...])
            g_high[part * pixels : (part + 1) * pixels] = high
            g_low[part * pixels : (part + 1) * pixels] = low
        acc[...] = jnp.zeros_like(acc)

    change = weight_ref[...] * product((g_high[...], g_low[...]), halves(vt_ref[...]))
    change_ref[...] = change
    acc[...] += rows_folded(change * change)

    @pl.when(step == pl.num_programs(0) - 1)
    def _():
        top = whole_sum(own_grad[...] * own_grad[...]) / col_count
        sums_ref[...] = packed_sums(sums_ref.shape, [top, whole_sum(acc[...])])


def pix_step_kernel(total, first, place, level_sums, sums_ref, u_ref, own_grad, other_grad, res_ref,
                    change_ref, u_out, res_out, even_ref, odd_ref, u_high, u_low):
    step = pl.program_id(0)
    pixels = own_grad.shape[0]
    top, curve = read_sums(sums_ref, 2)
    size = top / curve
    if first:
        (spread,) = read_sums(level_sums, 1)
    else:
        _, spread = column_sums(read_sums(level_sums, 4))
    level = level_from(spread, total)

    @pl.when(step == 0)
    def _():
        for part, ref in enumerate((own_grad, other_grad)):
            rows = slice(part * pixels, (part + 1) * pixels)
            u = u_ref[rows] - size * ref[...]
            u_out[rows] = u
            high, low = halves(u)
            u_high[rows] = high
            u_low[rows] = low

    res = res_ref[...]
    moved = size * change_ref[...]
    res_out[...] = res + moved
    misfit = -(jnp.clip(res, -level, level) + moved)
    grad = product((u_high[...], u_low[...]), halves(misfit), ((0,), (0,)))
    even_ref[0] = grad[:, :LANES]
    odd_ref[0] = grad[:, LANES:]


def shift_kernel(chips, place, u_ref, even_ref, odd_ref, weight_ref, res_ref,
                 shift_ref, sums_ref, u_high, u_low, acc, acc_top):
    step = pl.program_id(0)

    @pl.when(step == 0)
    def _():
        high, low = halves(u_ref[...])
        u_high[...] = high
        u_low[...] = low
        acc[...] = jnp.zeros_like(acc)
        acc_top[...] = jnp.zeros_like(acc_top)

    grad = jnp.concatenate([even_ref[0], odd_ref[0]], axis=1)
    acc_top[...] += rows_folded(grad * grad)
    shift = weight_ref[...] * product((u_high[...], u_low[...]), halves(grad))
    shift_ref[...] = shift
    res = res_ref[...]
    acc[0] += rows_folded(shift * shift)
    acc[1] += rows_folded(shift * res)
    acc[2] += rows_folded(res * res)

    @pl.when(step == pl.num_programs(0) - 1)
    def _():
        sums = [whole_sum(acc_top[...]) / chips] + [whole_sum(acc[k]) for k in range(3)]
        sums_ref[...] = packed_sums(sums_ref.shape, sums)


def rim_kernel(place, *refs):
    obs = refs[0:4]
    mask = refs[4:8]
    u_north, u_south, vt_ref, res_ref, weight_ref, u_high, u_low = refs[8:]
    step = pl.program_id(0)
    chunk = place[1] ^ step
    pixels = obs[0].shape[0]

    @pl.when(step == 0)
    def _():
        for part, ref in enumerate((u_north, u_south)):
            rows = slice(2 * part * pixels, 2 * (part + 1) * pixels)
            high, low = halves(ref[...])
            u_high[rows] = high
            u_low[rows] = low

    low_rank = product((u_high[...], u_low[...]), halves(vt_ref[...]))
    for part in range(4):
        weight = spread_mask(mask[part][...], chunk)
        weight_ref[part] = weight
        res_ref[part] = weight * (obs[part][...] - low_rank[part * pixels : (part + 1) * pixels])


def flux_of(diff, inverse):
    ratio = diff * inverse
    return diff / (1.0 + ratio * ratio)


def smooth_kernel(total, chips, place, sums_ref, res_ref, shift_ref, rim_ref, rim_weight, u_north, u_south,
                  grad_ref, own_ref, other_ref, u_high, u_low):
    step = pl.program_id(0)
    core, chip = place[0], place[2]
    pixels = own_ref.shape[0]

    @pl.when(step == 0)
    def _():
        for part, ref in enumerate((u_north, u_south)):
            rows = slice(2 * part * pixels, 2 * (part + 1) * pixels)
            high, low = halves(ref[...])
            u_high[rows] = high
            u_low[rows] = low

    size, spread = column_sums(read_sums(sums_ref, 4))
    level = level_from(spread, total)
    inverse = 1.0 / level
    rim_shift = product((u_high[...], u_low[...]), halves(grad_ref[0]))
    shifts = rim_shift.reshape(4, pixels, LANES)

    def cut(res):
        return res - jnp.clip(res, -level, level)

    own = [cut(res_ref[k] + size * shift_ref[k]) for k in range(2)]
    rim = [cut(rim_ref[k] + size * (rim_weight[k] * shifts[k])) for k in range(4)]

    def ordered(pair):
        return [jnp.where(core == 0, pair[0], pair[1]), jnp.where(core == 0, pair[1], pair[0])]

    rows = ordered(rim[0:2]) + ordered(own) + ordered(rim[2:4])
    keep_north = jnp.where(chip > 0, 1.0, 0.0).astype(f32)
    keep_south = jnp.where(chip < chips - 1, 1.0, 0.0).astype(f32)
    last = lax.broadcasted_iota(jnp.int32, (pixels, LANES), 0) % WIDTH == WIDTH - 1
    scaled = diffusion

    def smoothed(rows, north_edge, south_edge):
        count = len(rows)
        cross = []
        for k in range(count - 1):
            flux = flux_of(rows[k + 1] - rows[k], inverse)
            if k == north_edge:
                flux = flux * keep_north
            if k == south_edge:
                flux = flux * keep_south
            cross.append(flux)
        out = []
        for k in range(1, count - 1):
            east = jnp.where(last, 0.0, flux_of(pltpu.roll(rows[k], pixels - 1, 0) - rows[k], inverse))
            along = east - pltpu.roll(east, 1, 0)
            out.append(rows[k] + scaled * ((cross[k] - cross[k - 1]) + along))
        return out

    rows = smoothed(rows, 1, 3)
    rows = smoothed(rows, 0, 2)
    even, odd = rows
    own_ref[...] = jnp.where(core == 0, even, odd)
    other_ref[...] = jnp.where(core == 0, odd, even)


def factor_kernel(place, sums_ref, vt_ref, grad_ref, out_ref):
    size, _ = column_sums(read_sums(sums_ref, 4))
    out_ref[...] = (vt_ref[...] - size * grad_ref[0]).T


def grad_over_chips(even, odd):
    chips = lax.axis_size("pix") // 2
    kept = even + along_pix(odd, 2)
    mine = kept[0]
    for part in [along_pix(kept[k], 4 * k) for k in (1, 2, 3)]:
        mine = mine + part
    distance = GROUP
    while distance < chips:
        mine = mine + along_pix(mine, 2 * distance)
        distance *= 2
    even = jnp.stack([mine] + [along_pix(mine, 4 * k) for k in (1, 2, 3)])
    return even, along_pix(even, 2)


def per_device(observed, valid_mask, pix_factor, col_factor):
    pix_count = lax.axis_size("pix")
    col_count = lax.axis_size("col")
    devices = pix_count * col_count
    chips = pix_count // 2
    pixels, columns = observed.shape
    rank = pix_factor.shape[1]
    half = columns // 2
    dates = valid_mask.shape[1] // 2
    total = float(pixels * columns * pix_count * col_count)
    assert pixels == WIDTH and half == GROUP * LANES and chips % GROUP == 0 and PASSES == 2
    index = lax.axis_index("pix")
    core = index % 2
    chip = index // 2
    place = jnp.stack([core, chip % GROUP, chip]).astype(jnp.int32)

    def half_of(which):
        obs = lax.dynamic_slice(observed, (0, which * half), (pixels, half))
        mask = lax.dynamic_slice(valid_mask, (0, which * dates), (pixels, dates))
        return jnp.concatenate([obs, mask.astype(f32)], axis=1)

    other_half = half_of(1 - core)
    own_half = half_of(core)
    received = along_pix(other_half, 1)
    other_factor = along_pix(pix_factor, 1)
    rims = [
        to_chip(own_half, 1, 0), to_chip(other_half, 1, 1),
        to_chip(own_half, -1, 0), to_chip(other_half, -1, 1),
    ]

    both = 2 * pixels
    wide = 2 * LANES
    steps = half // wide
    chunk_in = pl.BlockSpec((pixels, LANES), lambda t, s: (0, s[1] ^ t))
    mask_in = pl.BlockSpec((pixels, dates), lambda t, s: (0, half // dates))
    sums_shape = (devices, LANES)
    pix_block = whole((pixels, rank))
    both_block = whole((both, rank))
    sums_block = whole(sums_shape)
    tile_block = tile(both, wide)
    vt_block = tile(rank, wide)
    grad_block = pl.BlockSpec((1, rank, LANES), lambda t, s: (t, 0, 0))
    local = shaped(both, half)
    factor_scratch = [pltpu.VMEM((both, rank), bf16)] * 2

    residual, weight, vt, sums = call(
        start_kernel, (GROUP,),
        [chunk_in, mask_in, chunk_in, mask_in, pix_block, pix_block,
         pl.BlockSpec((LANES, rank), lambda t, s: (s[0] * GROUP + (s[1] ^ t), 0))],
        [tile(both, LANES), tile(both, LANES), tile(rank, LANES), sums_block],
        [local, local, shaped(rank, half), shaped(*sums_shape)],
        factor_scratch + [pltpu.VMEM((8, LANES), f32)],
        place, own_half, own_half, received, received, pix_factor, other_factor, col_factor,
    )
    level_sums = everywhere(sums)
    u = jnp.concatenate([pix_factor, other_factor], axis=0)

    for iteration in range(ITERS):
        if iteration == 0:
            partial = call(
                functools.partial(first_grad_kernel, total), (steps,),
                [sums_block, tile_block, vt_block], both_block, shaped(both, rank), [],
                place, level_sums, residual, vt,
            )
        else:
            residual, vt, partial = call(
                functools.partial(next_grad_kernel, total), (steps,),
                [sums_block, tile_block, tile_block, vt_block, grad_block, grad_block],
                [tile_block, vt_block, both_block],
                [local, shaped(rank, half), shaped(both, rank)], [],
                place, level_sums, residual, shift, vt, even, odd,
            )
        own_grad = summed_over_col(partial[:pixels] + along_pix(partial[pixels:], 1))
        other_grad = along_pix(own_grad, 1)
        change, sums = call(
            functools.partial(change_kernel, col_count), (steps,),
            [pix_block, pix_block, vt_block, tile_block], [tile_block, sums_block],
            [local, shaped(*sums_shape)], factor_scratch + [pltpu.VMEM((8, wide), f32)],
            place, own_grad, other_grad, vt, weight,
        )
        pix_sums = everywhere(sums)
        u, residual, even, odd = call(
            functools.partial(pix_step_kernel, total, iteration == 0), (steps,),
            [sums_block, sums_block, both_block, pix_block, pix_block, tile_block, tile_block],
            [both_block, tile_block, grad_block, grad_block],
            [shaped(both, rank), local, shaped(steps, rank, LANES), shaped(steps, rank, LANES)],
            factor_scratch,
            place, level_sums, pix_sums, u, own_grad, other_grad, residual, change,
        )
        even, odd = grad_over_chips(even, odd)
        shift, sums = call(
            functools.partial(shift_kernel, chips), (steps,),
            [both_block, grad_block, grad_block, tile_block, tile_block], [tile_block, sums_block],
            [local, shaped(*sums_shape)],
            factor_scratch + [pltpu.VMEM((3, 8, wide), f32), pltpu.VMEM((8, wide), f32)],
            place, u, even, odd, weight, residual,
        )
        level_sums = everywhere(sums)

    u_north = to_chip(u, 1, 0)
    u_south = to_chip(u, -1, 0)
    rim_block = pl.BlockSpec((4, pixels, LANES), lambda t, s: (0, 0, t))
    rim_scratch = [pltpu.VMEM((2 * both, rank), bf16)] * 2
    rim_res, rim_weight = call(
        rim_kernel, (GROUP,),
        [chunk_in] * 4 + [mask_in] * 4 + [both_block, both_block, tile(rank, LANES)],
        [rim_block, rim_block], [shaped(4, pixels, half)] * 2, rim_scratch,
        place, *rims, *rims, u_north, u_south, vt,
    )
    grad = jnp.stack([even, odd], axis=1).reshape(GROUP, rank, LANES)
    pair_block = pl.BlockSpec((2, pixels, LANES), lambda t, s: (0, 0, t))
    own_cloud, other_cloud = call(
        functools.partial(smooth_kernel, total, chips), (GROUP,),
        [sums_block, pair_block, pair_block, rim_block, rim_block, both_block, both_block, grad_block],
        [chunk_in, chunk_in], [shaped(pixels, half)] * 2, rim_scratch,
        place, level_sums, residual.reshape(2, pixels, half), shift.reshape(2, pixels, half),
        rim_res, rim_weight, u_north, u_south, grad,
    )
    own_v = call(
        factor_kernel, (GROUP,),
        [sums_block, tile(rank, LANES), grad_block],
        pl.BlockSpec((LANES, rank), lambda t, s: (s[1] ^ t, 0)), shaped(half, rank), [],
        place, level_sums, vt, grad,
    )
    other_v = along_pix(own_v, 1)
    from_other = along_pix(other_cloud, 1)

    def joined(own, other, axis):
        pair = [jnp.where(core == 0, own, other), jnp.where(core == 0, other, own)]
        return jnp.concatenate(pair, axis=axis)

    return u[:pixels], joined(own_v, other_v, 0), joined(own_cloud, from_other, 1)


def solution(mesh):
    in_specs = (P("pix", "col"), P("pix", "col"), P("pix", None), P("col", None))
    out_specs = (P("pix", None), P("col", None), P("pix", "col"))
    return jax.shard_map(
        per_device, mesh=mesh, in_specs=in_specs, out_specs=out_specs, check_vma=False
    )
```

time: 779 us -> 361 us (0.46)
  blocking collectives: 284 us -> 30.3 us
  waiting for transfers between devices: 345 us -> 182 us
  Pallas kernels: 0 us -> 67.5 us
  matrix products: 56.5 us -> 0 us
  starting transfers between devices: 13.1 us -> 49.5 us
  other arithmetic: 39.3 us -> 12.9 us
  between operations: 24.3 us -> 1.13 us
    psum x7 -> x0, blocking collectives: 284 us -> none  [the longest x3 121 us: level_of(): spread = lax.psum(jnp.sum(weight * residual * residual), ('pix', 'col'))]
    psum x4 -> x0, waiting for transfers between devices: 240 us -> none  [the longest x2 195 us: per_device(): col_grad = lax.psum(local_grad, 'pix')]
    ppermute x4 -> x32, waiting for transfers between devices: 105 us -> 176 us  [the longest x24 120 us: along_pix(): return lax.ppermute(block, 'pix', [(i, i ^ distance) for i in range(count)])]
    pallas_call x0 -> x12, Pallas kernels: none -> 67.5 us  [call(): pl.pallas_call(kernel, grid_spec=pltpu.PrefetchScalarGridSpec(num_scalar_...]
    dot_general x9 -> x0, matrix products: 56.5 us -> none  [the longest x2 18.1 us: per_device(): lax.dot_general(misfit, pix_fac, (((0,), (0,)), ((), ())), precision=high...]
    all_to_all x0 -> x3, blocking collectives: none -> 30.3 us  [everywhere(): return lax.all_to_all(rows, ('pix', 'col'), 0, 0, tiled=True)]
    ppermute x4 -> x32, starting transfers between devices: 13 us -> 39.9 us  [the longest x6 20 us: to_chip(): return lax.ppermute(block, 'pix', route)]
    reduce_sum x6 -> x0, other arithmetic: 22.6 us -> none  [the longest x2 13.9 us: level_of(): spread = lax.psum(jnp.sum(weight * residual * residual), ('pix', 'col'))]
  transfers between devices with their start and end apart: 8 -> 34, of which waited for: 7 -> 29; matrix products, arithmetic and copies ran while one was open for 1% -> 3% of each run, Pallas kernels for 0% -> 3%
where the time goes in v1:
time: 361 us; the launch traced here: 357 us
  waiting for transfers between devices  182 us (50%)
  Pallas kernels  67.5 us (19%)
  starting transfers between devices  49.5 us (14%)
  blocking collectives  30.3 us (8%)
  local copies, waits for them, and re-layouts  13.6 us (4%)
  other arithmetic  12.9 us (4%)
    ppermute x24, waiting for transfers between devices, along_pix(): return lax.ppermute(block, 'pix', [(i, i ^ distance) for i in range(count)])  120 us
    pallas_call x12, Pallas kernels, call(): pl.pallas_call(kernel, grid_spec=pltpu.PrefetchScalarGridSpec(num_scalar_...  67.5 us
    ppermute x6, waiting for transfers between devices, to_chip(): return lax.ppermute(block, 'pix', route)  42.4 us
    all_to_all x3, blocking collectives, everywhere(): return lax.all_to_all(rows, ('pix', 'col'), 0, 0, tiled=True)  30.3 us
    ppermute x6, starting transfers between devices, to_chip(): return lax.ppermute(block, 'pix', route)  20 us
    ppermute x24, starting transfers between devices, along_pix(): return lax.ppermute(block, 'pix', [(i, i ^ distance) for i in range(count)])  17.5 us
    ppermute x2, waiting for transfers between devices, summed_over_col(): lax.ppermute(block, 'col', [(i, i ^ step) for i in range(count)])  12.8 us
    unnamed x66, local copies, waits for them, and re-layouts  9.87 us
  transfers between devices with their start and end apart: 34, of which 29 were waited for; matrix products, arithmetic and copies ran while one was open for 3% of the time, Pallas kernels for 3%

profile of v1, /device:TPU:13, one launch (start us, length us, event | category | flops | bytes accessed | tf_op | source)
XLA Modules:
  0.0 356.6 jit_solution(12140945092625071396)
XLA Ops:
  8.4 8.2 %shard_map.67 = (f32[512,1024]{1,0:T(8,128)S(1)}, f32[512,1024]{1,0:T(8,128)}, f32[256,1024]{1,0:T(8,128)S(1)}, f32[32,128]{1,0:T(8,128)S(1)}) custom-call(s32[3]{0:T(128)S(1)} %pad_add_fusion.place, f32[256,1152]{1,0:T(8,128)S(1)} %pad_maximum_fusion.2.own_obs.own_mask, f32[256,1152]{1,0:T(8,128)S(1)} %pad_maximum_fusion.2.own_obs.own_mask, ...), custom_call_target="tpu_custom_call" | custom-call | tf_op jit(solution)/shard_map/pallas_call | solution.py:90
  16.6 10.5 %all_to_all.55 = f32[32,1,128]{2,1,0:T(1,128)S(1)} all-to-all(f32[32,1,128]{2,1,0:T(1,128)S(1)} %bitcast.78), channel_id=1, replica_groups=mesh['pix'=16,'col'=2] {'pix','col'}, dimensions={0} | all-to-all | bytes 32768 | tf_op jit(solution)/shard_map/all_to_all | solution.py:45
  33.1 6.4 %collective-permute-done.3 = f32[256,256]{1,0:T(8,128)S(1)} collective-permute-done((f32[256,256]{1,0:T(8,128)S(1)}, f32[256,256]{1,0:T(8,128)S(1)}, u32[]{:S(2)}, u32[]{:S(2)}) %collective-permute-start.3) | collective-permute-done | bytes 262176 | tf_op jit(solution)/shard_map/ppermute | solution.py:39
  46.6 5.2 %all-to-all-start.1 = ((f32[32,1,128]{2,1,0:T(1,128)}), f32[32,1,128]{2,1,0:T(1,128)}, u32[]{:S(2)}, u32[]{:S(2)}) async-start(f32[32,1,128]{2,1,0:T(1,128)} %bitcast.77), calls=%async_computation.1 | async-start | bytes 32768 | tf_op jit(solution)/shard_map/all_to_all | solution.py:45
  59.2 5.3 %shard_map.70 = (f32[512,256]{1,0:T(8,128)S(1)}, f32[512,1024]{1,0:T(8,128)S(1)}, f32[4,256,128]{2,1,0:T(8,128)S(1)}, f32[4,256,128]{2,1,0:T(8,128)S(1)}) custom-call(s32[3]{0:T(128)S(1)} %copy-done.27, f32[32,128]{1,0:T(8,128)S(1)} %bitcast.71, f32[32,128]{1,0:T(8,128)} %bitcast.8.sums_ref, f32[512,256]{1,0:T(8,128)S(1)} %copy-done.18, ...), custom_call_target="tpu_custom_call" | custom-call | tf_op jit(solution)/shard_map/pallas_call | solution.py:90
  65.0 12.4 %collective-permute-done.5 = f32[4,256,128]{2,1,0:T(8,128)S(1)} collective-permute-done((f32[4,256,128]{2,1,0:T(8,128)S(1)}, f32[4,256,128]{2,1,0:T(8,128)S(1)}, u32[]{:S(2)}, u32[]{:S(2)}) %collective-permute-start.5) | collective-permute-done | bytes 524320 | tf_op jit(solution)/shard_map/ppermute | solution.py:25
  84.8 5.9 %collective-permute-done.8 = f32[256,128]{1,0:T(8,128)S(1)} collective-permute-done((f32[256,128]{1,0:T(8,128)S(1)}, f32[256,128]{1,0:T(8,128)S(1)}, u32[]{:S(2)}, u32[]{:S(2)}) %collective-permute-start.8) | collective-permute-done | bytes 131104 | tf_op jit(solution)/shard_map/ppermute | solution.py:25
  96.4 8.3 %collective-permute-done.11 = f32[256,128]{1,0:T(8,128)S(1)} collective-permute-done((f32[256,128]{1,0:T(8,128)S(1)}, f32[256,128]{1,0:T(8,128)S(1)}, u32[]{:S(2)}, u32[]{:S(2)}) %collective-permute-start.11) | collective-permute-done | bytes 131104 | tf_op jit(solution)/shard_map/ppermute | solution.py:25
  104.8 11.8 %collective-permute-done.12.odd_ref = f32[4,256,128]{2,1,0:T(8,128)S(1)} collective-permute-done((f32[4,256,128]{2,1,0:T(8,128)S(1)}, f32[4,256,128]{2,1,0:T(8,128)S(1)}, u32[]{:S(2)}, u32[]{:S(2)}) %collective-permute-start.12) | collective-permute-done | bytes 524320 | tf_op jit(solution)/shard_map/ppermute | solution.py:25
  122.2 11.2 %all_to_all.56 = f32[32,1,128]{2,1,0:T(1,128)S(1)} all-to-all(f32[32,1,128]{2,1,0:T(1,128)S(1)} %bitcast.79), channel_id=1, replica_groups=mesh['pix'=16,'col'=2] {'pix','col'}, dimensions={0} | all-to-all | bytes 32768 | tf_op jit(solution)/shard_map/all_to_all | solution.py:45
  133.4 5.3 %shard_map.72 = (f32[512,1024]{1,0:T(8,128)S(1)}, f32[256,1024]{1,0:T(8,128)S(1)}, f32[512,256]{1,0:T(8,128)S(1)}) custom-call(s32[3]{0:T(128)S(1)} %copy-done.28, f32[32,128]{1,0:T(8,128)S(1)} %bitcast.72, f32[512,1024]{1,0:T(8,128)} %copy-done.6, f32[512,1024]{1,0:T(8,128)} %copy-done.9, f32[256,1024]{1,0:T(8,128)S(1)} %copy-done.4, ...), custom_call_target="tpu_custom_call" | custom-call | tf_op jit(solution)/shard_map/pallas_call | solution.py:90
  143.3 6.4 %collective-permute-done.14 = f32[256,256]{1,0:T(8,128)S(1)} collective-permute-done((f32[256,256]{1,0:T(8,128)S(1)}, f32[256,256]{1,0:T(8,128)S(1)}, u32[]{:S(2)}, u32[]{:S(2)}) %collective-permute-start.14) | collective-permute-done | bytes 262176 | tf_op jit(solution)/shard_map/ppermute | solution.py:39
  156.2 8.5 %all_to_all.57 = f32[32,1,128]{2,1,0:T(1,128)S(1)} all-to-all(f32[32,1,128]{2,1,0:T(1,128)S(1)} %bitcast.80), channel_id=1, replica_groups=mesh['pix'=16,'col'=2] {'pix','col'}, dimensions={0} | all-to-all | bytes 32768 | tf_op jit(solution)/shard_map/all_to_all | solution.py:45
  164.7 5.6 %shard_map.74 = (f32[512,256]{1,0:T(8,128)S(1)}, f32[512,1024]{1,0:T(8,128)S(1)}, f32[4,256,128]{2,1,0:T(8,128)S(1)}, f32[4,256,128]{2,1,0:T(8,128)S(1)}) custom-call(s32[3]{0:T(128)S(1)} %copy-done.28, f32[32,128]{1,0:T(8,128)S(1)} %bitcast.73, f32[32,128]{1,0:T(8,128)S(1)} %bitcast.76, f32[512,256]{1,0:T(8,128)S(1)} %get-tuple-element.36.u_ref, ...), custom_call_target="tpu_custom_call" | custom-call | tf_op jit(solution)/shard_map/pallas_call | solution.py:90
  177.5 30.9 %collective-permute-done.16 = f32[4,256,128]{2,1,0:T(8,128)S(1)} collective-permute-done((f32[4,256,128]{2,1,0:T(8,128)S(1)}, f32[4,256,128]{2,1,0:T(8,128)S(1)}, u32[]{:S(2)}, u32[]{:S(2)}) %collective-permute-start.16) | collective-permute-done | bytes 524320 | tf_op jit(solution)/shard_map/ppermute | solution.py:25
  222.9 18.8 %collective-permute-done.20 = f32[256,128]{1,0:T(8,128)S(1)} collective-permute-done((f32[256,128]{1,0:T(8,128)S(1)}, f32[256,128]{1,0:T(8,128)S(1)}, u32[]{:S(2)}, u32[]{:S(2)}) %collective-permute-start.20) | collective-permute-done | bytes 131104 | tf_op jit(solution)/shard_map/ppermute | solution.py:25
  241.6 6.2 %collective-permute-done.21 = f32[256,128]{1,0:T(8,128)S(1)} collective-permute-done((f32[256,128]{1,0:T(8,128)S(1)}, f32[256,128]{1,0:T(8,128)S(1)}, u32[]{:S(2)}, u32[]{:S(2)}) %collective-permute-start.21) | collective-permute-done | bytes 131104 | tf_op jit(solution)/shard_map/ppermute | solution.py:25
  250.5 5.7 %collective-permute-done.22 = f32[256,128]{1,0:T(8,128)S(1)} collective-permute-done((f32[256,128]{1,0:T(8,128)S(1)}, f32[256,128]{1,0:T(8,128)S(1)}, u32[]{:S(2)}, u32[]{:S(2)}) %collective-permute-start.22) | collective-permute-done | bytes 131104 | tf_op jit(solution)/shard_map/ppermute | solution.py:25
  264.4 29.3 %collective-permute-done.25.refs_0_.refs_4_ = f32[256,1152]{1,0:T(8,128)S(1)} collective-permute-done((f32[256,1152]{1,0:T(8,128)S(1)}, f32[256,1152]{1,0:T(8,128)S(1)}, u32[]{:S(2)}, u32[]{:S(2)}) %collective-permute-start.25) | collective-permute-done | bytes 1179680 | tf_op jit(solution)/shard_map/ppermute | solution.py:32
  295.5 9.4 %collective-permute-done.29.refs_8_.u_north = f32[512,256]{1,0:T(8,128)S(1)} collective-permute-done((f32[512,256]{1,0:T(8,128)S(1)}, f32[512,256]{1,0:T(8,128)S(1)}, u32[]{:S(2)}, u32[]{:S(2)}) %collective-permute-start.29) | collective-permute-done | bytes 524320 | tf_op jit(solution)/shard_map/ppermute | solution.py:32
  306.7 9.9 %shard_map.77 = (f32[4,256,1024]{2,1,0:T(8,128)}, f32[4,256,1024]{2,1,0:T(8,128)}) custom-call(s32[3]{0:T(128)S(1)} %copy-done.28, f32[256,1152]{1,0:T(8,128)S(1)} %collective-permute-done.25.refs_0_.refs_4_, f32[256,1152]{1,0:T(8,128)S(1)} %collective-permute-done.26.refs_1_.refs_5_, f32[256,1152]{1,0:T(8,128)S(1)} %collective-permute-done.27.refs_2_.refs_6_, ...), custom_call_target="tpu_custom_call" | custom-call | tf_op jit(solution)/shard_map/pallas_call | solution.py:90
  318.0 4.9 %shard_map.75 = (f32[512,1024]{1,0:T(8,128)S(1)}, f32[32,128]{1,0:T(8,128)}) custom-call(s32[3]{0:T(128)S(1)} %copy-done.28, f32[512,256]{1,0:T(8,128)S(1)} %get-tuple-element.47.u_ref, f32[4,256,128]{2,1,0:T(8,128)S(1)} %get-tuple-element.64.even_ref, f32[4,256,128]{2,1,0:T(8,128)S(1)} %collective-permute-done.23.odd_ref, f32[512,1024]{1,0:T(8,128)S(1)} %copy-done, ...), custom_call_target="tpu_custom_call" | custom-call | tf_op jit(solution)/shard_map/pallas_call | solution.py:90
  324.2 4.4 %all-to-all-start.4 = ((f32[32,1,128]{2,1,0:T(1,128)}), f32[32,1,128]{2,1,0:T(1,128)S(1)}, u32[]{:S(2)}, u32[]{:S(2)}) async-start(f32[32,1,128]{2,1,0:T(1,128)} %bitcast.32), calls=%async_computation.4 | async-start | bytes 32768 | tf_op jit(solution)/shard_map/all_to_all | solution.py:45
  333.2 13.2 %shard_map.78 = (f32[256,1024]{1,0:T(8,128)S(1)}, f32[256,1024]{1,0:T(8,128)}) custom-call(s32[3]{0:T(128)S(1)} %copy-done.28, f32[32,128]{1,0:T(8,128)S(1)} %bitcast.74, f32[2,256,1024]{2,1,0:T(8,128)} %bitcast.67, f32[2,256,1024]{2,1,0:T(8,128)} %bitcast.68, f32[4,256,1024]{2,1,0:T(8,128)} %get-tuple-element.53.rim_ref, ...), custom_call_target="tpu_custom_call" | custom-call | tf_op jit(solution)/shard_map/pallas_call | solution.py:90
  (152 shorter events, 111.7 us)
Async XLA Ops:
  31.9 7.6 %collective-permute-start.3 = (f32[256,256]{1,0:T(8,128)S(1)}, f32[256,256]{1,0:T(8,128)S(1)}, u32[]{:S(2)}, u32[]{:S(2)}) collective-permute-start(f32[256,256]{1,0:T(8,128)S(1)} %slice_add_fusion), channel_id=1, source_target_pairs={{0,1},{1,0},{2,3},{3,2},{4,5},{5,4},{6,7},{7,6},{8,9},{9,8},{10,11... | collective-permute-start | bytes 786440 | tf_op jit(solution)/shard_map/ppermute | solution.py:39
  46.6 10.0 %all-to-all-start.1 = ((f32[32,1,128]{2,1,0:T(1,128)}), f32[32,1,128]{2,1,0:T(1,128)}, u32[]{:S(2)}, u32[]{:S(2)}) async-start(f32[32,1,128]{2,1,0:T(1,128)} %bitcast.77), calls=%async_computation.1 | async-start | bytes 32768 | tf_op jit(solution)/shard_map/all_to_all | solution.py:45
  64.6 12.8 %collective-permute-start.5 = (f32[4,256,128]{2,1,0:T(8,128)S(1)}, f32[4,256,128]{2,1,0:T(8,128)S(1)}, u32[]{:S(2)}, u32[]{:S(2)}) collective-permute-start(f32[4,256,128]{2,1,0:T(8,128)S(1)} %get-tuple-element.38), channel_id=1, source_target_pairs={{0,4},{2,6},{4,0},{6,2},{8,12},{10,14},{12,8},{14,10},{16,20},{18,... | collective-permute-start | bytes 1572872 | tf_op jit(solution)/shard_map/ppermute | solution.py:25
  78.7 6.1 %collective-permute-start.7 = (f32[256,128]{1,0:T(8,128)S(1)}, f32[256,128]{1,0:T(8,128)S(1)}, u32[]{:S(2)}, u32[]{:S(2)}) collective-permute-start(f32[256,128]{1,0:T(8,128)S(1)} %get-tuple-element.70), channel_id=1, source_target_pairs={{0,16},{2,18},{4,20},{6,22},{8,24},{10,26},{12,28},{14,30},{16,0},... | collective-permute-start | bytes 393224 | tf_op jit(solution)/shard_map/ppermute | solution.py:25
  78.9 11.7 %collective-permute-start.8 = (f32[256,128]{1,0:T(8,128)S(1)}, f32[256,128]{1,0:T(8,128)S(1)}, u32[]{:S(2)}, u32[]{:S(2)}) collective-permute-start(f32[256,128]{1,0:T(8,128)S(1)} %get-tuple-element.69), channel_id=1, source_target_pairs={{0,24},{2,26},{4,28},{6,30},{8,16},{10,18},{12,20},{14,22},{16,8},... | collective-permute-start | bytes 393224 | tf_op jit(solution)/shard_map/ppermute | solution.py:25
  90.8 5.6 %collective-permute-start.10 = (f32[256,128]{1,0:T(8,128)S(1)}, f32[256,128]{1,0:T(8,128)S(1)}, u32[]{:S(2)}, u32[]{:S(2)}) collective-permute-start(f32[256,128]{1,0:T(8,128)S(1)} %fusion.5), channel_id=1, source_target_pairs={{0,16},{2,18},{4,20},{6,22},{8,24},{10,26},{12,28},{14,30},{16,0},... | collective-permute-start | bytes 393224 | tf_op jit(solution)/shard_map/ppermute | solution.py:25
  92.4 12.2 %collective-permute-start.11 = (f32[256,128]{1,0:T(8,128)S(1)}, f32[256,128]{1,0:T(8,128)S(1)}, u32[]{:S(2)}, u32[]{:S(2)}) collective-permute-start(f32[256,128]{1,0:T(8,128)S(1)} %fusion.5), channel_id=1, source_target_pairs={{0,24},{2,26},{4,28},{6,30},{8,16},{10,18},{12,20},{14,22},{16,8},... | collective-permute-start | bytes 393224 | tf_op jit(solution)/shard_map/ppermute | solution.py:25
  104.7 11.9 %collective-permute-start.12 = (f32[4,256,128]{2,1,0:T(8,128)S(1)}, f32[4,256,128]{2,1,0:T(8,128)S(1)}, u32[]{:S(2)}, u32[]{:S(2)}) collective-permute-start(f32[4,256,128]{2,1,0:T(8,128)S(1)} %pad_maximum_fusion.6.even_ref), channel_id=1, source_target_pairs={{0,4},{2,6},{4,0},{6,2},{8,12},{10,14},{12,8},{14,10},{16,20},{18,... | collective-permute-start | bytes 1572872 | tf_op jit(solution)/shard_map/ppermute | solution.py:25
  142.1 7.6 %collective-permute-start.14 = (f32[256,256]{1,0:T(8,128)S(1)}, f32[256,256]{1,0:T(8,128)S(1)}, u32[]{:S(2)}, u32[]{:S(2)}) collective-permute-start(f32[256,256]{1,0:T(8,128)S(1)} %slice_add_fusion.1), channel_id=1, source_target_pairs={{0,1},{1,0},{2,3},{3,2},{4,5},{5,4},{6,7},{7,6},{8,9},{9,8},{10,11... | collective-permute-start | bytes 786440 | tf_op jit(solution)/shard_map/ppermute | solution.py:39
  170.3 38.1 %collective-permute-start.16 = (f32[4,256,128]{2,1,0:T(8,128)S(1)}, f32[4,256,128]{2,1,0:T(8,128)S(1)}, u32[]{:S(2)}, u32[]{:S(2)}) collective-permute-start(f32[4,256,128]{2,1,0:T(8,128)S(1)} %get-tuple-element.49), channel_id=1, source_target_pairs={{0,4},{2,6},{4,0},{6,2},{8,12},{10,14},{12,8},{14,10},{16,20},{18,... | collective-permute-start | bytes 1572872 | tf_op jit(solution)/shard_map/ppermute | solution.py:25
  170.7 89.5 %collective-permute-start.26 = (f32[256,1152]{1,0:T(8,128)}, f32[256,1152]{1,0:T(8,128)S(1)}, u32[]{:S(2)}, u32[]{:S(2)}) collective-permute-start(f32[256,1152]{1,0:T(8,128)} %pad_maximum_fusion.3), channel_id=1, source_target_pairs={{0,6},{2,4},{4,10},{6,8},{8,14},{10,12},{12,18},{14,16},{16,22},{1... | collective-permute-start | bytes 3538952 | tf_op jit(solution)/shard_map/ppermute | solution.py:32
  174.7 89.6 %collective-permute-start.28 = (f32[256,1152]{1,0:T(8,128)}, f32[256,1152]{1,0:T(8,128)S(1)}, u32[]{:S(2)}, u32[]{:S(2)}) collective-permute-start(f32[256,1152]{1,0:T(8,128)} %pad_maximum_fusion.3), channel_id=1, source_target_pairs={{4,2},{6,0},{8,6},{10,4},{12,10},{14,8},{16,14},{18,12},{20,18},{2... | collective-permute-start | bytes 3538952 | tf_op jit(solution)/shard_map/ppermute | solution.py:32
  208.5 4.2 %collective-permute-start.17 = (f32[256,128]{1,0:T(8,128)S(1)}, f32[256,128]{1,0:T(8,128)S(1)}, u32[]{:S(2)}, u32[]{:S(2)}) collective-permute-start(f32[256,128]{1,0:T(8,128)S(1)} %get-tuple-element.65), channel_id=1, source_target_pairs={{0,8},{2,10},{4,12},{6,14},{8,0},{10,2},{12,4},{14,6},{16,24},{18,... | collective-permute-start | bytes 393224 | tf_op jit(solution)/shard_map/ppermute | solution.py:25
  208.6 6.3 %collective-permute-start.18 = (f32[256,128]{1,0:T(8,128)S(1)}, f32[256,128]{1,0:T(8,128)S(1)}, u32[]{:S(2)}, u32[]{:S(2)}) collective-permute-start(f32[256,128]{1,0:T(8,128)S(1)} %get-tuple-element.67), channel_id=1, source_target_pairs={{0,16},{2,18},{4,20},{6,22},{8,24},{10,26},{12,28},{14,30},{16,0},... | collective-permute-start | bytes 393224 | tf_op jit(solution)/shard_map/ppermute | solution.py:25
  210.1 12.7 %collective-permute-start.19 = (f32[256,128]{1,0:T(8,128)S(1)}, f32[256,128]{1,0:T(8,128)S(1)}, u32[]{:S(2)}, u32[]{:S(2)}) collective-permute-start(f32[256,128]{1,0:T(8,128)S(1)} %get-tuple-element.66), channel_id=1, source_target_pairs={{0,24},{2,26},{4,28},{6,30},{8,16},{10,18},{12,20},{14,22},{16,8},... | collective-permute-start | bytes 393224 | tf_op jit(solution)/shard_map/ppermute | solution.py:25
  212.7 80.9 %collective-permute-start.25 = (f32[256,1152]{1,0:T(8,128)S(1)}, f32[256,1152]{1,0:T(8,128)S(1)}, u32[]{:S(2)}, u32[]{:S(2)}) collective-permute-start(f32[256,1152]{1,0:T(8,128)S(1)} %pad_maximum_fusion.2.own_obs.own_mask), channel_id=1, source_target_pairs={{0,4},{2,6},{4,8},{6,10},{8,12},{10,14},{12,16},{14,18},{16,20},{1... | collective-permute-start | bytes 3538952 | tf_op jit(solution)/shard_map/ppermute | solution.py:32
  214.9 80.6 %collective-permute-start.27 = (f32[256,1152]{1,0:T(8,128)S(1)}, f32[256,1152]{1,0:T(8,128)S(1)}, u32[]{:S(2)}, u32[]{:S(2)}) collective-permute-start(f32[256,1152]{1,0:T(8,128)S(1)} %pad_maximum_fusion.2.own_obs.own_mask), channel_id=1, source_target_pairs={{4,0},{6,2},{8,4},{10,6},{12,8},{14,10},{16,12},{18,14},{20,16},{2... | collective-permute-start | bytes 3538952 | tf_op jit(solution)/shard_map/ppermute | solution.py:32
  222.8 18.8 %collective-permute-start.20 = (f32[256,128]{1,0:T(8,128)S(1)}, f32[256,128]{1,0:T(8,128)S(1)}, u32[]{:S(2)}, u32[]{:S(2)}) collective-permute-start(f32[256,128]{1,0:T(8,128)S(1)} %fusion.2), channel_id=1, source_target_pairs={{0,8},{2,10},{4,12},{6,14},{8,0},{10,2},{12,4},{14,6},{16,24},{18,... | collective-permute-start | bytes 393224 | tf_op jit(solution)/shard_map/ppermute | solution.py:25
  241.6 6.2 %collective-permute-start.21 = (f32[256,128]{1,0:T(8,128)S(1)}, f32[256,128]{1,0:T(8,128)S(1)}, u32[]{:S(2)}, u32[]{:S(2)}) collective-permute-start(f32[256,128]{1,0:T(8,128)S(1)} %fusion.2), channel_id=1, source_target_pairs={{0,16},{2,18},{4,20},{6,22},{8,24},{10,26},{12,28},{14,30},{16,0},... | collective-permute-start | bytes 393224 | tf_op jit(solution)/shard_map/ppermute | solution.py:25
  247.8 8.4 %collective-permute-start.22 = (f32[256,128]{1,0:T(8,128)S(1)}, f32[256,128]{1,0:T(8,128)S(1)}, u32[]{:S(2)}, u32[]{:S(2)}) collective-permute-start(f32[256,128]{1,0:T(8,128)S(1)} %fusion.2), channel_id=1, source_target_pairs={{0,24},{2,26},{4,28},{6,30},{8,16},{10,18},{12,20},{14,22},{16,8},... | collective-permute-start | bytes 393224 | tf_op jit(solution)/shard_map/ppermute | solution.py:25
  256.2 48.7 %collective-permute-start.29 = (f32[512,256]{1,0:T(8,128)S(1)}, f32[512,256]{1,0:T(8,128)S(1)}, u32[]{:S(2)}, u32[]{:S(2)}) collective-permute-start(f32[512,256]{1,0:T(8,128)S(1)} %get-tuple-element.47.u_ref), channel_id=1, source_target_pairs={{0,4},{2,6},{4,8},{6,10},{8,12},{10,14},{12,16},{14,18},{16,20},{1... | collective-permute-start | bytes 1572872 | tf_op jit(solution)/shard_map/ppermute | solution.py:32
  260.2 46.5 %collective-permute-start.30 = (f32[512,256]{1,0:T(8,128)S(1)}, f32[512,256]{1,0:T(8,128)S(1)}, u32[]{:S(2)}, u32[]{:S(2)}) collective-permute-start(f32[512,256]{1,0:T(8,128)S(1)} %get-tuple-element.47.u_ref), channel_id=1, source_target_pairs={{4,0},{6,2},{8,4},{10,6},{12,8},{14,10},{16,12},{18,14},{20,16},{2... | collective-permute-start | bytes 1572872 | tf_op jit(solution)/shard_map/ppermute | solution.py:32
  264.2 53.7 %collective-permute-start.23 = (f32[4,256,128]{2,1,0:T(8,128)S(1)}, f32[4,256,128]{2,1,0:T(8,128)S(1)}, u32[]{:S(2)}, u32[]{:S(2)}) collective-permute-start(f32[4,256,128]{2,1,0:T(8,128)S(1)} %get-tuple-element.64.even_ref), channel_id=1, source_target_pairs={{0,4},{2,6},{4,0},{6,2},{8,12},{10,14},{12,8},{14,10},{16,20},{18,... | collective-permute-start | bytes 1572872 | tf_op jit(solution)/shard_map/ppermute | solution.py:25
  324.2 9.0 %all-to-all-start.4 = ((f32[32,1,128]{2,1,0:T(1,128)}), f32[32,1,128]{2,1,0:T(1,128)S(1)}, u32[]{:S(2)}, u32[]{:S(2)}) async-start(f32[32,1,128]{2,1,0:T(1,128)} %bitcast.32), calls=%async_computation.4 | async-start | bytes 32768 | tf_op jit(solution)/shard_map/all_to_all | solution.py:45
  (43 other events, 781.7 us)

commit v2 on v1

--- a/solution.py
+++ b/solution.py
@@ -25,10 +25,14 @@
     return lax.ppermute(block, "pix", [(i, i ^ distance) for i in range(count)])
 
 
-def to_chip(block, distance, crossed):
+def to_odd_or_even(block, far, crossed):
     count = lax.axis_size("pix")
-    route = [(i, (i ^ crossed) + 2 * distance) for i in range(count)]
-    route = [(a, b) for a, b in route if 0 <= b < count]
+    route = []
+    for i in range(count):
+        chip = i // 2
+        target = ((chip + 1) ^ 1) - 1 if far else chip ^ 1
+        if 0 <= target < count // 2:
+            route.append((i, 2 * target + (i % 2 ^ crossed)))
     return lax.ppermute(block, "pix", route)
 
 
@@ -86,19 +90,48 @@
     return jnp.dot(mask.astype(bf16), pick, preferred_element_type=f32)
 
 
-def call(kernel, grid, in_specs, out_specs, out_shape, scratch, place, *args):
-    return pl.pallas_call(
-        kernel,
+def call(kernel, grid, in_specs, out_specs, out_shape, scratch, place, *args, after=(), through=()):
+    single = not isinstance(out_shape, (list, tuple))
+    if single:
+        out_specs, out_shape = [out_specs], [out_shape]
+    extra_in, extra_out = len(after) + len(through), len(through)
+    inputs, outputs = len(in_specs), len(out_specs)
+    anywhere = pl.BlockSpec(memory_space=pl.ANY)
+
+    def body(place_ref, *refs):
+        first = inputs + extra_in
+        kernel(place_ref, *refs[:inputs], *refs[first : first + outputs], *refs[first + outputs + extra_out :])
+
+    results = pl.pallas_call(
+        body,
         grid_spec=pltpu.PrefetchScalarGridSpec(
             num_scalar_prefetch=1,
             grid=grid,
-            in_specs=in_specs,
-            out_specs=out_specs,
+            in_specs=list(in_specs) + [anywhere] * extra_in,
+            out_specs=list(out_specs) + [anywhere] * extra_out,
             scratch_shapes=scratch,
         ),
-        out_shape=out_shape,
+        out_shape=list(out_shape) + [jax.ShapeDtypeStruct(x.shape, x.dtype) for x in through],
+        input_output_aliases={1 + inputs + len(after) + k: outputs + k for k in range(extra_out)},
         compiler_params=pltpu.CompilerParams(vmem_limit_bytes=48 * 2**20),
-    )(place, *args)
+    )(place, *args, *after, *through)
+    if through:
+        return results[:outputs], results[outputs:]
+    return results[0] if single else results
+
+
+def held_until(array, *after):
+    def body(*refs):
+        pass
+
+    anywhere = pl.BlockSpec(memory_space=pl.ANY)
+    return pl.pallas_call(
+        body,
+        in_specs=[anywhere] * (1 + len(after)),
+        out_specs=anywhere,
+        out_shape=jax.ShapeDtypeStruct(array.shape, array.dtype),
+        input_output_aliases={0: 0},
+    )(array, *after)
 
 
 def whole(shape):
@@ -275,15 +308,16 @@
 def rim_kernel(place, *refs):
     obs = refs[0:4]
     mask = refs[4:8]
-    u_north, u_south, vt_ref, res_ref, weight_ref, u_high, u_low = refs[8:]
+    factors = refs[8:12]
+    vt_ref, res_ref, weight_ref, u_high, u_low = refs[12:]
     step = pl.program_id(0)
     chunk = place[1] ^ step
     pixels = obs[0].shape[0]
 
     @pl.when(step == 0)
     def _():
-        for part, ref in enumerate((u_north, u_south)):
-            rows = slice(2 * part * pixels, 2 * (part + 1) * pixels)
+        for part, ref in enumerate(factors):
+            rows = slice(part * pixels, (part + 1) * pixels)
             high, low = halves(ref[...])
             u_high[rows] = high
             u_low[rows] = low
@@ -300,16 +334,17 @@
     return diff / (1.0 + ratio * ratio)
 
 
-def smooth_kernel(total, chips, place, sums_ref, res_ref, shift_ref, rim_ref, rim_weight, u_north, u_south,
-                  grad_ref, own_ref, other_ref, u_high, u_low):
+def smooth_kernel(total, chips, place, sums_ref, res_ref, shift_ref, rim_ref, rim_weight, *refs):
+    factors = refs[:4]
+    grad_ref, own_ref, other_ref, u_high, u_low, rim_shift = refs[4:]
     step = pl.program_id(0)
     core, chip = place[0], place[2]
     pixels = own_ref.shape[0]
 
     @pl.when(step == 0)
     def _():
-        for part, ref in enumerate((u_north, u_south)):
-            rows = slice(2 * part * pixels, 2 * (part + 1) * pixels)
+        for part, ref in enumerate(factors):
+            rows = slice(part * pixels, (part + 1) * pixels)
             high, low = halves(ref[...])
             u_high[rows] = high
             u_low[rows] = low
@@ -317,19 +352,22 @@
     size, spread = column_sums(read_sums(sums_ref, 4))
     level = level_from(spread, total)
     inverse = 1.0 / level
-    rim_shift = product((u_high[...], u_low[...]), halves(grad_ref[0]))
-    shifts = rim_shift.reshape(4, pixels, LANES)
+    moved = product((u_high[...], u_low[...]), halves(grad_ref[0]))
+    rim_shift[...] = moved.reshape(rim_shift.shape)
 
     def cut(res):
         return res - jnp.clip(res, -level, level)
 
-    own = [cut(res_ref[k] + size * shift_ref[k]) for k in range(2)]
-    rim = [cut(rim_ref[k] + size * (rim_weight[k] * shifts[k])) for k in range(4)]
-
-    def ordered(pair):
-        return [jnp.where(core == 0, pair[0], pair[1]), jnp.where(core == 0, pair[1], pair[0])]
-
-    rows = ordered(rim[0:2]) + ordered(own) + ordered(rim[2:4])
+    def own(k):
+        return cut(res_ref[k] + size * shift_ref[k])
+
+    def rim(k):
+        return cut(rim_ref[k] + size * (rim_weight[k] * rim_shift[k]))
+
+    south = 2 * (chip % 2)
+    north = 2 - south
+    rows = [rim(north + core), rim(north + 1 - core), own(core), own(1 - core),
+            rim(south + core), rim(south + 1 - core)]
     keep_north = jnp.where(chip > 0, 1.0, 0.0).astype(f32)
     keep_south = jnp.where(chip < chips - 1, 1.0, 0.0).astype(f32)
     last = lax.broadcasted_iota(jnp.int32, (pixels, LANES), 0) % WIDTH == WIDTH - 1
@@ -364,9 +402,11 @@
     out_ref[...] = (vt_ref[...] - size * grad_ref[0]).T
 
 
-def grad_over_chips(even, odd):
+def grad_over_chips(even, odd, half):
     chips = lax.axis_size("pix") // 2
-    kept = even + along_pix(odd, 2)
+    from_odd = along_pix(odd, 2)
+    kept = even + from_odd
+    half = held_until(half, from_odd)
     mine = kept[0]
     for part in [along_pix(kept[k], 4 * k) for k in (1, 2, 3)]:
         mine = mine + part
@@ -375,7 +415,7 @@
         mine = mine + along_pix(mine, 2 * distance)
         distance *= 2
     even = jnp.stack([mine] + [along_pix(mine, 4 * k) for k in (1, 2, 3)])
-    return even, along_pix(even, 2)
+    return even, half
 
 
 def per_device(observed, valid_mask, pix_factor, col_factor):
@@ -403,10 +443,8 @@
     own_half = half_of(core)
     received = along_pix(other_half, 1)
     other_factor = along_pix(pix_factor, 1)
-    rims = [
-        to_chip(own_half, 1, 0), to_chip(other_half, 1, 1),
-        to_chip(own_half, -1, 0), to_chip(other_half, -1, 1),
-    ]
+    sent = [own_half, other_half]
+    rims = []
 
     both = 2 * pixels
     wide = 2 * LANES
@@ -420,7 +458,7 @@
     tile_block = tile(both, wide)
     vt_block = tile(rank, wide)
     grad_block = pl.BlockSpec((1, rank, LANES), lambda t, s: (t, 0, 0))
-    local = shaped(both, half)
+    local = pltpu.HBM((both, half), f32)
     factor_scratch = [pltpu.VMEM((both, rank), bf16)] * 2
 
     residual, weight, vt, sums = call(
@@ -436,6 +474,8 @@
     u = jnp.concatenate([pix_factor, other_factor], axis=0)
 
     for iteration in range(ITERS):
+        sent[iteration] = held_until(sent[iteration], level_sums)
+        rims.append(to_odd_or_even(sent[iteration], True, iteration))
         if iteration == 0:
             partial = call(
                 functools.partial(first_grad_kernel, total), (steps,),
@@ -465,9 +505,17 @@
             [both_block, tile_block, grad_block, grad_block],
             [shaped(both, rank), local, shaped(steps, rank, LANES), shaped(steps, rank, LANES)],
             factor_scratch,
-            place, level_sums, pix_sums, u, own_grad, other_grad, residual, change,
+            place, level_sums, pix_sums, u, own_grad, other_grad, residual, change, after=rims[-1:],
         )
-        even, odd = grad_over_chips(even, odd)
+        if iteration == ITERS - 1:
+            u_own = u[:pixels]
+            u_near = to_odd_or_even(u_own, False, 0)
+            u_far = to_odd_or_even(u_own, True, 0)
+            factors = [u_near, along_pix(u_near, 1), u_far, along_pix(u_far, 1)]
+        even, sent[iteration] = grad_over_chips(even, odd, sent[iteration])
+        rims.append(to_odd_or_even(sent[iteration], False, iteration))
+        even = held_until(even, rims[-1])
+        odd = along_pix(even, 2)
         shift, sums = call(
             functools.partial(shift_kernel, chips), (steps,),
             [both_block, grad_block, grad_block, tile_block, tile_block], [tile_block, sums_block],
@@ -477,24 +525,24 @@
         )
         level_sums = everywhere(sums)
 
-    u_north = to_chip(u, 1, 0)
-    u_south = to_chip(u, -1, 0)
+    rims = [rims[1], rims[3], rims[0], rims[2]]
     rim_block = pl.BlockSpec((4, pixels, LANES), lambda t, s: (0, 0, t))
     rim_scratch = [pltpu.VMEM((2 * both, rank), bf16)] * 2
     rim_res, rim_weight = call(
         rim_kernel, (GROUP,),
-        [chunk_in] * 4 + [mask_in] * 4 + [both_block, both_block, tile(rank, LANES)],
+        [chunk_in] * 4 + [mask_in] * 4 + [pix_block] * 4 + [tile(rank, LANES)],
         [rim_block, rim_block], [shaped(4, pixels, half)] * 2, rim_scratch,
-        place, *rims, *rims, u_north, u_south, vt,
+        place, *rims, *rims, *factors, vt,
     )
     grad = jnp.stack([even, odd], axis=1).reshape(GROUP, rank, LANES)
     pair_block = pl.BlockSpec((2, pixels, LANES), lambda t, s: (0, 0, t))
     own_cloud, other_cloud = call(
         functools.partial(smooth_kernel, total, chips), (GROUP,),
-        [sums_block, pair_block, pair_block, rim_block, rim_block, both_block, both_block, grad_block],
-        [chunk_in, chunk_in], [shaped(pixels, half)] * 2, rim_scratch,
+        [sums_block, pair_block, pair_block, rim_block, rim_block] + [pix_block] * 4 + [grad_block],
+        [chunk_in, chunk_in], [shaped(pixels, half)] * 2,
+        rim_scratch + [pltpu.VMEM((4, pixels, LANES), f32)],
         place, level_sums, residual.reshape(2, pixels, half), shift.reshape(2, pixels, half),
-        rim_res, rim_weight, u_north, u_south, grad,
+        rim_res, rim_weight, *factors, grad,
     )
     own_v = call(
         factor_kernel, (GROUP,),
@@ -509,7 +557,7 @@
         pair = [jnp.where(core == 0, own, other), jnp.where(core == 0, other, own)]
         return jnp.concatenate(pair, axis=axis)
 
-    return u[:pixels], joined(own_v, other_v, 0), joined(own_cloud, from_other, 1)
+    return u_own, joined(own_v, other_v, 0), joined(own_cloud, from_other, 1)
 
 
 def solution(mesh):

time: 361 us -> 307 us (0.85)
  waiting for transfers between devices: 182 us -> 108 us
  local copies, waits for them, and re-layouts: 13.6 us -> 33 us
  starting transfers between devices: 49.5 us -> 44.1 us
    ppermute x24 -> x26, waiting for transfers between devices: 120 us -> 82.7 us  [along_pix(): return lax.ppermute(block, 'pix', [(i, i ^ distance) for i in range(count)])]
    ppermute x6, waiting for transfers between devices: 42.4 us -> 6.23 us  [to_odd_or_even(): return lax.ppermute(block, 'pix', route)]
    unnamed x66 -> x100, local copies, waits for them, and re-layouts: 9.87 us -> 29.4 us
    ppermute x6, starting transfers between devices: 20 us -> 15.7 us  [to_odd_or_even(): return lax.ppermute(block, 'pix', route)]
    pallas_call x12 -> x18, Pallas kernels: 67.5 us -> 69.7 us  [the longest x12 69.7 us: call(): pl.pallas_call(body, grid_spec=pltpu.PrefetchScalarGridSpec(num_scalar_pr...]
    ppermute x24 -> x26, starting transfers between devices: 17.5 us -> 19.7 us  [along_pix(): return lax.ppermute(block, 'pix', [(i, i ^ distance) for i in range(count)])]
  transfers between devices with their start and end apart: 34 -> 36, of which waited for: 29 -> 27; matrix products, arithmetic and copies ran while one was open for 3% -> 4% of each run, Pallas kernels for 3% -> 10%
where the time goes in v2:
time: 307 us; the launch traced here: 303 us
  waiting for transfers between devices  108 us (35%)
  Pallas kernels  69.7 us (23%)
  starting transfers between devices  44.1 us (14%)
  local copies, waits for them, and re-layouts  33 us (11%)
  blocking collectives  30.2 us (10%)
  other arithmetic  16.2 us (5%)
    ppermute x26, waiting for transfers between devices, along_pix(): return lax.ppermute(block, 'pix', [(i, i ^ distance) for i in range(count)])  82.7 us
    pallas_call x12, Pallas kernels, call(): pl.pallas_call(body, grid_spec=pltpu.PrefetchScalarGridSpec(num_scalar_pr...  69.7 us
    all_to_all x3, blocking collectives, everywhere(): return lax.all_to_all(rows, ('pix', 'col'), 0, 0, tiled=True)  30.2 us
    unnamed x100, local copies, waits for them, and re-layouts  29.4 us
    ppermute x26, starting transfers between devices, along_pix(): return lax.ppermute(block, 'pix', [(i, i ^ distance) for i in range(count)])  19.7 us
    ppermute x6, starting transfers between devices, to_odd_or_even(): return lax.ppermute(block, 'pix', route)  15.7 us
    ppermute x2, waiting for transfers between devices, summed_over_col(): lax.ppermute(block, 'col', [(i, i ^ step) for i in range(count)])  13 us
    all_to_all x2, starting transfers between devices, everywhere(): return lax.all_to_all(rows, ('pix', 'col'), 0, 0, tiled=True)  6.34 us
  transfers between devices with their start and end apart: 36, of which 27 were waited for; matrix products, arithmetic and copies ran while one was open for 4% of the time, Pallas kernels for 10%

profile of v2, /device:TPU:13, one launch (start us, length us, event | category | flops | bytes accessed | tf_op | source)
XLA Modules:
  0.0 302.6 jit_solution(109566322958448638)
XLA Ops:
  12.2 6.6 %shard_map.67 = (f32[512,1024]{1,0:T(8,128)}, f32[512,1024]{1,0:T(8,128)}, f32[256,1024]{1,0:T(8,128)S(1)}, f32[32,128]{1,0:T(8,128)S(1)}) custom-call(s32[3]{0:T(128)S(1)} %pad_add_fusion.place_ref, f32[256,1152]{1,0:T(8,128)S(1)} %pad_maximum_fusion.2.refs_0_.refs_1_, f32[256,1152]{1,0:T(8,128)S(1)} %pad_maximum_fusion.2.refs_0_.refs_1_, ...), custom_call_target="tpu_custom_call" | custom-call | tf_op jit(solution)/shard_map/pallas_call | solution.py:105
  20.6 10.6 %all_to_all.55 = f32[32,1,128]{2,1,0:T(1,128)} all-to-all(f32[32,1,128]{2,1,0:T(1,128)S(1)} %bitcast.79), channel_id=1, replica_groups=mesh['pix'=16,'col'=2] {'pix','col'}, dimensions={0} | all-to-all | bytes 32768 | tf_op jit(solution)/shard_map/all_to_all | solution.py:49
  43.5 6.4 %collective-permute-done.3 = f32[256,256]{1,0:T(8,128)S(1)} collective-permute-done((f32[256,256]{1,0:T(8,128)S(1)}, f32[256,256]{1,0:T(8,128)S(1)}, u32[]{:S(2)}, u32[]{:S(2)}) %collective-permute-start.3) | collective-permute-done | bytes 262176 | tf_op jit(solution)/shard_map/ppermute | solution.py:43
  68.8 5.4 %shard_map.71 = (f32[512,256]{1,0:T(8,128)S(1)}, f32[512,1024]{1,0:T(8,128)}, f32[4,256,128]{2,1,0:T(8,128)S(1)}, f32[4,256,128]{2,1,0:T(8,128)S(1)}) custom-call(s32[3]{0:T(128)S(1)} %copy-done.46, f32[32,128]{1,0:T(8,128)S(1)} %bitcast.71, f32[32,128]{1,0:T(8,128)} %bitcast.8.refs_1_, f32[512,256]{1,0:T(8,128)S(1)} %copy-done.25, ...), custom_call_target="tpu_custom_call" | custom-call | tf_op jit(solution)/shard_map/pallas_call | solution.py:105
  76.1 12.5 %collective-permute-done.6.refs_1_ = f32[4,256,128]{2,1,0:T(8,128)} collective-permute-done((f32[4,256,128]{2,1,0:T(8,128)S(1)}, f32[4,256,128]{2,1,0:T(8,128)}, u32[]{:S(2)}, u32[]{:S(2)}) %collective-permute-start.6) | collective-permute-done | bytes 524320 | tf_op jit(solution)/shard_map/ppermute | solution.py:25
  97.5 6.5 %collective-permute-done.9 = f32[256,128]{1,0:T(8,128)S(1)} collective-permute-done((f32[256,128]{1,0:T(8,128)S(1)}, f32[256,128]{1,0:T(8,128)S(1)}, u32[]{:S(2)}, u32[]{:S(2)}) %collective-permute-start.9) | collective-permute-done | bytes 131104 | tf_op jit(solution)/shard_map/ppermute | solution.py:25
  110.2 7.6 %collective-permute-done.12 = f32[256,128]{1,0:T(8,128)S(1)} collective-permute-done((f32[256,128]{1,0:T(8,128)S(1)}, f32[256,128]{1,0:T(8,128)S(1)}, u32[]{:S(2)}, u32[]{:S(2)}) %collective-permute-start.12) | collective-permute-done | bytes 131104 | tf_op jit(solution)/shard_map/ppermute | solution.py:25
  119.8 10.8 %collective-permute-done.14.refs_2_.refs_5_ = f32[4,256,128]{2,1,0:T(8,128)S(1)} collective-permute-done((f32[4,256,128]{2,1,0:T(8,128)}, f32[4,256,128]{2,1,0:T(8,128)S(1)}, u32[]{:S(2)}, u32[]{:S(2)}) %collective-permute-start.14) | collective-permute-done | bytes 524320 | tf_op jit(solution)/shard_map/ppermute | solution.py:25
  134.5 3.8 %shard_map.74 = (f32[512,1024]{1,0:T(8,128)}, f32[32,128]{1,0:T(8,128)S(1)}) custom-call(s32[3]{0:T(128)S(1)} %copy-done.47, f32[512,256]{1,0:T(8,128)S(1)} %copy-done.21, f32[4,256,128]{2,1,0:T(8,128)S(1)} %copy-done.12, f32[4,256,128]{2,1,0:T(8,128)S(1)} %collective-permute-done.14.refs_2_.refs_5_, f32[512,1024]{1,0:T(8,128)S(1)} %copy-done, ...), custom_call_target="tpu_custom_call" | custom-call | tf_op jit(solution)/shard_map/pallas_call | solution.py:105
  138.3 12.1 %all_to_all.56 = f32[32,1,128]{2,1,0:T(1,128)} all-to-all(f32[32,1,128]{2,1,0:T(1,128)S(1)} %bitcast.80), channel_id=1, replica_groups=mesh['pix'=16,'col'=2] {'pix','col'}, dimensions={0} | all-to-all | bytes 32768 | tf_op jit(solution)/shard_map/all_to_all | solution.py:49
  150.4 3.9 %collective-permute-start.18 = (f32[256,1152]{1,0:T(8,128)}, f32[256,1152]{1,0:T(8,128)S(1)}, u32[]{:S(2)}, u32[]{:S(2)}) collective-permute-start(f32[256,1152]{1,0:T(8,128)} %shard_map.77.refs_0_), channel_id=1, source_target_pairs={{4,10},{6,8},{8,6},{10,4},{12,18},{14,16},{16,14},{18,12},{20,26},... | collective-permute-start | bytes 3538952 | tf_op jit(solution)/shard_map/ppermute | solution.py:36
  159.1 5.8 %shard_map.75 = (f32[512,1024]{1,0:T(8,128)}, f32[256,1024]{1,0:T(8,128)S(1)}, f32[512,256]{1,0:T(8,128)S(1)}) custom-call(s32[3]{0:T(128)S(1)} %copy-done.47, f32[32,128]{1,0:T(8,128)S(1)} %bitcast.73, f32[512,1024]{1,0:T(8,128)S(1)} %copy-done.11, f32[512,1024]{1,0:T(8,128)} %get-tuple-element.41.refs_2_, f32[256,1024]{1,0:T(8,128)S(1)} %copy-done.8, ...), custom_call_target="tpu_custom_call" | custom-call | tf_op jit(solution)/shard_map/pallas_call | solution.py:105
  167.8 6.6 %collective-permute-done.16 = f32[256,256]{1,0:T(8,128)S(1)} collective-permute-done((f32[256,256]{1,0:T(8,128)S(1)}, f32[256,256]{1,0:T(8,128)S(1)}, u32[]{:S(2)}, u32[]{:S(2)}) %collective-permute-start.16) | collective-permute-done | bytes 262176 | tf_op jit(solution)/shard_map/ppermute | solution.py:43
  176.7 3.7 %shard_map.76 = (f32[512,1024]{1,0:T(8,128)}, f32[32,128]{1,0:T(8,128)S(1)}) custom-call(s32[3]{0:T(128)S(1)} %copy-done.47, f32[256,256]{1,0:T(8,128)S(1)} %add.69.refs_0_.refs_3_, f32[256,256]{1,0:T(8,128)S(1)} %collective-permute-done.17.refs_1_.refs_4_, f32[256,1024]{1,0:T(8,128)S(1)} %get-tuple-element.43.refs_2_.refs_1_.refs_12_, f32[512,1024]{1,0:T(8,128)S(1)} %copy-done), custom_call_target="tpu_custom_call" | custom-call | tf_op jit(solution)/shard_map/pallas_call | solution.py:105
  180.4 7.6 %all_to_all.57 = f32[32,1,128]{2,1,0:T(1,128)S(1)} all-to-all(f32[32,1,128]{2,1,0:T(1,128)S(1)} %bitcast.81), channel_id=1, replica_groups=mesh['pix'=16,'col'=2] {'pix','col'}, dimensions={0} | all-to-all | bytes 32768 | tf_op jit(solution)/shard_map/all_to_all | solution.py:49
  188.0 5.7 %shard_map.78 = (f32[512,256]{1,0:T(8,128)S(1)}, f32[512,1024]{1,0:T(8,128)}, f32[4,256,128]{2,1,0:T(8,128)S(1)}, f32[4,256,128]{2,1,0:T(8,128)S(1)}) custom-call(s32[3]{0:T(128)S(1)} %copy-done.47, f32[32,128]{1,0:T(8,128)S(1)} %bitcast.74, f32[32,128]{1,0:T(8,128)S(1)} %bitcast.77, f32[512,256]{1,0:T(8,128)S(1)} %copy-done.22, ...), custom_call_target="tpu_custom_call" | custom-call | tf_op jit(solution)/shard_map/pallas_call | solution.py:105
  195.6 12.5 %collective-permute-done.19.refs_1_ = f32[4,256,128]{2,1,0:T(8,128)} collective-permute-done((f32[4,256,128]{2,1,0:T(8,128)S(1)}, f32[4,256,128]{2,1,0:T(8,128)}, u32[]{:S(2)}, u32[]{:S(2)}) %collective-permute-start.19) | collective-permute-done | bytes 524320 | tf_op jit(solution)/shard_map/ppermute | solution.py:25
  219.4 6.7 %collective-permute-done.22 = f32[256,128]{1,0:T(8,128)S(1)} collective-permute-done((f32[256,128]{1,0:T(8,128)S(1)}, f32[256,128]{1,0:T(8,128)S(1)}, u32[]{:S(2)}, u32[]{:S(2)}) %collective-permute-start.22) | collective-permute-done | bytes 131104 | tf_op jit(solution)/shard_map/ppermute | solution.py:25
  230.9 4.9 %collective-permute-start.31 = (f32[256,256]{1,0:T(8,128)}, f32[256,256]{1,0:T(8,128)}, u32[]{:S(2)}, u32[]{:S(2)}) collective-permute-start(f32[256,256]{1,0:T(8,128)} %slice.47), channel_id=1, source_target_pairs={{4,8},{6,10},{8,4},{10,6},{12,16},{14,18},{16,12},{18,14},{20,24},... | collective-permute-start | bytes 786440 | tf_op jit(solution)/shard_map/ppermute | solution.py:36
  235.9 4.5 %collective-permute-done.25 = f32[256,128]{1,0:T(8,128)S(1)} collective-permute-done((f32[256,128]{1,0:T(8,128)S(1)}, f32[256,128]{1,0:T(8,128)S(1)}, u32[]{:S(2)}, u32[]{:S(2)}) %collective-permute-start.25) | collective-permute-done | bytes 131104 | tf_op jit(solution)/shard_map/ppermute | solution.py:25
  242.8 6.2 %collective-permute-done.29.refs_8_.refs_5_ = f32[256,256]{1,0:T(8,128)S(1)} collective-permute-done((f32[256,256]{1,0:T(8,128)}, f32[256,256]{1,0:T(8,128)S(1)}, u32[]{:S(2)}, u32[]{:S(2)}) %collective-permute-start.29) | collective-permute-done | bytes 262176 | tf_op jit(solution)/shard_map/ppermute | solution.py:36
  252.4 11.1 %shard_map.83 = (f32[4,256,1024]{2,1,0:T(8,128)}, f32[4,256,1024]{2,1,0:T(8,128)}) custom-call(s32[3]{0:T(128)S(1)} %copy-done.47, f32[256,1152]{1,0:T(8,128)} %collective-permute-done.13.refs_1_.refs_0_.refs_4_, f32[256,1152]{1,0:T(8,128)} %collective-permute-done.26.refs_1_.refs_5_, f32[256,1152]{1,0:T(8,128)S(1)} %collective-permute-done.5.refs_7_.refs_2_.refs_6_, ...), custom_call_target="tpu_custom_call" | custom-call | tf_op jit(solution)/shard_map/pallas_call | solution.py:105
  263.5 3.8 %shard_map.81 = (f32[512,1024]{1,0:T(8,128)}, f32[32,128]{1,0:T(8,128)}) custom-call(s32[3]{0:T(128)S(1)} %copy-done.47, f32[512,256]{1,0:T(8,128)S(1)} %copy-done.30, f32[4,256,128]{2,1,0:T(8,128)S(1)} %copy-done.16, f32[4,256,128]{2,1,0:T(8,128)S(1)} %collective-permute-done.27.refs_2_, f32[512,1024]{1,0:T(8,128)S(1)} %copy-done, f32[512,1024]{1,0:T(8,128)S(1)} %copy-done.9), custom_call_target="tpu_custom_call" | custom-call | tf_op jit(solution)/shard_map/pallas_call | solution.py:105
  277.1 14.9 %shard_map.84 = (f32[256,1024]{1,0:T(8,128)S(1)}, f32[256,1024]{1,0:T(8,128)}) custom-call(s32[3]{0:T(128)S(1)} %copy-done.47, f32[32,128]{1,0:T(8,128)S(1)} %bitcast.75, f32[2,256,1024]{2,1,0:T(8,128)} %bitcast.66, f32[2,256,1024]{2,1,0:T(8,128)} %bitcast.82, f32[4,256,1024]{2,1,0:T(8,128)} %get-tuple-element.53.refs_3_, ...), custom_call_target="tpu_custom_call" | custom-call | tf_op jit(solution)/shard_map/pallas_call | solution.py:105
  (196 shorter events, 121.5 us)
Async XLA Ops:
  31.2 33.4 %collective-permute-start.5 = (f32[256,1152]{1,0:T(8,128)}, f32[256,1152]{1,0:T(8,128)S(1)}, u32[]{:S(2)}, u32[]{:S(2)}) collective-permute-start(f32[256,1152]{1,0:T(8,128)} %shard_map.70.refs_0_), channel_id=1, source_target_pairs={{4,8},{6,10},{8,4},{10,6},{12,16},{14,18},{16,12},{18,14},{20,24},... | collective-permute-start | bytes 3538952 | tf_op jit(solution)/shard_map/ppermute | solution.py:36
  42.3 7.6 %collective-permute-start.3 = (f32[256,256]{1,0:T(8,128)S(1)}, f32[256,256]{1,0:T(8,128)S(1)}, u32[]{:S(2)}, u32[]{:S(2)}) collective-permute-start(f32[256,256]{1,0:T(8,128)S(1)} %slice_add_fusion), channel_id=1, source_target_pairs={{0,1},{1,0},{2,3},{3,2},{4,5},{5,4},{6,7},{7,6},{8,9},{9,8},{10,11... | collective-permute-start | bytes 786440 | tf_op jit(solution)/shard_map/ppermute | solution.py:43
  56.7 7.9 %all-to-all-start.1 = ((f32[32,1,128]{2,1,0:T(1,128)}), f32[32,1,128]{2,1,0:T(1,128)}, u32[]{:S(2)}, u32[]{:S(2)}) async-start(f32[32,1,128]{2,1,0:T(1,128)} %bitcast.78), calls=%async_computation.1 | async-start | bytes 32768 | tf_op jit(solution)/shard_map/all_to_all | solution.py:49
  75.8 12.8 %collective-permute-start.6 = (f32[4,256,128]{2,1,0:T(8,128)S(1)}, f32[4,256,128]{2,1,0:T(8,128)}, u32[]{:S(2)}, u32[]{:S(2)}) collective-permute-start(f32[4,256,128]{2,1,0:T(8,128)S(1)} %get-tuple-element.38), channel_id=1, source_target_pairs={{0,4},{2,6},{4,0},{6,2},{8,12},{10,14},{12,8},{14,10},{16,20},{18,... | collective-permute-start | bytes 1572872 | tf_op jit(solution)/shard_map/ppermute | solution.py:25
  88.6 30.1 %collective-permute-start.13 = (f32[256,1152]{1,0:T(8,128)}, f32[256,1152]{1,0:T(8,128)}, u32[]{:S(2)}, u32[]{:S(2)}) collective-permute-start(f32[256,1152]{1,0:T(8,128)} %shard_map.72), channel_id=1, source_target_pairs={{0,4},{2,6},{4,0},{6,2},{8,12},{10,14},{12,8},{14,10},{16,20},{18,... | collective-permute-start | bytes 3538952 | tf_op jit(solution)/shard_map/ppermute | solution.py:36
  91.6 5.9 %collective-permute-start.8 = (f32[256,128]{1,0:T(8,128)S(1)}, f32[256,128]{1,0:T(8,128)S(1)}, u32[]{:S(2)}, u32[]{:S(2)}) collective-permute-start(f32[256,128]{1,0:T(8,128)S(1)} %get-tuple-element.68), channel_id=1, source_target_pairs={{0,16},{2,18},{4,20},{6,22},{8,24},{10,26},{12,28},{14,30},{16,0},... | collective-permute-start | bytes 393224 | tf_op jit(solution)/shard_map/ppermute | solution.py:25
  91.9 12.0 %collective-permute-start.9 = (f32[256,128]{1,0:T(8,128)S(1)}, f32[256,128]{1,0:T(8,128)S(1)}, u32[]{:S(2)}, u32[]{:S(2)}) collective-permute-start(f32[256,128]{1,0:T(8,128)S(1)} %get-tuple-element.67), channel_id=1, source_target_pairs={{0,24},{2,26},{4,28},{6,30},{8,16},{10,18},{12,20},{14,22},{16,8},... | collective-permute-start | bytes 393224 | tf_op jit(solution)/shard_map/ppermute | solution.py:25
  104.1 6.2 %collective-permute-start.11 = (f32[256,128]{1,0:T(8,128)S(1)}, f32[256,128]{1,0:T(8,128)S(1)}, u32[]{:S(2)}, u32[]{:S(2)}) collective-permute-start(f32[256,128]{1,0:T(8,128)S(1)} %fusion.5), channel_id=1, source_target_pairs={{0,16},{2,18},{4,20},{6,22},{8,24},{10,26},{12,28},{14,30},{16,0},... | collective-permute-start | bytes 393224 | tf_op jit(solution)/shard_map/ppermute | solution.py:25
  105.9 12.0 %collective-permute-start.12 = (f32[256,128]{1,0:T(8,128)S(1)}, f32[256,128]{1,0:T(8,128)S(1)}, u32[]{:S(2)}, u32[]{:S(2)}) collective-permute-start(f32[256,128]{1,0:T(8,128)S(1)} %fusion.5), channel_id=1, source_target_pairs={{0,24},{2,26},{4,28},{6,30},{8,16},{10,18},{12,20},{14,22},{16,8},... | collective-permute-start | bytes 393224 | tf_op jit(solution)/shard_map/ppermute | solution.py:25
  118.7 11.9 %collective-permute-start.14 = (f32[4,256,128]{2,1,0:T(8,128)}, f32[4,256,128]{2,1,0:T(8,128)S(1)}, u32[]{:S(2)}, u32[]{:S(2)}) collective-permute-start(f32[4,256,128]{2,1,0:T(8,128)} %shard_map.73.refs_1_.refs_4_), channel_id=1, source_target_pairs={{0,4},{2,6},{4,0},{6,2},{8,12},{10,14},{12,8},{14,10},{16,20},{18,... | collective-permute-start | bytes 1572872 | tf_op jit(solution)/shard_map/ppermute | solution.py:25
  150.4 37.6 %collective-permute-start.18 = (f32[256,1152]{1,0:T(8,128)}, f32[256,1152]{1,0:T(8,128)S(1)}, u32[]{:S(2)}, u32[]{:S(2)}) collective-permute-start(f32[256,1152]{1,0:T(8,128)} %shard_map.77.refs_0_), channel_id=1, source_target_pairs={{4,10},{6,8},{8,6},{10,4},{12,18},{14,16},{16,14},{18,12},{20,26},... | collective-permute-start | bytes 3538952 | tf_op jit(solution)/shard_map/ppermute | solution.py:36
  166.7 7.8 %collective-permute-start.16 = (f32[256,256]{1,0:T(8,128)S(1)}, f32[256,256]{1,0:T(8,128)S(1)}, u32[]{:S(2)}, u32[]{:S(2)}) collective-permute-start(f32[256,256]{1,0:T(8,128)S(1)} %slice_add_fusion.1), channel_id=1, source_target_pairs={{0,1},{1,0},{2,3},{3,2},{4,5},{5,4},{6,7},{7,6},{8,9},{9,8},{10,11... | collective-permute-start | bytes 786440 | tf_op jit(solution)/shard_map/ppermute | solution.py:43
  195.3 12.8 %collective-permute-start.19 = (f32[4,256,128]{2,1,0:T(8,128)S(1)}, f32[4,256,128]{2,1,0:T(8,128)}, u32[]{:S(2)}, u32[]{:S(2)}) collective-permute-start(f32[4,256,128]{2,1,0:T(8,128)S(1)} %get-tuple-element.49), channel_id=1, source_target_pairs={{0,4},{2,6},{4,0},{6,2},{8,12},{10,14},{12,8},{14,10},{16,20},{18,... | collective-permute-start | bytes 1572872 | tf_op jit(solution)/shard_map/ppermute | solution.py:25
  208.1 33.1 %collective-permute-start.26 = (f32[256,1152]{1,0:T(8,128)}, f32[256,1152]{1,0:T(8,128)}, u32[]{:S(2)}, u32[]{:S(2)}) collective-permute-start(f32[256,1152]{1,0:T(8,128)} %shard_map.79), channel_id=1, source_target_pairs={{0,6},{2,4},{4,2},{6,0},{8,14},{10,12},{12,10},{14,8},{16,22},{18,... | collective-permute-start | bytes 3538952 | tf_op jit(solution)/shard_map/ppermute | solution.py:36
  211.3 5.9 %collective-permute-start.20 = (f32[256,128]{1,0:T(8,128)S(1)}, f32[256,128]{1,0:T(8,128)S(1)}, u32[]{:S(2)}, u32[]{:S(2)}) collective-permute-start(f32[256,128]{1,0:T(8,128)S(1)} %get-tuple-element.63), channel_id=1, source_target_pairs={{0,8},{2,10},{4,12},{6,14},{8,0},{10,2},{12,4},{14,6},{16,24},{18,... | collective-permute-start | bytes 393224 | tf_op jit(solution)/shard_map/ppermute | solution.py:25
  212.5 6.9 %collective-permute-start.21 = (f32[256,128]{1,0:T(8,128)S(1)}, f32[256,128]{1,0:T(8,128)S(1)}, u32[]{:S(2)}, u32[]{:S(2)}) collective-permute-start(f32[256,128]{1,0:T(8,128)S(1)} %get-tuple-element.65), channel_id=1, source_target_pairs={{0,16},{2,18},{4,20},{6,22},{8,24},{10,26},{12,28},{14,30},{16,0},... | collective-permute-start | bytes 393224 | tf_op jit(solution)/shard_map/ppermute | solution.py:25
  212.8 13.2 %collective-permute-start.22 = (f32[256,128]{1,0:T(8,128)S(1)}, f32[256,128]{1,0:T(8,128)S(1)}, u32[]{:S(2)}, u32[]{:S(2)}) collective-permute-start(f32[256,128]{1,0:T(8,128)S(1)} %get-tuple-element.64), channel_id=1, source_target_pairs={{0,24},{2,26},{4,28},{6,30},{8,16},{10,18},{12,20},{14,22},{16,8},... | collective-permute-start | bytes 393224 | tf_op jit(solution)/shard_map/ppermute | solution.py:25
  226.1 4.9 %collective-permute-start.23 = (f32[256,128]{1,0:T(8,128)S(1)}, f32[256,128]{1,0:T(8,128)S(1)}, u32[]{:S(2)}, u32[]{:S(2)}) collective-permute-start(f32[256,128]{1,0:T(8,128)S(1)} %fusion.2), channel_id=1, source_target_pairs={{0,8},{2,10},{4,12},{6,14},{8,0},{10,2},{12,4},{14,6},{16,24},{18,... | collective-permute-start | bytes 393224 | tf_op jit(solution)/shard_map/ppermute | solution.py:25
  226.2 9.7 %collective-permute-start.24 = (f32[256,128]{1,0:T(8,128)S(1)}, f32[256,128]{1,0:T(8,128)S(1)}, u32[]{:S(2)}, u32[]{:S(2)}) collective-permute-start(f32[256,128]{1,0:T(8,128)S(1)} %fusion.2), channel_id=1, source_target_pairs={{0,16},{2,18},{4,20},{6,22},{8,24},{10,26},{12,28},{14,30},{16,0},... | collective-permute-start | bytes 393224 | tf_op jit(solution)/shard_map/ppermute | solution.py:25
  227.6 12.7 %collective-permute-start.25 = (f32[256,128]{1,0:T(8,128)S(1)}, f32[256,128]{1,0:T(8,128)S(1)}, u32[]{:S(2)}, u32[]{:S(2)}) collective-permute-start(f32[256,128]{1,0:T(8,128)S(1)} %fusion.2), channel_id=1, source_target_pairs={{0,24},{2,26},{4,28},{6,30},{8,16},{10,18},{12,20},{14,22},{16,8},... | collective-permute-start | bytes 393224 | tf_op jit(solution)/shard_map/ppermute | solution.py:25
  229.5 19.5 %collective-permute-start.29 = (f32[256,256]{1,0:T(8,128)}, f32[256,256]{1,0:T(8,128)S(1)}, u32[]{:S(2)}, u32[]{:S(2)}) collective-permute-start(f32[256,256]{1,0:T(8,128)} %slice.47), channel_id=1, source_target_pairs={{0,4},{2,6},{4,0},{6,2},{8,12},{10,14},{12,8},{14,10},{16,20},{18,... | collective-permute-start | bytes 786440 | tf_op jit(solution)/shard_map/ppermute | solution.py:36
  230.9 18.1 %collective-permute-start.31 = (f32[256,256]{1,0:T(8,128)}, f32[256,256]{1,0:T(8,128)}, u32[]{:S(2)}, u32[]{:S(2)}) collective-permute-start(f32[256,256]{1,0:T(8,128)} %slice.47), channel_id=1, source_target_pairs={{4,8},{6,10},{8,4},{10,6},{12,16},{14,18},{16,12},{18,14},{20,24},... | collective-permute-start | bytes 786440 | tf_op jit(solution)/shard_map/ppermute | solution.py:36
  241.2 22.3 %collective-permute-start.27 = (f32[4,256,128]{2,1,0:T(8,128)}, f32[4,256,128]{2,1,0:T(8,128)S(1)}, u32[]{:S(2)}, u32[]{:S(2)}) collective-permute-start(f32[4,256,128]{2,1,0:T(8,128)} %shard_map.80.refs_1_), channel_id=1, source_target_pairs={{0,4},{2,6},{4,0},{6,2},{8,12},{10,14},{12,8},{14,10},{16,20},{18,... | collective-permute-start | bytes 1572872 | tf_op jit(solution)/shard_map/ppermute | solution.py:25
  267.3 7.9 %all-to-all-start.4 = ((f32[32,1,128]{2,1,0:T(1,128)}), f32[32,1,128]{2,1,0:T(1,128)S(1)}, u32[]{:S(2)}, u32[]{:S(2)}) async-start(f32[32,1,128]{2,1,0:T(1,128)} %bitcast.32), calls=%async_computation.4 | async-start | bytes 32768 | tf_op jit(solution)/shard_map/all_to_all | solution.py:49
  (62 other events, 357.9 us)

commit v3 on v2

v3 whole, which is shorter than its diff:
```python
import functools

import jax
import jax.numpy as jnp
from jax import lax
from jax.experimental import pallas as pl
from jax.experimental.pallas import tpu as pltpu
from jax.sharding import PartitionSpec as P

BANDS = 8
WIDTH = 256
ITERS = 2
PASSES = 2
LANES = 128
GROUP = 8

threshold_scale = 1.0
diffusion = 0.2
f32 = jnp.float32
bf16 = jnp.bfloat16


def along_pix(block, distance):
    count = lax.axis_size("pix")
    return lax.ppermute(block, "pix", [(i, i ^ distance) for i in range(count)])


def to_odd_or_even(block, far, crossed):
    count = lax.axis_size("pix")
    route = []
    for i in range(count):
        chip = i // 2
        target = ((chip + 1) ^ 1) - 1 if far else chip ^ 1
        if 0 <= target < count // 2:
            route.append((i, 2 * target + (i % 2 ^ crossed)))
    return lax.ppermute(block, "pix", route)


def summed_over_col(block):
    count = lax.axis_size("col")
    step = 1
    while step < count:
        block = block + lax.ppermute(block, "col", [(i, i ^ step) for i in range(count)])
        step *= 2
    return block


def everywhere(rows):
    return lax.all_to_all(rows, ("pix", "col"), 0, 0, tiled=True)


def halves(x):
    high = x.astype(bf16)
    return high, (x - high.astype(f32)).astype(bf16)


def product(a, b, dims=((1,), (0,))):
    def part(x, y):
        return lax.dot_general(x, y, (dims, ((), ())), preferred_element_type=f32)

    return part(a[0], b[0]) + (part(a[0], b[1]) + part(a[1], b[0]))


def rows_folded(x):
    return jnp.sum(x.reshape(x.shape[0] // 8, 8, x.shape[1]), axis=0)


def whole_sum(x):
    return jnp.sum(jnp.sum(x, axis=0, keepdims=True), axis=1, keepdims=True)


def packed_sums(shape, sums):
    lane = lax.broadcasted_iota(jnp.int32, shape, 1)
    packed = jnp.zeros(shape, f32)
    for place, value in enumerate(sums):
        packed = packed + jnp.where(lane == place, value, 0.0)
    return packed


def read_sums(ref, count):
    total = jnp.sum(ref[...], axis=0, keepdims=True)
    return [total[:, k : k + 1] for k in range(count)]


def spread_mask(mask, chip, step):
    dates = mask.shape[1]
    date = lax.broadcasted_iota(jnp.int32, (dates, 2 * LANES), 0)
    lane = lax.broadcasted_iota(jnp.int32, (dates, 2 * LANES), 1)
    chunk = chip ^ (2 * step + lane // LANES)
    pick = (date == chunk * (LANES // BANDS) + lane % LANES // BANDS).astype(bf16)
    return jnp.dot(mask.astype(bf16), pick, preferred_element_type=f32)


def call(kernel, grid, in_specs, out_specs, out_shape, scratch, *args, place=None, after=()):
    single = not isinstance(out_shape, (list, tuple))
    if single:
        out_specs, out_shape = [out_specs], [out_shape]
    inputs = len(in_specs)
    lead = 0 if place is None else 1

    def body(*refs):
        used = lead + inputs
        kernel(*refs[:used], *refs[used + len(after) :])

    results = pl.pallas_call(
        body,
        grid_spec=pltpu.PrefetchScalarGridSpec(
            num_scalar_prefetch=lead,
            grid=grid,
            in_specs=list(in_specs) + [pl.BlockSpec(memory_space=pl.ANY)] * len(after),
            out_specs=list(out_specs),
            scratch_shapes=scratch,
        ),
        out_shape=list(out_shape),
        compiler_params=pltpu.CompilerParams(vmem_limit_bytes=24 * 2**20),
    )(*([place] if lead else []), *args, *after)
    return results[0] if single else results


def in_hbm(array):
    return pltpu.with_memory_space_constraint(array, pltpu.HBM)


def held_until(array, *after):
    def body(*refs):
        pass

    anywhere = pl.BlockSpec(memory_space=pl.ANY)
    return pl.pallas_call(
        body,
        in_specs=[anywhere] * (1 + len(after)),
        out_specs=anywhere,
        out_shape=jax.ShapeDtypeStruct(array.shape, array.dtype),
        input_output_aliases={0: 0},
    )(array, *after)


def whole(shape):
    return pl.BlockSpec(shape, lambda t, *s: (0,) * len(shape))


def tile(rows, cols):
    return pl.BlockSpec((rows, cols), lambda t, *s: (0, t))


def shaped(*shape):
    return jax.ShapeDtypeStruct(shape, f32)


def split_factor(refs, high_ref, low_ref):
    pixels = refs[0].shape[0]
    for part, ref in enumerate(refs):
        rows = slice(part * pixels, (part + 1) * pixels)
        high_ref[rows], low_ref[rows] = halves(ref[...])


def start_kernel(place, own_0, own_1, own_mask, other_0, other_1, other_mask, own_u, other_u, v_0, v_1,
                 res_ref, weight_ref, vt_ref, sums_ref, u_high, u_low, acc):
    step = pl.program_id(0)
    pixels = own_u.shape[0]

    @pl.when(step == 0)
    def _():
        split_factor((own_u, other_u), u_high, u_low)
        acc[...] = jnp.zeros_like(acc)

    vt = jnp.concatenate([v_0[...].T, v_1[...].T], axis=1)
    vt_ref[...] = vt
    low_rank = product((u_high[...], u_low[...]), halves(vt))
    strips = ((own_0, own_1, own_mask), (other_0, other_1, other_mask))
    for part, (left, right, mask) in enumerate(strips):
        rows = slice(part * pixels, (part + 1) * pixels)
        weight = spread_mask(mask[...], place[1], step)
        obs = jnp.concatenate([left[...], right[...]], axis=1)
        res = weight * (obs - low_rank[rows])
        weight_ref[rows] = weight
        res_ref[rows] = res
        acc[...] += rows_folded(res * res)

    @pl.when(step == pl.num_programs(0) - 1)
    def _():
        sums_ref[...] = packed_sums(sums_ref.shape, [whole_sum(acc[...])])


def level_from(spread, total):
    return threshold_scale * jnp.sqrt(jnp.maximum(spread, 0.0) / total + 1e-06)


def add_parts(step, part, own_ref, other_ref):
    pixels = own_ref.shape[0]

    @pl.when(step == 0)
    def _():
        own_ref[...] = part[:pixels]
        other_ref[...] = part[pixels:]

    @pl.when(step > 0)
    def _():
        own_ref[...] += part[:pixels]
        other_ref[...] += part[pixels:]


def first_grad_kernel(total, sums_ref, res_ref, vt_ref, own_ref, other_ref):
    (spread,) = read_sums(sums_ref, 1)
    level = level_from(spread, total)
    misfit = -jnp.clip(res_ref[...], -level, level)
    part = product(halves(misfit), halves(vt_ref[...]), ((1,), (1,)))
    add_parts(pl.program_id(0), part, own_ref, other_ref)


def column_sums(sums):
    top, curve, cross, before = sums
    step = top / curve
    return step, before + 2.0 * step * cross + step * step * curve


def next_grad_kernel(total, sums_ref, res_ref, shift_ref, vt_ref, even_ref, odd_ref,
                     res_out, vt_out, own_ref, other_ref):
    size, spread = column_sums(read_sums(sums_ref, 4))
    level = level_from(spread, total)
    grad = jnp.concatenate([even_ref[0], odd_ref[0]], axis=1)
    vt = vt_ref[...] - size * grad
    vt_out[...] = vt
    res = res_ref[...] + size * shift_ref[...]
    res_out[...] = res
    misfit = -jnp.clip(res, -level, level)
    part = product(halves(misfit), halves(vt), ((1,), (1,)))
    add_parts(pl.program_id(0), part, own_ref, other_ref)


def change_kernel(col_count, own_grad, other_grad, vt_ref, weight_ref,
                  change_ref, sums_ref, g_high, g_low, acc):
    step = pl.program_id(0)

    @pl.when(step == 0)
    def _():
        split_factor((own_grad, other_grad), g_high, g_low)
        acc[...] = jnp.zeros_like(acc)

    change = weight_ref[...] * product((g_high[...], g_low[...]), halves(vt_ref[...]))
    change_ref[...] = change
    acc[...] += rows_folded(change * change)

    @pl.when(step == pl.num_programs(0) - 1)
    def _():
        top = whole_sum(own_grad[...] * own_grad[...]) / col_count
        sums_ref[...] = packed_sums(sums_ref.shape, [top, whole_sum(acc[...])])


def pix_step_kernel(total, first, level_sums, sums_ref, own_u, other_u, own_grad, other_grad, res_ref,
                    change_ref, own_out, other_out, res_out, even_ref, odd_ref, ut_high, ut_low):
    step = pl.program_id(0)
    pixels = own_grad.shape[0]
    top, curve = read_sums(sums_ref, 2)
    size = top / curve
    if first:
        (spread,) = read_sums(level_sums, 1)
    else:
        _, spread = column_sums(read_sums(level_sums, 4))
    level = level_from(spread, total)

    @pl.when(step == 0)
    def _():
        strips = ((own_u, own_grad, own_out), (other_u, other_grad, other_out))
        for part, (old, grad, out) in enumerate(strips):
            u = old[...] - size * grad[...]
            out[...] = u
            cols = slice(part * pixels, (part + 1) * pixels)
            ut_high[:, cols], ut_low[:, cols] = halves(u.T)

    res = res_ref[...]
    moved = size * change_ref[...]
    res_out[...] = res + moved
    misfit = -(jnp.clip(res, -level, level) + moved)
    grad = product((ut_high[...], ut_low[...]), halves(misfit))
    even_ref[0] = grad[:, :LANES]
    odd_ref[0] = grad[:, LANES:]


def shift_kernel(chips, own_u, other_u, even_ref, odd_ref, weight_ref, res_ref,
                 shift_ref, sums_ref, u_high, u_low, acc, acc_top):
    step = pl.program_id(0)

    @pl.when(step == 0)
    def _():
        split_factor((own_u, other_u), u_high, u_low)
        acc[...] = jnp.zeros_like(acc)
        acc_top[...] = jnp.zeros_like(acc_top)

    grad = jnp.concatenate([even_ref[0], odd_ref[0]], axis=1)
    acc_top[...] += rows_folded(grad * grad)
    shift = weight_ref[...] * product((u_high[...], u_low[...]), halves(grad))
    shift_ref[...] = shift
    res = res_ref[...]
    acc[0] += rows_folded(shift * shift)
    acc[1] += rows_folded(shift * res)
    acc[2] += rows_folded(res * res)

    @pl.when(step == pl.num_programs(0) - 1)
    def _():
        sums = [whole_sum(acc_top[...]) / chips] + [whole_sum(acc[k]) for k in range(3)]
        sums_ref[...] = packed_sums(sums_ref.shape, sums)


def rim_kernel(place, *refs):
    obs = refs[0:8]
    mask = refs[8:12]
    factors = refs[12:16]
    vt_ref, res_ref, weight_ref, u_high, u_low = refs[16:]
    step = pl.program_id(0)
    pixels = factors[0].shape[0]

    @pl.when(step == 0)
    def _():
        split_factor(factors, u_high, u_low)

    low_rank = product((u_high[...], u_low[...]), halves(vt_ref[...]))
    for part in range(4):
        weight = spread_mask(mask[part][...], place[1], step)
        weight_ref[part] = weight
        rows = jnp.concatenate([obs[2 * part][...], obs[2 * part + 1][...]], axis=1)
        res_ref[part] = weight * (rows - low_rank[part * pixels : (part + 1) * pixels])


def add_kernel(kept_ref, from_ref, *out_refs):
    for k, ref in enumerate(out_refs):
        ref[...] = kept_ref[k] + from_ref[k]


def stack_kernel(*refs):
    for k, ref in enumerate(refs[:-1]):
        refs[-1][k] = ref[...]


def flux_of(diff, inverse):
    ratio = diff * inverse
    below = 1.0 + ratio * ratio
    guess = pl.reciprocal(below, approx=True)
    return diff * (guess * (2.0 - below * guess))


def smooth_kernel(total, chips, place, sums_ref, res_ref, shift_ref, rim_ref, rim_weight, *refs):
    factors = refs[:4]
    own_vt, other_vt, own_grad, other_grad, own_ref, other_ref, v_ref, u_high, u_low, rim_shift = refs[4:]
    step = pl.program_id(0)
    core, chip = place[0], place[2]
    pixels = own_ref.shape[0]

    @pl.when(step == 0)
    def _():
        split_factor(factors, u_high, u_low)

    size, spread = column_sums(read_sums(sums_ref, 4))
    level = level_from(spread, total)
    inverse = 1.0 / level
    v_ref[core] = (own_vt[...] - size * own_grad[0]).T
    v_ref[1 - core] = (other_vt[...] - size * other_grad[0]).T
    moved = product((u_high[...], u_low[...]), halves(own_grad[0]))
    rim_shift[...] = moved.reshape(rim_shift.shape)

    def cut(res):
        return res - jnp.clip(res, -level, level)

    def own(k):
        return cut(res_ref[k] + size * shift_ref[k])

    def rim(k):
        return cut(rim_ref[k] + size * (rim_weight[k] * rim_shift[k]))

    south = 2 * (chip % 2)
    north = 2 - south
    rows = [rim(north + core), rim(north + 1 - core), own(core), own(1 - core),
            rim(south + core), rim(south + 1 - core)]
    keep_north = jnp.where(chip > 0, 1.0, 0.0).astype(f32)
    keep_south = jnp.where(chip < chips - 1, 1.0, 0.0).astype(f32)
    last = lax.broadcasted_iota(jnp.int32, (pixels, LANES), 0) % WIDTH == WIDTH - 1
    scaled = diffusion

    def smoothed(rows, north_edge, south_edge):
        count = len(rows)
        cross = []
        for k in range(count - 1):
            flux = flux_of(rows[k + 1] - rows[k], inverse)
            if k == north_edge:
                flux = flux * keep_north
            if k == south_edge:
                flux = flux * keep_south
            cross.append(flux)
        out = []
        for k in range(1, count - 1):
            east = jnp.where(last, 0.0, flux_of(pltpu.roll(rows[k], pixels - 1, 0) - rows[k], inverse))
            along = east - pltpu.roll(east, 1, 0)
            out.append(rows[k] + scaled * ((cross[k] - cross[k - 1]) + along))
        return out

    rows = smoothed(rows, 1, 3)
    rows = smoothed(rows, 0, 2)
    even, odd = rows
    own_ref[...] = jnp.where(core == 0, even, odd)
    other_ref[...] = jnp.where(core == 0, odd, even)


def grad_over_chips(even, odd, half):
    chips = lax.axis_size("pix") // 2
    count, rank, lanes = even.shape
    block = whole((rank, lanes))
    blocks = whole(even.shape)
    from_odd = along_pix(odd, 2)
    half = held_until(half, from_odd)
    kept = call(add_kernel, (1,), [blocks] * 2, [block] * count, [shaped(rank, lanes)] * count, [], even, from_odd)
    mine = kept[0]
    for part in [along_pix(kept[k], 4 * k) for k in (1, 2, 3)]:
        mine = mine + part
    distance = GROUP
    while distance < chips:
        mine = mine + along_pix(mine, 2 * distance)
        distance *= 2
    parts = [mine] + [along_pix(mine, 4 * k) for k in (1, 2, 3)]
    return parts, half


def per_device(observed, valid_mask, pix_factor, col_factor):
    pix_count = lax.axis_size("pix")
    col_count = lax.axis_size("col")
    devices = pix_count * col_count
    chips = pix_count // 2
    pixels, columns = observed.shape
    rank = pix_factor.shape[1]
    half = columns // 2
    dates = valid_mask.shape[1] // 2
    total = float(pixels * columns * pix_count * col_count)
    assert pixels == WIDTH and half == GROUP * LANES and chips % GROUP == 0 and PASSES == 2
    index = lax.axis_index("pix")
    core = index % 2
    chip = index // 2
    place = jnp.stack([core, chip % GROUP, chip]).astype(jnp.int32)

    def half_of(which):
        obs = lax.dynamic_slice(observed, (0, which * half), (pixels, half))
        mask = lax.dynamic_slice(valid_mask, (0, which * dates), (pixels, dates))
        return in_hbm(jnp.concatenate([obs, mask.astype(f32)], axis=1))

    other_half = half_of(1 - core)
    received = in_hbm(along_pix(other_half, 1))
    own_half = half_of(core)
    other_u = along_pix(pix_factor, 1)
    own_u = pix_factor
    sent = [own_half, other_half]
    rims = []

    both = 2 * pixels
    wide = 2 * LANES
    steps = half // wide
    chunk_in = [
        pl.BlockSpec((pixels, LANES), lambda t, s: (0, s[1] ^ (2 * t))),
        pl.BlockSpec((pixels, LANES), lambda t, s: (0, s[1] ^ (2 * t + 1))),
    ]
    mask_in = pl.BlockSpec((pixels, dates), lambda t, s: (0, half // dates))
    sums_shape = pltpu.HBM((devices, LANES), f32)
    pix_block = whole((pixels, rank))
    pix_shape = shaped(pixels, rank)
    sums_block = whole((devices, LANES))
    tile_block = tile(both, wide)
    vt_block = tile(rank, wide)
    grad_block = pl.BlockSpec((1, rank, LANES), lambda t: (t, 0, 0))
    grad_shape = shaped(steps, rank, LANES)
    local = pltpu.HBM((both, half), f32)
    factor_scratch = [pltpu.VMEM((both, rank), bf16)] * 2
    v_in = [
        pl.BlockSpec((LANES, rank), lambda t, s: (s[0] * GROUP + (s[1] ^ (2 * t)), 0)),
        pl.BlockSpec((LANES, rank), lambda t, s: (s[0] * GROUP + (s[1] ^ (2 * t + 1)), 0)),
    ]
    v = in_hbm(col_factor)

    residual, weight, vt, sums = call(
        start_kernel, (steps,),
        chunk_in + [mask_in] + chunk_in + [mask_in, pix_block, pix_block] + v_in,
        [tile_block, tile_block, vt_block, sums_block],
        [local, local, shaped(rank, half), sums_shape],
        factor_scratch + [pltpu.VMEM((8, wide), f32)],
        own_half, own_half, own_half, received, received, received, own_u, other_u, v, v, place=place,
    )
    weight = in_hbm(weight)
    level_sums = everywhere(sums)

    for iteration in range(ITERS):
        sent[iteration] = held_until(sent[iteration], level_sums)
        rims.append(in_hbm(to_odd_or_even(sent[iteration], True, iteration)))
        if iteration == 0:
            residual = in_hbm(residual)
            own_part, other_part = call(
                functools.partial(first_grad_kernel, total), (steps,),
                [sums_block, tile_block, vt_block], [pix_block] * 2, [pix_shape] * 2, [],
                level_sums, residual, vt,
            )
        else:
            residual, vt, own_part, other_part = call(
                functools.partial(next_grad_kernel, total), (steps,),
                [sums_block, tile_block, tile_block, vt_block, grad_block, grad_block],
                [tile_block, vt_block, pix_block, pix_block],
                [local, shaped(rank, half), pix_shape, pix_shape], [],
                level_sums, in_hbm(residual), in_hbm(shift), vt, even, odd,
            )
        own_grad = summed_over_col(own_part + along_pix(other_part, 1))
        other_grad = along_pix(own_grad, 1)
        change, sums = call(
            functools.partial(change_kernel, col_count), (steps,),
            [pix_block, pix_block, vt_block, tile_block], [tile_block, sums_block],
            [local, sums_shape], factor_scratch + [pltpu.VMEM((8, wide), f32)],
            own_grad, other_grad, vt, weight,
        )
        pix_sums = everywhere(sums)
        own_u, other_u, residual, even, odd = call(
            functools.partial(pix_step_kernel, total, iteration == 0), (steps,),
            [sums_block, sums_block] + [pix_block] * 4 + [tile_block, tile_block],
            [pix_block, pix_block, tile_block, grad_block, grad_block],
            [pix_shape, pix_shape, local, grad_shape, grad_shape],
            [pltpu.VMEM((rank, both), bf16)] * 2,
            level_sums, pix_sums, own_u, other_u, own_grad, other_grad, in_hbm(residual), in_hbm(change),
            after=rims[-1:],
        )
        if iteration == ITERS - 1:
            u_near = to_odd_or_even(own_u, False, 0)
            u_far = to_odd_or_even(own_u, True, 0)
            factors = [u_near, along_pix(u_near, 1), u_far, along_pix(u_far, 1)]
            other_vt = along_pix(vt, 1)
        parts, sent[iteration] = grad_over_chips(even, odd, sent[iteration])
        rims.append(in_hbm(to_odd_or_even(sent[iteration], False, iteration)))
        even = call(
            stack_kernel, (1,), [whole((rank, LANES))] * steps, whole((steps, rank, LANES)), grad_shape, [],
            *parts, after=rims[-1:],
        )
        odd = along_pix(even, 2)
        shift, sums = call(
            functools.partial(shift_kernel, chips), (steps,),
            [pix_block, pix_block, grad_block, grad_block, tile_block, tile_block], [tile_block, sums_block],
            [local, sums_shape],
            factor_scratch + [pltpu.VMEM((3, 8, wide), f32), pltpu.VMEM((8, wide), f32)],
            own_u, other_u, even, odd, weight, in_hbm(residual),
        )
        level_sums = everywhere(sums)

    rims = [rims[1], rims[3], rims[0], rims[2]]
    rim_scratch = [pltpu.VMEM((2 * both, rank), bf16)] * 2
    rim_block = pl.BlockSpec((4, pixels, wide), lambda t, s: (0, 0, t))
    rim_shape = pltpu.HBM((4, pixels, half), f32)
    rim_res, rim_weight = call(
        rim_kernel, (steps,),
        chunk_in * 4 + [mask_in] * 4 + [pix_block] * 4 + [vt_block],
        [rim_block] * 2, [rim_shape] * 2, rim_scratch,
        *[rim for rim in rims for _ in range(2)], *rims, *factors, vt, place=place, after=[sums],
    )

    def all_chunks(even, odd):
        return jnp.stack([even, odd], axis=1).reshape(GROUP, rank, LANES)

    own_chunks = all_chunks(even, odd)
    other_chunks = along_pix(own_chunks, 1)
    pair_block = pl.BlockSpec((2, pixels, LANES), lambda t, s: (0, 0, t))
    rim_block = pl.BlockSpec((4, pixels, LANES), lambda t, s: (0, 0, t))
    chunk_block = pl.BlockSpec((1, rank, LANES), lambda t, s: (t, 0, 0))
    own_cloud, other_cloud, v = call(
        functools.partial(smooth_kernel, total, chips), (GROUP,),
        [sums_block, pair_block, pair_block, rim_block, rim_block] + [pix_block] * 4
        + [tile(rank, LANES)] * 2 + [chunk_block] * 2,
        [
            pl.BlockSpec((pixels, LANES), lambda t, s: (0, s[0] * GROUP + (s[1] ^ t))),
            pl.BlockSpec((pixels, LANES), lambda t, s: (0, s[1] ^ t)),
            pl.BlockSpec((2, LANES, rank), lambda t, s: (0, s[1] ^ t, 0)),
        ],
        [shaped(pixels, columns), shaped(pixels, half), shaped(2, half, rank)],
        rim_scratch + [pltpu.VMEM((4, pixels, LANES), f32)],
        level_sums, in_hbm(residual.reshape(2, pixels, half)), in_hbm(shift.reshape(2, pixels, half)),
        in_hbm(rim_res), in_hbm(rim_weight), *factors, vt, other_vt, own_chunks, other_chunks, place=place,
    )
    from_other = along_pix(other_cloud, 1)
    cloud = lax.dynamic_update_slice(own_cloud, from_other, (0, (1 - core) * half))
    return own_u, v.reshape(columns, rank), cloud


def solution(mesh):
    in_specs = (P("pix", "col"), P("pix", "col"), P("pix", None), P("col", None))
    out_specs = (P("pix", None), P("col", None), P("pix", "col"))
    return jax.shard_map(
        per_device, mesh=mesh, in_specs=in_specs, out_specs=out_specs, check_vma=False
    )
```

time: 307 us -> 294 us (0.958)
  local copies, waits for them, and re-layouts: 33 us -> 15 us
  other arithmetic: 16.2 us -> 3.81 us
  blocking collectives: 30.2 us -> 39 us
  waiting for transfers between devices: 108 us -> 115 us
    unnamed x100 -> x38, local copies, waits for them, and re-layouts: 29.4 us -> 11.1 us
    all_to_all x3 -> x4, blocking collectives: 30.2 us -> 39 us  [everywhere(): return lax.all_to_all(rows, ('pix', 'col'), 0, 0, tiled=True)]
    ppermute x26 -> x27, waiting for transfers between devices: 82.7 us -> 89.9 us  [along_pix(): return lax.ppermute(block, 'pix', [(i, i ^ distance) for i in range(count)])]
    all_to_all x2 -> x1, waiting for transfers between devices: 6.17 us -> 0.01 us  [everywhere(): return lax.all_to_all(rows, ('pix', 'col'), 0, 0, tiled=True)]
    ppermute x6, waiting for transfers between devices: 6.23 us -> 12.3 us  [to_odd_or_even(): return lax.ppermute(block, 'pix', route)]
    concatenate x5 -> x2, other arithmetic: 7.29 us -> 2.47 us  [half_of(): return in_hbm(jnp.concatenate([obs, mask.astype(f32)], axis=1))]
    ppermute x26 -> x27, starting transfers between devices: 19.7 us -> 23.9 us  [along_pix(): return lax.ppermute(block, 'pix', [(i, i ^ distance) for i in range(count)])]
    select_n x2 -> x0, other arithmetic: 3.2 us -> none  [joined(): pair = [jnp.where(core == 0, own, other), jnp.where(core == 0, other, own)]]
  transfers between devices with their start and end apart: 36 -> 36, of which waited for: 27 -> 24; matrix products, arithmetic and copies ran while one was open for 4% -> 1% of each run, Pallas kernels for 10% -> 11%
where the time goes in v3:
time: 294 us; the launch traced here: 291 us
  waiting for transfers between devices  115 us (39%)
  Pallas kernels  71.9 us (24%)
  starting transfers between devices  45.6 us (16%)
  blocking collectives  39 us (13%)
  local copies, waits for them, and re-layouts  15 us (5%)
  other arithmetic  3.81 us (1%)
    ppermute x27, waiting for transfers between devices, along_pix(): return lax.ppermute(block, 'pix', [(i, i ^ distance) for i in range(count)])  89.9 us
    pallas_call x15, Pallas kernels, call(): pl.pallas_call(body, grid_spec=pltpu.PrefetchScalarGridSpec(num_scalar_pr...  71.9 us
    all_to_all x4, blocking collectives, everywhere(): return lax.all_to_all(rows, ('pix', 'col'), 0, 0, tiled=True)  39 us
    ppermute x27, starting transfers between devices, along_pix(): return lax.ppermute(block, 'pix', [(i, i ^ distance) for i in range(count)])  23.9 us
    ppermute x6, starting transfers between devices, to_odd_or_even(): return lax.ppermute(block, 'pix', route)  15.9 us
    ppermute x2, waiting for transfers between devices, summed_over_col(): lax.ppermute(block, 'col', [(i, i ^ step) for i in range(count)])  13 us
    ppermute x6, waiting for transfers between devices, to_odd_or_even(): return lax.ppermute(block, 'pix', route)  12.3 us
    unnamed x38, local copies, waits for them, and re-layouts  11.1 us
  transfers between devices with their start and end apart: 36, of which 24 were waited for; matrix products, arithmetic and copies ran while one was open for 1% of the time, Pallas kernels for 11%

profile of v3, /device:TPU:13, one launch (start us, length us, event | category | flops | bytes accessed | tf_op | source)
XLA Modules:
  0.0 291.4 jit_solution(3662775830334933353)
XLA Ops:
  9.5 6.6 %shard_map.67 = (f32[512,1024]{1,0:T(8,128)}, f32[512,1024]{1,0:T(8,128)}, f32[256,1024]{1,0:T(8,128)S(1)}, f32[32,128]{1,0:T(8,128)}) custom-call(s32[3]{0:T(128)S(1)} %pad_add_fusion.refs_0_, f32[256,1152]{1,0:T(8,128)} %pad_maximum_fusion.refs_1_.refs_2_.refs_3_.refs_0_, f32[256,1152]{1,0:T(8,128)} %pad_maximum_fusion.refs_1_.refs_2_.refs_3_.refs_0_, ...), custom_call_target="tpu_custom_call" | custom-call | tf_op jit(solution)/shard_map/pallas_call | solution.py:105
  16.1 10.5 %all_to_all.55 = f32[32,1,128]{2,1,0:T(1,128)} all-to-all(f32[32,1,128]{2,1,0:T(1,128)} %bitcast.45), channel_id=1, replica_groups=mesh['pix'=16,'col'=2] {'pix','col'}, dimensions={0} | all-to-all | bytes 32768 | tf_op jit(solution)/shard_map/all_to_all | solution.py:49
  36.9 6.4 %collective-permute-done.3 = f32[256,256]{1,0:T(8,128)S(1)} collective-permute-done((f32[256,256]{1,0:T(8,128)S(1)}, f32[256,256]{1,0:T(8,128)S(1)}, u32[]{:S(2)}, u32[]{:S(2)}) %collective-permute-start.3) | collective-permute-done | bytes 262176 | tf_op jit(solution)/shard_map/ppermute | solution.py:43
  50.6 7.8 %all_to_all.56 = f32[32,1,128]{2,1,0:T(1,128)S(1)} all-to-all(f32[32,1,128]{2,1,0:T(1,128)} %bitcast.46), channel_id=1, replica_groups=mesh['pix'=16,'col'=2] {'pix','col'}, dimensions={0} | all-to-all | bytes 32768 | tf_op jit(solution)/shard_map/all_to_all | solution.py:49
  59.4 5.1 %shard_map.71 = (f32[256,256]{1,0:T(8,128)S(1)}, f32[256,256]{1,0:T(8,128)S(1)}, f32[512,1024]{1,0:T(8,128)}, f32[4,256,128]{2,1,0:T(8,128)S(1)}, f32[4,256,128]{2,1,0:T(8,128)S(1)}) custom-call(f32[32,128]{1,0:T(8,128)S(1)} %bitcast.38, f32[32,128]{1,0:T(8,128)S(1)} %bitcast.40, f32[256,256]{1,0:T(8,128)S(1)} %copy-done.4, ...), custom_call_target="tpu_custom_call" | custom-call | tf_op jit(solution)/shard_map/pallas_call | solution.py:105
  65.1 12.2 %collective-permute-done.6.refs_1_ = f32[4,256,128]{2,1,0:T(8,128)S(1)} collective-permute-done((f32[4,256,128]{2,1,0:T(8,128)S(1)}, f32[4,256,128]{2,1,0:T(8,128)S(1)}, u32[]{:S(2)}, u32[]{:S(2)}) %collective-permute-start.6) | collective-permute-done | bytes 524320 | tf_op jit(solution)/shard_map/ppermute | solution.py:25
  86.4 7.4 %collective-permute-done.9 = f32[256,128]{1,0:T(8,128)S(1)} collective-permute-done((f32[256,128]{1,0:T(8,128)S(1)}, f32[256,128]{1,0:T(8,128)S(1)}, u32[]{:S(2)}, u32[]{:S(2)}) %collective-permute-start.9) | collective-permute-done | bytes 131104 | tf_op jit(solution)/shard_map/ppermute | solution.py:25
  106.1 10.1 %collective-permute-done.14.refs_3_.refs_5_ = f32[4,256,128]{2,1,0:T(8,128)S(1)} collective-permute-done((f32[4,256,128]{2,1,0:T(8,128)S(1)}, f32[4,256,128]{2,1,0:T(8,128)S(1)}, u32[]{:S(2)}, u32[]{:S(2)}) %collective-permute-start.14) | collective-permute-done | bytes 524320 | tf_op jit(solution)/shard_map/ppermute | solution.py:25
  116.2 5.0 %shard_map.75 = (f32[512,1024]{1,0:T(8,128)}, f32[32,128]{1,0:T(8,128)}) custom-call(f32[256,256]{1,0:T(8,128)S(1)} %get-tuple-element.52.refs_0_.refs_2_, f32[256,256]{1,0:T(8,128)S(1)} %get-tuple-element.53.refs_1_.refs_3_, f32[4,256,128]{2,1,0:T(8,128)S(1)} %shard_map.74.refs_2_.refs_4_, f32[4,256,128]{2,1,0:T(8,128)S(1)} %collective-permute-done.14.refs_3_.refs_5_, ...), custom_call_target="tpu_custom_call" | custom-call | tf_op jit(solution)/shard_map/pallas_call | solution.py:105
  121.9 12.9 %all_to_all.57 = f32[32,1,128]{2,1,0:T(1,128)} all-to-all(f32[32,1,128]{2,1,0:T(1,128)} %bitcast.47), channel_id=1, replica_groups=mesh['pix'=16,'col'=2] {'pix','col'}, dimensions={0} | all-to-all | bytes 32768 | tf_op jit(solution)/shard_map/all_to_all | solution.py:49
  138.9 5.7 %shard_map.76 = (f32[512,1024]{1,0:T(8,128)}, f32[256,1024]{1,0:T(8,128)S(1)}, f32[256,256]{1,0:T(8,128)S(1)}, f32[256,256]{1,0:T(8,128)S(1)}) custom-call(f32[32,128]{1,0:T(8,128)S(1)} %bitcast.34, f32[512,1024]{1,0:T(8,128)} %get-tuple-element.60.refs_5_.refs_1_, f32[512,1024]{1,0:T(8,128)} %get-tuple-element.62.refs_2_, ...), custom_call_target="tpu_custom_call" | custom-call | tf_op jit(solution)/shard_map/pallas_call | solution.py:105
  147.4 6.6 %collective-permute-done.16 = f32[256,256]{1,0:T(8,128)S(1)} collective-permute-done((f32[256,256]{1,0:T(8,128)S(1)}, f32[256,256]{1,0:T(8,128)S(1)}, u32[]{:S(2)}, u32[]{:S(2)}) %collective-permute-start.16) | collective-permute-done | bytes 262176 | tf_op jit(solution)/shard_map/ppermute | solution.py:43
  160.9 7.8 %all_to_all.58 = f32[32,1,128]{2,1,0:T(1,128)S(1)} all-to-all(f32[32,1,128]{2,1,0:T(1,128)} %bitcast.48), channel_id=1, replica_groups=mesh['pix'=16,'col'=2] {'pix','col'}, dimensions={0} | all-to-all | bytes 32768 | tf_op jit(solution)/shard_map/all_to_all | solution.py:49
  169.7 5.6 %shard_map.79 = (f32[256,256]{1,0:T(8,128)}, f32[256,256]{1,0:T(8,128)S(1)}, f32[512,1024]{1,0:T(8,128)}, f32[4,256,128]{2,1,0:T(8,128)S(1)}, f32[4,256,128]{2,1,0:T(8,128)S(1)}) custom-call(f32[32,128]{1,0:T(8,128)S(1)} %bitcast.35, f32[32,128]{1,0:T(8,128)S(1)} %bitcast.39, f32[256,256]{1,0:T(8,128)S(1)} %get-tuple-element.52.refs_0_.refs_2_, ...), custom_call_target="tpu_custom_call" | custom-call | tf_op jit(solution)/shard_map/pallas_call | solution.py:105
  176.4 12.4 %collective-permute-done.19.refs_1_ = f32[4,256,128]{2,1,0:T(8,128)S(1)} collective-permute-done((f32[4,256,128]{2,1,0:T(8,128)S(1)}, f32[4,256,128]{2,1,0:T(8,128)S(1)}, u32[]{:S(2)}, u32[]{:S(2)}) %collective-permute-start.19) | collective-permute-done | bytes 524320 | tf_op jit(solution)/shard_map/ppermute | solution.py:25
  200.7 6.6 %collective-permute-done.22 = f32[256,128]{1,0:T(8,128)S(1)} collective-permute-done((f32[256,128]{1,0:T(8,128)S(1)}, f32[256,128]{1,0:T(8,128)S(1)}, u32[]{:S(2)}, u32[]{:S(2)}) %collective-permute-start.22) | collective-permute-done | bytes 131104 | tf_op jit(solution)/shard_map/ppermute | solution.py:25
  210.0 7.0 %collective-permute-done.25.refs_3_ = f32[256,128]{1,0:T(8,128)S(1)} collective-permute-done((f32[256,128]{1,0:T(8,128)S(1)}, f32[256,128]{1,0:T(8,128)S(1)}, u32[]{:S(2)}, u32[]{:S(2)}) %collective-permute-start.25) | collective-permute-done | bytes 131104 | tf_op jit(solution)/shard_map/ppermute | solution.py:25
  221.5 10.6 %collective-permute-done.27.refs_3_ = f32[4,256,128]{2,1,0:T(8,128)S(1)} collective-permute-done((f32[4,256,128]{2,1,0:T(8,128)S(1)}, f32[4,256,128]{2,1,0:T(8,128)S(1)}, u32[]{:S(2)}, u32[]{:S(2)}) %collective-permute-start.27) | collective-permute-done | bytes 524320 | tf_op jit(solution)/shard_map/ppermute | solution.py:25
  233.9 6.1 %collective-permute-start.30 = (f32[256,256]{1,0:T(8,128)S(1)}, f32[256,256]{1,0:T(8,128)S(1)}, u32[]{:S(2)}, u32[]{:S(2)}) collective-permute-start(f32[256,256]{1,0:T(8,128)S(1)} %copy-done.9), channel_id=1, source_target_pairs={{4,8},{6,10},{8,4},{10,6},{12,16},{14,18},{16,12},{18,14},{20,24},... | collective-permute-start | bytes 786440 | tf_op jit(solution)/shard_map/ppermute | solution.py:36
  240.1 5.9 %collective-permute-done.30.refs_15_.refs_8_ = f32[256,256]{1,0:T(8,128)S(1)} collective-permute-done((f32[256,256]{1,0:T(8,128)S(1)}, f32[256,256]{1,0:T(8,128)S(1)}, u32[]{:S(2)}, u32[]{:S(2)}) %collective-permute-start.30) | collective-permute-done | bytes 262176 | tf_op jit(solution)/shard_map/ppermute | solution.py:36
  247.4 5.0 %collective-permute-done.28.refs_13_.refs_6_ = f32[256,256]{1,0:T(8,128)S(1)} collective-permute-done((f32[256,256]{1,0:T(8,128)S(1)}, f32[256,256]{1,0:T(8,128)S(1)}, u32[]{:S(2)}, u32[]{:S(2)}) %collective-permute-start.28) | collective-permute-done | bytes 262176 | tf_op jit(solution)/shard_map/ppermute | solution.py:36
  252.9 5.1 %shard_map.83 = (f32[512,1024]{1,0:T(8,128)}, f32[32,128]{1,0:T(8,128)}) custom-call(f32[256,256]{1,0:T(8,128)S(1)} %copy-done.9, f32[256,256]{1,0:T(8,128)S(1)} %copy-done.11, f32[4,256,128]{2,1,0:T(8,128)S(1)} %shard_map.82.refs_2_, f32[4,256,128]{2,1,0:T(8,128)S(1)} %collective-permute-done.27.refs_3_, f32[512,1024]{1,0:T(8,128)} %get-tuple-element.49.refs_3_.refs_4_, ...), custom_call_target="tpu_custom_call" | custom-call | tf_op jit(solution)/shard_map/pallas_call | solution.py:105
  262.1 8.4 %shard_map.84 = (f32[4,256,1024]{2,1,0:T(8,128)}, f32[4,256,1024]{2,1,0:T(8,128)}) custom-call(s32[3]{0:T(128)S(1)} %pad_add_fusion.refs_0_, f32[256,1152]{1,0:T(8,128)} %copy-done.13, f32[256,1152]{1,0:T(8,128)} %copy-done.13, f32[256,1152]{1,0:T(8,128)} %copy-done.14, f32[256,1152]{1,0:T(8,128)} %copy-done.14, f32[256,1152]{1,0:T(8,128)} %copy-done.15, ...), custom_call_target="tpu_custom_call" | custom-call | tf_op jit(solution)/shard_map/pallas_call | solution.py:105
  270.6 17.1 %shard_map.85 = (f32[256,2048]{1,0:T(8,128)}, f32[256,1024]{1,0:T(8,128)S(1)}, f32[2,1024,256]{2,1,0:T(8,128)}) custom-call(s32[3]{0:T(128)S(1)} %pad_add_fusion.refs_0_, f32[32,128]{1,0:T(8,128)S(1)} %bitcast.41, f32[2,256,1024]{2,1,0:T(8,128)} %bitcast.43, f32[2,256,1024]{2,1,0:T(8,128)} %bitcast.44, f32[4,256,1024]{2,1,0:T(8,128)} %get-tuple-element.80.refs_4_, ...), custom_call_target="tpu_custom_call" | custom-call | tf_op jit(solution)/shard_map/pallas_call | solution.py:105
  (123 shorter events, 96.6 us)
Async XLA Ops:
  26.6 31.8 %collective-permute-start.5 = (f32[256,1152]{1,0:T(8,128)}, f32[256,1152]{1,0:T(8,128)S(1)}, u32[]{:S(2)}, u32[]{:S(2)}) collective-permute-start(f32[256,1152]{1,0:T(8,128)} %shard_map.70.refs_0_), channel_id=1, source_target_pairs={{4,8},{6,10},{8,4},{10,6},{12,16},{14,18},{16,12},{18,14},{20,24},... | collective-permute-start | bytes 3538952 | tf_op jit(solution)/shard_map/ppermute | solution.py:36
  35.8 7.6 %collective-permute-start.3 = (f32[256,256]{1,0:T(8,128)S(1)}, f32[256,256]{1,0:T(8,128)S(1)}, u32[]{:S(2)}, u32[]{:S(2)}) collective-permute-start(f32[256,256]{1,0:T(8,128)S(1)} %add.57), channel_id=1, source_target_pairs={{0,1},{1,0},{2,3},{3,2},{4,5},{5,4},{6,7},{7,6},{8,9},{9,8},{10,11... | collective-permute-start | bytes 786440 | tf_op jit(solution)/shard_map/ppermute | solution.py:43
  64.5 12.7 %collective-permute-start.6 = (f32[4,256,128]{2,1,0:T(8,128)S(1)}, f32[4,256,128]{2,1,0:T(8,128)S(1)}, u32[]{:S(2)}, u32[]{:S(2)}) collective-permute-start(f32[4,256,128]{2,1,0:T(8,128)S(1)} %get-tuple-element.55), channel_id=1, source_target_pairs={{0,4},{2,6},{4,0},{6,2},{8,12},{10,14},{12,8},{14,10},{16,20},{18,... | collective-permute-start | bytes 1572872 | tf_op jit(solution)/shard_map/ppermute | solution.py:25
  78.1 26.1 %collective-permute-start.13 = (f32[256,1152]{1,0:T(8,128)}, f32[256,1152]{1,0:T(8,128)S(1)}, u32[]{:S(2)}, u32[]{:S(2)}) collective-permute-start(f32[256,1152]{1,0:T(8,128)} %shard_map.73), channel_id=1, source_target_pairs={{0,4},{2,6},{4,0},{6,2},{8,12},{10,14},{12,8},{14,10},{16,20},{18,... | collective-permute-start | bytes 3538952 | tf_op jit(solution)/shard_map/ppermute | solution.py:36
  81.8 11.9 %collective-permute-start.9 = (f32[256,128]{1,0:T(8,128)S(1)}, f32[256,128]{1,0:T(8,128)S(1)}, u32[]{:S(2)}, u32[]{:S(2)}) collective-permute-start(f32[256,128]{1,0:T(8,128)S(1)} %get-tuple-element.59), channel_id=1, source_target_pairs={{0,24},{2,26},{4,28},{6,30},{8,16},{10,18},{12,20},{14,22},{16,8},... | collective-permute-start | bytes 393224 | tf_op jit(solution)/shard_map/ppermute | solution.py:25
  94.3 8.5 %collective-permute-start.11 = (f32[256,128]{1,0:T(8,128)S(1)}, f32[256,128]{1,0:T(8,128)S(1)}, u32[]{:S(2)}, u32[]{:S(2)}) collective-permute-start(f32[256,128]{1,0:T(8,128)S(1)} %add_add_fusion.1.refs_0_), channel_id=1, source_target_pairs={{0,16},{2,18},{4,20},{6,22},{8,24},{10,26},{12,28},{14,30},{16,0},... | collective-permute-start | bytes 393224 | tf_op jit(solution)/shard_map/ppermute | solution.py:25
  94.3 8.5 %collective-permute-start.10 = (f32[256,128]{1,0:T(8,128)S(1)}, f32[256,128]{1,0:T(8,128)S(1)}, u32[]{:S(2)}, u32[]{:S(2)}) collective-permute-start(f32[256,128]{1,0:T(8,128)S(1)} %add_add_fusion.1.refs_0_), channel_id=1, source_target_pairs={{0,8},{2,10},{4,12},{6,14},{8,0},{10,2},{12,4},{14,6},{16,24},{18,... | collective-permute-start | bytes 393224 | tf_op jit(solution)/shard_map/ppermute | solution.py:25
  105.2 11.0 %collective-permute-start.14 = (f32[4,256,128]{2,1,0:T(8,128)S(1)}, f32[4,256,128]{2,1,0:T(8,128)S(1)}, u32[]{:S(2)}, u32[]{:S(2)}) collective-permute-start(f32[4,256,128]{2,1,0:T(8,128)S(1)} %shard_map.74.refs_2_.refs_4_), channel_id=1, source_target_pairs={{0,4},{2,6},{4,0},{6,2},{8,12},{10,14},{12,8},{14,10},{16,20},{18,... | collective-permute-start | bytes 1572872 | tf_op jit(solution)/shard_map/ppermute | solution.py:25
  134.9 33.8 %collective-permute-start.18 = (f32[256,1152]{1,0:T(8,128)}, f32[256,1152]{1,0:T(8,128)S(1)}, u32[]{:S(2)}, u32[]{:S(2)}) collective-permute-start(f32[256,1152]{1,0:T(8,128)} %shard_map.78.refs_0_), channel_id=1, source_target_pairs={{4,10},{6,8},{8,6},{10,4},{12,18},{14,16},{16,14},{18,12},{20,26},... | collective-permute-start | bytes 3538952 | tf_op jit(solution)/shard_map/ppermute | solution.py:36
  146.2 7.8 %collective-permute-start.16 = (f32[256,256]{1,0:T(8,128)S(1)}, f32[256,256]{1,0:T(8,128)S(1)}, u32[]{:S(2)}, u32[]{:S(2)}) collective-permute-start(f32[256,256]{1,0:T(8,128)S(1)} %add.62), channel_id=1, source_target_pairs={{0,1},{1,0},{2,3},{3,2},{4,5},{5,4},{6,7},{7,6},{8,9},{9,8},{10,11... | collective-permute-start | bytes 786440 | tf_op jit(solution)/shard_map/ppermute | solution.py:43
  176.0 12.7 %collective-permute-start.19 = (f32[4,256,128]{2,1,0:T(8,128)S(1)}, f32[4,256,128]{2,1,0:T(8,128)S(1)}, u32[]{:S(2)}, u32[]{:S(2)}) collective-permute-start(f32[4,256,128]{2,1,0:T(8,128)S(1)} %get-tuple-element.72), channel_id=1, source_target_pairs={{0,4},{2,6},{4,0},{6,2},{8,12},{10,14},{12,8},{14,10},{16,20},{18,... | collective-permute-start | bytes 1572872 | tf_op jit(solution)/shard_map/ppermute | solution.py:25
  189.6 28.3 %collective-permute-start.26 = (f32[256,1152]{1,0:T(8,128)}, f32[256,1152]{1,0:T(8,128)S(1)}, u32[]{:S(2)}, u32[]{:S(2)}) collective-permute-start(f32[256,1152]{1,0:T(8,128)} %shard_map.81), channel_id=1, source_target_pairs={{0,6},{2,4},{4,2},{6,0},{8,14},{10,12},{12,10},{14,8},{16,22},{18,... | collective-permute-start | bytes 3538952 | tf_op jit(solution)/shard_map/ppermute | solution.py:36
  194.0 13.2 %collective-permute-start.22 = (f32[256,128]{1,0:T(8,128)S(1)}, f32[256,128]{1,0:T(8,128)S(1)}, u32[]{:S(2)}, u32[]{:S(2)}) collective-permute-start(f32[256,128]{1,0:T(8,128)S(1)} %get-tuple-element.76), channel_id=1, source_target_pairs={{0,24},{2,26},{4,28},{6,30},{8,16},{10,18},{12,20},{14,22},{16,8},... | collective-permute-start | bytes 393224 | tf_op jit(solution)/shard_map/ppermute | solution.py:25
  207.3 9.8 %collective-permute-start.25 = (f32[256,128]{1,0:T(8,128)S(1)}, f32[256,128]{1,0:T(8,128)S(1)}, u32[]{:S(2)}, u32[]{:S(2)}) collective-permute-start(f32[256,128]{1,0:T(8,128)S(1)} %add_add_fusion.refs_0_), channel_id=1, source_target_pairs={{0,24},{2,26},{4,28},{6,30},{8,16},{10,18},{12,20},{14,22},{16,8},... | collective-permute-start | bytes 393224 | tf_op jit(solution)/shard_map/ppermute | solution.py:25
  207.7 10.1 %collective-permute-start.24 = (f32[256,128]{1,0:T(8,128)S(1)}, f32[256,128]{1,0:T(8,128)S(1)}, u32[]{:S(2)}, u32[]{:S(2)}) collective-permute-start(f32[256,128]{1,0:T(8,128)S(1)} %add_add_fusion.refs_0_), channel_id=1, source_target_pairs={{0,16},{2,18},{4,20},{6,22},{8,24},{10,26},{12,28},{14,30},{16,0},... | collective-permute-start | bytes 393224 | tf_op jit(solution)/shard_map/ppermute | solution.py:25
  207.9 10.0 %collective-permute-start.23 = (f32[256,128]{1,0:T(8,128)S(1)}, f32[256,128]{1,0:T(8,128)S(1)}, u32[]{:S(2)}, u32[]{:S(2)}) collective-permute-start(f32[256,128]{1,0:T(8,128)S(1)} %add_add_fusion.refs_0_), channel_id=1, source_target_pairs={{0,8},{2,10},{4,12},{6,14},{8,0},{10,2},{12,4},{14,6},{16,24},{18,... | collective-permute-start | bytes 393224 | tf_op jit(solution)/shard_map/ppermute | solution.py:25
  218.9 13.3 %collective-permute-start.27 = (f32[4,256,128]{2,1,0:T(8,128)S(1)}, f32[4,256,128]{2,1,0:T(8,128)S(1)}, u32[]{:S(2)}, u32[]{:S(2)}) collective-permute-start(f32[4,256,128]{2,1,0:T(8,128)S(1)} %shard_map.82.refs_2_), channel_id=1, source_target_pairs={{0,4},{2,6},{4,0},{6,2},{8,12},{10,14},{12,8},{14,10},{16,20},{18,... | collective-permute-start | bytes 1572872 | tf_op jit(solution)/shard_map/ppermute | solution.py:25
  220.8 49.8 %collective-permute-start.32 = (f32[256,1024]{1,0:T(8,128)S(1)}, f32[256,1024]{1,0:T(8,128)}, u32[]{:S(2)}, u32[]{:S(2)}) collective-permute-start(f32[256,1024]{1,0:T(8,128)S(1)} %get-tuple-element.65.refs_2_.refs_17_.refs_10_), channel_id=1, source_target_pairs={{0,2},{2,0},{4,6},{6,4},{8,10},{10,8},{12,14},{14,12},{16,18},{18,... | collective-permute-start | bytes 3145736 | tf_op jit(solution)/shard_map/ppermute | solution.py:25
  232.3 38.3 %collective-permute-start.33 = (f32[8,256,128]{2,1,0:T(8,128)S(1)}, f32[8,256,128]{2,1,0:T(8,128)}, u32[]{:S(2)}, u32[]{:S(2)}) collective-permute-start(f32[8,256,128]{2,1,0:T(8,128)S(1)} %bitcast.30), channel_id=1, source_target_pairs={{0,2},{2,0},{4,6},{6,4},{8,10},{10,8},{12,14},{14,12},{16,18},{18,... | collective-permute-start | bytes 3145736 | tf_op jit(solution)/shard_map/ppermute | solution.py:25
  233.9 12.1 %collective-permute-start.30 = (f32[256,256]{1,0:T(8,128)S(1)}, f32[256,256]{1,0:T(8,128)S(1)}, u32[]{:S(2)}, u32[]{:S(2)}) collective-permute-start(f32[256,256]{1,0:T(8,128)S(1)} %copy-done.9), channel_id=1, source_target_pairs={{4,8},{6,10},{8,4},{10,6},{12,16},{14,18},{16,12},{18,14},{20,24},... | collective-permute-start | bytes 786440 | tf_op jit(solution)/shard_map/ppermute | solution.py:36
  240.0 12.4 %collective-permute-start.28 = (f32[256,256]{1,0:T(8,128)S(1)}, f32[256,256]{1,0:T(8,128)S(1)}, u32[]{:S(2)}, u32[]{:S(2)}) collective-permute-start(f32[256,256]{1,0:T(8,128)S(1)} %copy-done.9), channel_id=1, source_target_pairs={{0,4},{2,6},{4,0},{6,2},{8,12},{10,14},{12,8},{14,10},{16,20},{18,... | collective-permute-start | bytes 786440 | tf_op jit(solution)/shard_map/ppermute | solution.py:36
  246.0 15.3 %collective-permute-start.31 = (f32[256,256]{1,0:T(8,128)S(1)}, f32[256,256]{1,0:T(8,128)S(1)}, u32[]{:S(2)}, u32[]{:S(2)}) collective-permute-start(f32[256,256]{1,0:T(8,128)S(1)} %collective-permute-done.30.refs_15_.refs_8_), channel_id=1, source_target_pairs={{0,2},{2,0},{4,6},{6,4},{8,10},{10,8},{12,14},{14,12},{16,18},{18,... | collective-permute-start | bytes 786440 | tf_op jit(solution)/shard_map/ppermute | solution.py:25
  252.4 9.0 %collective-permute-start.29 = (f32[256,256]{1,0:T(8,128)S(1)}, f32[256,256]{1,0:T(8,128)S(1)}, u32[]{:S(2)}, u32[]{:S(2)}) collective-permute-start(f32[256,256]{1,0:T(8,128)S(1)} %collective-permute-done.28.refs_13_.refs_6_), channel_id=1, source_target_pairs={{0,2},{2,0},{4,6},{6,4},{8,10},{10,8},{12,14},{14,12},{16,18},{18,... | collective-permute-start | bytes 786440 | tf_op jit(solution)/shard_map/ppermute | solution.py:25
  257.9 12.6 %all-to-all-start.4 = ((f32[32,1,128]{2,1,0:T(1,128)}), f32[32,1,128]{2,1,0:T(1,128)S(1)}, u32[]{:S(2)}, u32[]{:S(2)}) async-start(f32[32,1,128]{2,1,0:T(1,128)} %bitcast.42), calls=%async_computation.4 | async-start | bytes 32768 | tf_op jit(solution)/shard_map/all_to_all | solution.py:49
  (31 other events, 114.1 us)

commit v4 on v0

v4 whole, which is shorter than its diff:
```python
import functools

import jax
import jax.numpy as jnp
from jax import lax
from jax.experimental import pallas as pl
from jax.experimental.pallas import tpu as pltpu
from jax.sharding import PartitionSpec as P

BANDS = 8
WIDTH = 256
ITERS = 2
PASSES = 2
LANES = 128
GROUP = 8

threshold_scale = 1.0
diffusion = 0.2
f32 = jnp.float32
bf16 = jnp.bfloat16


def along_pix(block, distance):
    count = lax.axis_size("pix")
    return lax.ppermute(block, "pix", [(i, i ^ distance) for i in range(count)])


def to_near(block, crossed):
    count = lax.axis_size("pix")
    return lax.ppermute(block, "pix", [(i, i ^ 2 ^ crossed) for i in range(count)])


def to_far(block):
    count = lax.axis_size("pix")
    route = [(i, i + (4 if i // 2 % 2 == 0 else -4)) for i in range(count)]
    return lax.ppermute(block, "pix", [(a, b) for a, b in route if 0 <= b < count])


def summed_over_col(block):
    count = lax.axis_size("col")
    step = 1
    while step < count:
        block = plus(block, lax.ppermute(block, "col", [(i, i ^ step) for i in range(count)]))
        step *= 2
    return block


def everywhere(sums):
    count = lax.axis_size("col")
    devices = lax.axis_size("pix") * count
    bits = [count << k for k in range(1, (devices // count).bit_length() - 1)]
    bits = [bits[0]] + [1 << k for k in range(count.bit_length() - 1)] + bits[1:]
    stages = [[count]] + [bits[k : k + 2] for k in range(0, len(bits), 2)]
    for stage in stages:
        moves = [0]
        for bit in stage:
            moves += [move ^ bit for move in moves]
        parts = [
            lax.ppermute(sums, ("pix", "col"), [(i, i ^ move) for i in range(devices)]) for move in moves[1:]
        ]
        sums = plus(sums, *parts)
    return sums


def halves(x):
    high = x.astype(bf16)
    return high, (x - high.astype(f32)).astype(bf16)


def left_parts(x, axis):
    high, low = halves(x)
    return jnp.concatenate([high, high, low], axis=axis)


def right_parts(x, axis):
    high, low = halves(x)
    return jnp.concatenate([high, low, high], axis=axis)


def product(a, b, summed=0):
    return lax.dot_general(a, b, (((1,), (summed,)), ((), ())), preferred_element_type=f32)


def rows_folded(x):
    return jnp.sum(x.reshape(x.shape[0] // 8, 8, x.shape[1]), axis=0)


def whole_sum(x):
    return jnp.sum(jnp.sum(x, axis=0, keepdims=True), axis=1, keepdims=True)


def packed_sums(shape, sums):
    lane = lax.broadcasted_iota(jnp.int32, shape, 1)
    row = lax.broadcasted_iota(jnp.int32, shape, 0)
    packed = jnp.zeros(shape, f32)
    for place, value in enumerate(sums):
        packed = packed + jnp.where((lane == place) & (row == 0), value, 0.0)
    return packed


def read_sums(ref, count):
    total = jnp.sum(ref[...], axis=0, keepdims=True)
    return [total[:, k : k + 1] for k in range(count)]


def spread_mask(mask, chip, step):
    dates = mask.shape[1]
    date = lax.broadcasted_iota(jnp.int32, (dates, 2 * LANES), 0)
    lane = lax.broadcasted_iota(jnp.int32, (dates, 2 * LANES), 1)
    chunk = chip ^ (2 * step + lane // LANES)
    pick = (date == chunk * (LANES // BANDS) + lane % LANES // BANDS).astype(bf16)
    return jnp.dot(mask.astype(f32).astype(bf16), pick, preferred_element_type=f32)


SMEM = pl.BlockSpec(memory_space=pltpu.SMEM)
VMEM = pl.BlockSpec(memory_space=pltpu.VMEM)
ANY = pl.BlockSpec(memory_space=pl.ANY)


def call(kernel, in_specs, out_specs, out_shape, scratch, *args, grid=(), place=None, after=(), beside=()):
    inputs = len(in_specs)
    lead = 0 if place is None else 1

    def body(*refs):
        used = lead + inputs
        kernel(*refs[:used], *refs[used + len(after) + len(beside) :])

    results = pl.pallas_call(
        body,
        grid_spec=pltpu.PrefetchScalarGridSpec(
            num_scalar_prefetch=lead,
            grid=grid,
            in_specs=list(in_specs) + [ANY] * len(after) + [VMEM] * len(beside),
            out_specs=list(out_specs),
            scratch_shapes=scratch,
        ),
        out_shape=list(out_shape),
        compiler_params=pltpu.CompilerParams(vmem_limit_bytes=16 * 2**20),
    )(*([place] if lead else []), *args, *after, *[in_vmem(x) for x in beside])
    return list(results)


def plus_kernel(*refs):
    total = refs[0][...]
    for ref in refs[1:-1]:
        total = total + ref[...]
    refs[-1][...] = total


def plus(*arrays):
    (total,) = call(plus_kernel, [VMEM] * len(arrays), [VMEM], [shaped(*arrays[0].shape)], [], *arrays)
    return total


def in_vmem(array):
    return pltpu.with_memory_space_constraint(array, pltpu.VMEM)


def in_hbm(array):
    return pltpu.with_memory_space_constraint(array, pltpu.HBM)


def held_until(array, *after):
    def body(*refs):
        pass

    return pl.pallas_call(
        body,
        in_specs=[ANY] * (1 + len(after)),
        out_specs=ANY,
        out_shape=jax.ShapeDtypeStruct(array.shape, array.dtype),
        input_output_aliases={0: 0},
        compiler_params=pltpu.CompilerParams(vmem_limit_bytes=2**20),
    )(array, *after)


def shaped(*shape):
    return jax.ShapeDtypeStruct(shape, f32)


def tiles(ref):
    return [slice(start, start + 2 * LANES) for start in range(0, ref.shape[-1], 2 * LANES)]


def pack_strip(obs_ref, mask_ref, out_refs):
    columns = obs_ref.shape[1]
    start = 0
    for ref in out_refs:
        rows = slice(start, start + ref.shape[0])
        ref[:, :columns] = obs_ref[rows]
        ref[:, columns:] = mask_ref[rows].astype(f32)
        start += ref.shape[0]


def pack_kernel(which, obs_ref, mask_ref, *out_refs):
    pack_strip(obs_ref, mask_ref, out_refs)


def split_factor(refs, parts_ref):
    pixels = refs[0].shape[0]
    for part, ref in enumerate(refs):
        parts_ref[part * pixels : (part + 1) * pixels] = left_parts(ref[...], 1)


def chunk_starts(chip, step):
    return [pl.multiple_of((chip ^ (2 * step + b)) * LANES, LANES) for b in range(2)]


def own_kernel(place, obs_ref, mask_ref, v_ref, u_ref, low_ref, high_ref, vt_ref, res_ref, weight_ref, sum_ref):
    pack_strip(obs_ref, mask_ref, (low_ref, high_ref))
    u = left_parts(u_ref[...], 1)
    spread = 0.0
    for step, cols in enumerate(tiles(vt_ref)):
        starts = chunk_starts(place[1], step)
        vt = jnp.concatenate([v_ref[pl.ds(start, LANES)].T for start in starts], axis=1)
        vt_ref[:, cols] = vt
        weight = spread_mask(mask_ref[...], place[1], step)
        obs = jnp.concatenate([obs_ref[:, pl.ds(start, LANES)] for start in starts], axis=1)
        res = weight * (obs - product(u, right_parts(vt, 0)))
        weight_ref[:, cols] = weight
        res_ref[:, cols] = res
        spread = spread + rows_folded(res * res)
    sum_ref[...] = spread


def residual_of_pieces(pieces, chip, step, low_rank):
    half = pieces[0].shape[1] // (BANDS + 1) * BANDS
    start = 0
    for piece in pieces:
        rows = slice(start, start + piece.shape[0])
        weight = spread_mask(piece[:, half:], chip, step)
        obs = jnp.concatenate([piece[:, pl.ds(first, LANES)] for first in chunk_starts(chip, step)], axis=1)
        yield rows, weight * (obs - low_rank[rows]), weight
        start += piece.shape[0]


def other_kernel(place, low_piece, high_piece, u_ref, vt_ref, own_res, own_weight, own_sum,
                 res_ref, weight_ref, sums_ref):
    pixels = own_res.shape[0]
    res_ref[:pixels] = own_res[...]
    weight_ref[:pixels] = own_weight[...]
    u = left_parts(u_ref[...], 1)
    spread = own_sum[...]
    for step, cols in enumerate(tiles(vt_ref)):
        low_rank = product(u, right_parts(vt_ref[:, cols], 0))
        for rows, res, weight in residual_of_pieces((low_piece, high_piece), place[1], step, low_rank):
            below = slice(pixels + rows.start, pixels + rows.stop)
            weight_ref[below, cols] = weight
            res_ref[below, cols] = res
            spread = spread + rows_folded(res * res)
    sums_ref[...] = packed_sums(sums_ref.shape, [whole_sum(spread)])


def level_from(spread, total):
    return threshold_scale * jnp.sqrt(jnp.maximum(spread, 0.0) / total + 1e-06)


def store_parts(grad, own_ref, other_ref):
    pixels = own_ref.shape[0]
    own_ref[...] = grad[:pixels]
    other_ref[...] = grad[pixels:]


def first_grad_kernel(total, sums_ref, res_ref, vt_ref, own_ref, other_ref):
    (spread,) = read_sums(sums_ref, 1)
    level = level_from(spread, total)
    grad = None
    for cols in tiles(res_ref):
        misfit = -jnp.clip(res_ref[:, cols], -level, level)
        part = product(left_parts(misfit, 1), right_parts(vt_ref[:, cols], 1), 1)
        grad = part if grad is None else grad + part
    store_parts(grad, own_ref, other_ref)


def column_sums(sums):
    top, curve, cross, before = sums
    step = top / curve
    return step, before + 2.0 * step * cross + step * step * curve


def next_grad_kernel(total, sums_ref, res_ref, shift_ref, vt_ref, even_ref, odd_ref,
                     res_out, vt_out, own_ref, other_ref):
    size, spread = column_sums(read_sums(sums_ref, 4))
    level = level_from(spread, total)
    grad = None
    for k, cols in enumerate(tiles(res_ref)):
        vt = vt_ref[:, cols] - size * jnp.concatenate([even_ref[k], odd_ref[k]], axis=1)
        vt_out[:, cols] = vt
        res = res_ref[:, cols] + size * shift_ref[:, cols]
        res_out[:, cols] = res
        misfit = -jnp.clip(res, -level, level)
        part = product(left_parts(misfit, 1), right_parts(vt, 1), 1)
        grad = part if grad is None else grad + part
    store_parts(grad, own_ref, other_ref)


def change_kernel(col_count, own_grad, other_grad, vt_ref, weight_ref, change_ref, sums_ref, g_parts):
    split_factor((own_grad, other_grad), g_parts)
    curve = 0.0
    for cols in tiles(vt_ref):
        change = weight_ref[:, cols] * product(g_parts[...], right_parts(vt_ref[:, cols], 0))
        change_ref[:, cols] = change
        curve = curve + rows_folded(change * change)
    top = whole_sum(own_grad[...] * own_grad[...]) / col_count
    sums_ref[...] = packed_sums(sums_ref.shape, [top, whole_sum(curve)])


def pix_step_kernel(total, first, level_sums, sums_ref, own_u, other_u, own_grad, other_grad, res_ref,
                    change_ref, own_out, other_out, res_out, even_ref, odd_ref, ut_parts):
    pixels = own_grad.shape[0]
    top, curve = read_sums(sums_ref, 2)
    size = top / curve
    if first:
        (spread,) = read_sums(level_sums, 1)
    else:
        _, spread = column_sums(read_sums(level_sums, 4))
    level = level_from(spread, total)
    strips = ((own_u, own_grad, own_out), (other_u, other_grad, other_out))
    for part, (old, grad, out) in enumerate(strips):
        u = old[...] - size * grad[...]
        out[...] = u
        high, low = halves(u.T)
        for k, value in enumerate((high, high, low)):
            first_col = (2 * k + part) * pixels
            ut_parts[:, first_col : first_col + pixels] = value
    for k, cols in enumerate(tiles(res_ref)):
        res = res_ref[:, cols]
        moved = size * change_ref[:, cols]
        res_out[:, cols] = res + moved
        misfit = -(jnp.clip(res, -level, level) + moved)
        grad = product(ut_parts[...], right_parts(misfit, 0))
        even_ref[k] = grad[:, :LANES]
        odd_ref[k] = grad[:, LANES:]


def shift_kernel(chips, own_u, other_u, even_ref, odd_ref, weight_ref, res_ref, shift_ref, sums_ref, u_parts):
    split_factor((own_u, other_u), u_parts)
    top = curve = cross = spread = 0.0
    for k, cols in enumerate(tiles(res_ref)):
        grad = jnp.concatenate([even_ref[k], odd_ref[k]], axis=1)
        top = top + rows_folded(grad * grad)
        shift = weight_ref[:, cols] * product(u_parts[...], right_parts(grad, 0))
        shift_ref[:, cols] = shift
        res = res_ref[:, cols]
        curve = curve + rows_folded(shift * shift)
        cross = cross + rows_folded(shift * res)
        spread = spread + rows_folded(res * res)
    sums = [whole_sum(top) / chips, whole_sum(curve), whole_sum(cross), whole_sum(spread)]
    sums_ref[...] = packed_sums(sums_ref.shape, sums)


def rim_kernel(place, *refs):
    packs = [refs[2 * k : 2 * k + 2] for k in range(4)]
    factors = refs[8:12]
    vt_ref, res_ref, weight_ref, u_parts = refs[12:]
    pixels = factors[0].shape[0]
    split_factor(factors, u_parts)
    for step, cols in enumerate(tiles(vt_ref)):
        low_rank = product(u_parts[...], right_parts(vt_ref[:, cols], 0))
        for part, pieces in enumerate(packs):
            strip = low_rank[part * pixels : (part + 1) * pixels]
            for rows, res, weight in residual_of_pieces(pieces, place[1], step, strip):
                weight_ref[part, rows, cols] = weight
                res_ref[part, rows, cols] = res


def add_kernel(kept_ref, from_ref, *refs):
    count = kept_ref.shape[0]
    held = (len(refs) - count) // 2
    for k, ref in enumerate(refs[held : held + count]):
        ref[...] = kept_ref[k] + from_ref[k]
    for source, target in zip(refs[:held], refs[held + count :]):
        target[...] = source[...]


def stack_kernel(*refs):
    for k, ref in enumerate(refs[:-1]):
        refs[-1][k] = ref[...]


def flux_of(diff, inverse):
    ratio = diff * inverse
    below = 1.0 + ratio * ratio
    guess = pl.reciprocal(below, approx=True)
    return diff * (guess * (2.0 - below * guess))


PAD = 8
SPAN = 64


def smooth_rows(source, target, inverse, keep_north, keep_south, north_edge, south_edge):
    count = source.shape[0]
    for start in range(0, WIDTH, SPAN):
        row = lax.broadcasted_iota(jnp.int32, (SPAN + 2 * PAD, LANES), 0) + (start - PAD)
        inside = (row >= 0) & (row < WIDTH - 1)
        around = slice(start, start + SPAN + 2 * PAD)
        middle = slice(PAD, PAD + SPAN)
        before = None
        here = source[0, around]
        for k in range(count - 1):
            after = source[k + 1, around]
            cross = flux_of(after[middle] - here[middle], inverse)
            if k == north_edge:
                cross = cross * keep_north
            if k == south_edge:
                cross = cross * keep_south
            if k > 0:
                east = flux_of(pltpu.roll(here, SPAN + 2 * PAD - 1, 0) - here, inverse)
                east = jnp.where(inside, east, 0.0)
                west = pltpu.roll(east, 1, 0)
                along = east[middle] - west[middle]
                target(k - 1, start, here[middle] + diffusion * ((cross - before) + along))
            before = cross
            here = after


def smooth_kernel(total, chips, place, sums_ref, res_ref, shift_ref, rim_ref, rim_weight, *refs):
    factors = refs[:4]
    own_vt, other_vt, own_even, own_odd, other_even, other_odd = refs[4:10]
    own_ref, other_ref, v_ref, u_parts, rim_shift, layer, once = refs[10:]
    step = pl.program_id(0)
    core, chip = place[0], place[2]
    pixels = own_ref.shape[0]

    @pl.when(step == 0)
    def _():
        split_factor(factors, u_parts)

    size, spread = column_sums(read_sums(sums_ref, 4))
    level = level_from(spread, total)
    inverse = 1.0 / level
    grad = jnp.concatenate([own_even[step], own_odd[step]], axis=1)
    moved = product(u_parts[...], right_parts(grad, 0))
    rim_shift[...] = moved.reshape(rim_shift.shape)

    def cut(res):
        return res - jnp.clip(res, -level, level)

    south = 2 * (chip % 2)
    beyond_own = jnp.where(core == 0, 2 - south, south)
    beyond_other = 2 - beyond_own
    keep_north = jnp.where(chip > 0, 1.0, 0.0).astype(f32)
    keep_south = jnp.where(chip < chips - 1, 1.0, 0.0).astype(f32)
    keep_own = jnp.where(core == 0, keep_north, keep_south)
    keep_other = jnp.where(core == 0, keep_south, keep_north)
    inner = slice(PAD, PAD + pixels)
    pair = ((own_even, other_even), (own_odd, other_odd))
    for b in range(2):
        cols = pl.ds(pl.multiple_of((2 * step + b) * LANES, LANES), LANES)
        here = slice(b * LANES, (b + 1) * LANES)
        there = pl.ds(pl.multiple_of((chip % 2 ^ b) * LANES, LANES), LANES)
        v_ref[core, there] = (own_vt[:, cols] - size * pair[b][0][step]).T
        v_ref[1 - core, there] = (other_vt[:, cols] - size * pair[b][1][step]).T
        for k in range(2):
            layer[2 + k, inner] = cut(res_ref[k, :, cols] + size * shift_ref[k, :, cols])
            for first, base in ((0, beyond_own), (4, beyond_other)):
                rim = base + k
                moved = size * (rim_weight[rim, :, cols] * rim_shift[rim, :, here])
                layer[first + k, inner] = cut(rim_ref[rim, :, cols] + moved)

        def to_once(strip, start, value):
            once[strip, PAD + start : PAD + start + SPAN] = value

        def to_cloud(strip, start, value):
            ref = other_ref if strip else own_ref
            ref[start : start + SPAN, there] = value

        smooth_rows(layer, to_once, inverse, keep_own, keep_other, 1, 3)
        smooth_rows(once, to_cloud, inverse, keep_own, keep_other, 0, 2)


def summed_over_chips(even, odd, held, beside):
    chips = lax.axis_size("pix") // 2
    count, rank, lanes = even.shape
    from_odd = along_pix(odd, 2)
    shapes = [shaped(rank, lanes)] + [pltpu.HBM((rank, lanes), f32)] * (count - 1)
    shapes += [pltpu.HBM(x.shape, f32) for x in held]
    kept = call(
        add_kernel, [VMEM] * (2 + len(held)), [VMEM] * len(shapes), shapes, [], even, from_odd, *held, beside=beside,
    )
    mine = plus(kept[0], *[along_pix(kept[k], 4 * k) for k in (1, 2, 3)])
    distance = GROUP
    while distance < chips:
        mine = plus(mine, along_pix(mine, 2 * distance))
        distance *= 2
    parts = [mine] + [along_pix(mine, 4 * k) for k in (1, 2, 3)]
    return parts, from_odd, kept[count:]


def per_device(observed, valid_mask, pix_factor, col_factor):
    pix_count = lax.axis_size("pix")
    col_count = lax.axis_size("col")
    chips = pix_count // 2
    pixels, columns = observed.shape
    rank = pix_factor.shape[1]
    half = columns // 2
    dates = valid_mask.shape[1] // 2
    total = float(pixels * columns * pix_count * col_count)
    assert pixels == WIDTH and half == GROUP * LANES and chips % GROUP == 0 and PASSES == 2
    index = lax.axis_index("pix")
    core = index % 2
    chip = index // 2
    place = jnp.stack([core, chip % GROUP, chip]).astype(jnp.int32)

    both = 2 * pixels
    wide = 2 * LANES
    steps = half // wide
    sums_shape = shaped(8, LANES)
    pix_shape = shaped(pixels, rank)
    grad_shape = shaped(steps, rank, LANES)
    vt_shape = pltpu.VMEM((rank, half), f32)
    local = pltpu.VMEM((both, half), f32)
    strip = pltpu.VMEM((pixels, half), f32)
    factor_scratch = [pltpu.VMEM((both, 3 * rank), bf16)]

    pieces = [pltpu.VMEM((pixels // 2, half + dates), f32)] * 2

    half_in = [pl.BlockSpec((pixels, half), lambda t, s: (0, s[0])), pl.BlockSpec((pixels, dates), lambda t, s: (0, s[0]))]
    other_pieces = call(
        pack_kernel, half_in, [VMEM] * 2, pieces, [], in_hbm(observed), in_hbm(valid_mask),
        grid=(1,), place=jnp.reshape(1 - core, (1,)).astype(jnp.int32),
    )
    received = [along_pix(piece, 1) for piece in other_pieces]
    own_u, other_u = pix_factor, along_pix(pix_factor, 1)
    *own_pieces, vt, own_res, own_weight, own_sum = call(
        own_kernel, half_in + [pl.BlockSpec((half, rank), lambda t, s: (s[0], 0)), VMEM], [VMEM] * 6,
        pieces + [vt_shape, strip, strip, shaped(8, wide)], [],
        in_hbm(observed), in_hbm(valid_mask), in_hbm(col_factor), own_u, grid=(1,), place=place,
    )
    residual, weight, sums = call(
        other_kernel, [SMEM] + [VMEM] * 7, [VMEM] * 3, [local, local, sums_shape], [],
        place, *received, other_u, in_vmem(vt), in_vmem(own_res), in_vmem(own_weight), own_sum,
    )
    level_sums = everywhere(sums)

    near_own, near_other, far_own, far_other = [None, None], [None, None], [None, None], [None, None]
    for iteration in range(ITERS):
        first = iteration == 0
        if first:
            near_own[0] = to_near(held_until(own_pieces[0], level_sums), 0)
            passed = [near_own[0]]
            own_part, other_part = call(
                functools.partial(first_grad_kernel, total), [VMEM] * 3, [VMEM] * 2, [pix_shape] * 2, [],
                level_sums, in_vmem(residual), in_vmem(vt),
            )
        else:
            near_other[1] = to_near(held_until(other_pieces[1], level_sums), 1)
            near_other[0] = held_until(near_other[0], level_sums)
            far_other[0] = to_far(near_other[0])
            passed = [near_other[1], far_other[0]]
            residual, vt, own_part, other_part = call(
                functools.partial(next_grad_kernel, total), [VMEM] * 6, [VMEM] * 4,
                [local, vt_shape, pix_shape, pix_shape], [],
                level_sums, in_vmem(residual), in_vmem(shift), in_vmem(vt), even, odd, after=far_own[1:],
            )
        own_grad = summed_over_col(plus(own_part, along_pix(other_part, 1)))
        other_grad = along_pix(own_grad, 1)
        change, sums = call(
            functools.partial(change_kernel, col_count), [VMEM] * 4, [VMEM] * 2,
            [local, sums_shape], factor_scratch, own_grad, other_grad, in_vmem(vt), in_vmem(weight),
            beside=[residual],
        )
        pix_sums = everywhere(sums)
        own_u, other_u, residual, even, odd = call(
            functools.partial(pix_step_kernel, total, first), [VMEM] * 8, [VMEM] * 5,
            [pix_shape, pix_shape, local, grad_shape, grad_shape], [pltpu.VMEM((rank, 3 * both), bf16)],
            level_sums, pix_sums, own_u, other_u, own_grad, other_grad, in_vmem(residual),
            in_vmem(change), after=passed, beside=[vt, weight],
        )
        alive = [residual, vt, weight, own_u, other_u]
        if first:
            near_own[0] = held_until(near_own[0], odd)
            far_own[0] = to_far(near_own[0])
            parts, moved, _ = summed_over_chips(even, odd, [], alive)
            near_own[1] = to_near(held_until(own_pieces[1], moved), 0)
            near_other[0] = to_near(held_until(other_pieces[0], moved), 1)
            passed = [far_own[0], near_own[1], near_other[0]]
        else:
            near_other[1] = held_until(near_other[1], odd)
            far_other[1] = to_far(near_other[1])
            parts, moved, sent = summed_over_chips(even, odd, [own_u], alive)
            near_u = to_near(sent[0], 0)
            other_vt = along_pix(vt, 1)
            passed = [far_other[1], near_u]
        (even,) = call(
            stack_kernel, [VMEM] * steps, [VMEM], [grad_shape], [], *parts, after=passed, beside=alive,
        )
        odd = along_pix(even, 2)
        if first:
            near_own[1] = held_until(near_own[1], even)
            far_own[1] = to_far(near_own[1])
        else:
            near_u = held_until(near_u, even)
            far_u = to_far(near_u)
        shift, sums = call(
            functools.partial(shift_kernel, chips), [VMEM] * 6, [VMEM] * 2,
            [local, sums_shape], factor_scratch, own_u, other_u, even, odd, in_vmem(weight),
            in_vmem(residual), beside=[vt],
        )
        level_sums = everywhere(sums)

    factors = [near_u, along_pix(near_u, 1), far_u, along_pix(far_u, 1)]
    rim_scratch = [pltpu.VMEM((2 * both, 3 * rank), bf16)]
    rim_shape = pltpu.VMEM((4, pixels, half), f32)
    rim_res, rim_weight = call(
        rim_kernel, [SMEM] + [VMEM] * 13, [VMEM] * 2, [rim_shape] * 2, rim_scratch,
        place, *near_own, *near_other, *far_own, *far_other, *factors, in_vmem(vt), after=[sums],
    )
    grads = [even, odd, along_pix(even, 1), along_pix(odd, 1)]
    pair = lambda s, t: s[1] // 2 ^ t
    own_cloud, other_cloud, v = call(
        functools.partial(smooth_kernel, total, chips), [VMEM] * 15,
        [
            pl.BlockSpec((pixels, wide), lambda t, s: (0, s[0] * steps + pair(s, t))),
            pl.BlockSpec((pixels, wide), lambda t, s: (0, pair(s, t))),
            pl.BlockSpec((2, wide, rank), lambda t, s: (0, pair(s, t), 0)),
        ],
        [shaped(pixels, columns), shaped(pixels, half), shaped(2, half, rank)],
        rim_scratch + [
            pltpu.VMEM((4, pixels, wide), f32),
            pltpu.VMEM((6, pixels + 2 * PAD, LANES), f32),
            pltpu.VMEM((4, pixels + 2 * PAD, LANES), f32),
        ],
        level_sums, in_vmem(residual.reshape(2, pixels, half)), in_vmem(shift.reshape(2, pixels, half)),
        in_vmem(rim_res), in_vmem(rim_weight), *factors, in_vmem(vt), other_vt, *grads, grid=(steps,), place=place,
    )
    from_other = along_pix(other_cloud, 1)
    cloud = lax.dynamic_update_slice(own_cloud, from_other, (0, (1 - core) * half))
    return own_u, v.reshape(columns, rank), cloud


def solution(mesh):
    in_specs = (P("pix", "col"), P("pix", "col"), P("pix", None), P("col", None))
    out_specs = (P("pix", None), P("col", None), P("pix", "col"))
    return jax.shard_map(
        per_device, mesh=mesh, in_specs=in_specs, out_specs=out_specs, check_vma=False
    )
```

time: 779 us -> 247 us (0.32)
  blocking collectives: 284 us -> 0 us
  waiting for transfers between devices: 345 us -> 96.7 us
  starting transfers between devices: 13.1 us -> 112 us
  matrix products: 56.5 us -> 0 us
  other arithmetic: 39.3 us -> 0.08 us
  Pallas kernels: 0 us -> 34.4 us
  between operations: 24.3 us -> 1.02 us
    psum x7 -> x0, blocking collectives: 284 us -> none  [the longest x3 121 us: level_of(): spread = lax.psum(jnp.sum(weight * residual * residual), ('pix', 'col'))]
    psum x4 -> x0, waiting for transfers between devices: 240 us -> none  [the longest x2 195 us: per_device(): col_grad = lax.psum(local_grad, 'pix')]
    ppermute x4 -> x76, starting transfers between devices: 13 us -> 112 us  [the longest x29 54.2 us: along_pix(): return lax.ppermute(block, 'pix', [(i, i ^ distance) for i in range(count)])]
    dot_general x9 -> x0, matrix products: 56.5 us -> none  [the longest x2 18.1 us: per_device(): lax.dot_general(misfit, pix_fac, (((0,), (0,)), ((), ())), precision=high...]
    pallas_call x0 -> x47, Pallas kernels: none -> 34.4 us  [the longest x38 34.4 us: call(): pl.pallas_call(body, grid_spec=pltpu.PrefetchScalarGridSpec(num_scalar_pr...]
    reduce_sum x6 -> x0, other arithmetic: 22.6 us -> none  [the longest x2 13.9 us: level_of(): spread = lax.psum(jnp.sum(weight * residual * residual), ('pix', 'col'))]
    ppermute x4 -> x76, waiting for transfers between devices: 105 us -> 96.7 us  [the longest x29 61.3 us: along_pix(): return lax.ppermute(block, 'pix', [(i, i ^ distance) for i in range(count)])]
  transfers between devices with their start and end apart: 8 -> 76, of which waited for: 7 -> 42; matrix products, arithmetic and copies ran while one was open for 1% -> 0% of each run, Pallas kernels for 0% -> 5%
where the time goes in v4:
time: 247 us; the launch traced here: 246 us
  starting transfers between devices  112 us (45%)
  waiting for transfers between devices  96.7 us (39%)
  Pallas kernels  34.4 us (14%)
    ppermute x29, waiting for transfers between devices, along_pix(): return lax.ppermute(block, 'pix', [(i, i ^ distance) for i in range(count)])  61.3 us
    ppermute x29, starting transfers between devices, along_pix(): return lax.ppermute(block, 'pix', [(i, i ^ distance) for i in range(count)])  54.2 us
    ppermute x35, starting transfers between devices, everywhere(): lax.ppermute(sums, ('pix', 'col'), [(i, i ^ move) for i in range(devices)])  35.3 us
    pallas_call x38, Pallas kernels, call(): pl.pallas_call(body, grid_spec=pltpu.PrefetchScalarGridSpec(num_scalar_pr...  34.4 us
    ppermute x35, waiting for transfers between devices, everywhere(): lax.ppermute(sums, ('pix', 'col'), [(i, i ^ move) for i in range(devices)])  21.2 us
    ppermute x2, waiting for transfers between devices, summed_over_col(): lax.ppermute(block, 'col', [(i, i ^ step) for i in range(count)])  14.2 us
    ppermute x5, starting transfers between devices, to_far(): lax.ppermute(block, 'pix', [(a, b) for a, b in route if 0 <= b < count])  12 us
    ppermute x5, starting transfers between devices, to_near(): lax.ppermute(block, 'pix', [(i, i ^ 2 ^ crossed) for i in range(count)])  9.46 us
  transfers between devices with their start and end apart: 76, of which 42 were waited for; matrix products, arithmetic and copies ran while one was open for 0% of the time, Pallas kernels for 5%

profile of v4, /device:TPU:13, one launch (start us, length us, event | category | flops | bytes accessed | tf_op | source)
XLA Modules:
  0.0 245.8 jit_solution(12042430513576601955)
XLA Ops:
  3.3 3.1 %shard_map.68 = (f32[128,1152]{1,0:T(8,128)S(1)}, f32[128,1152]{1,0:T(8,128)S(1)}, f32[256,1024]{1,0:T(8,128)S(1)}, f32[256,1024]{1,0:T(8,128)S(1)}, f32[256,1024]{1,0:T(8,128)S(1)}, /*index=5*/f32[8,256]{1,0:T(8,128)S(1)}) custom-call(s32[3]{0:T(128)S(1)} %pad_add_fusion.refs_0_, f32[256,2048]{1,0:T(8,128)} %refs_1_.3, s32[256,256]{1,0:T(8,128)} %refs_2_.4, ...), custom_call_target="tpu_custom_call" | custom-call | tf_op jit(solution)/shard_map/pallas_call | solution.py:128
  20.3 3.3 %collective-permute-start.10 = (f32[256,256]{1,0:T(8,128)S(1)}, f32[256,256]{1,0:T(8,128)S(1)}, u32[]{:S(2)}, u32[]{:S(2)}) collective-permute-start(f32[256,256]{1,0:T(8,128)S(1)} %get-tuple-element.61), channel_id=1, source_target_pairs={{0,2},{2,0},{4,6},{6,4},{8,10},{10,8},{12,14},{14,12},{16,18},{18,... | collective-permute-start | bytes 786440 | tf_op jit(solution)/shard_map/ppermute | solution.py:25
  25.0 7.3 %collective-permute-done.11.refs_1_ = f32[256,256]{1,0:T(8,128)S(1)} collective-permute-done((f32[256,256]{1,0:T(8,128)S(1)}, f32[256,256]{1,0:T(8,128)S(1)}, u32[]{:S(2)}, u32[]{:S(2)}) %collective-permute-start.11) | collective-permute-done | bytes 262176 | tf_op jit(solution)/shard_map/ppermute | solution.py:43
  41.4 2.4 collective-permute-start.19
  52.6 6.8 %collective-permute-done.21.refs_1_ = f32[4,256,128]{2,1,0:T(8,128)S(1)} collective-permute-done((f32[4,256,128]{2,1,0:T(8,128)S(1)}, f32[4,256,128]{2,1,0:T(8,128)S(1)}, u32[]{:S(2)}, u32[]{:S(2)}) %collective-permute-start.21) | collective-permute-done | bytes 524320 | tf_op jit(solution)/shard_map/ppermute | solution.py:25
  60.3 6.3 %collective-permute-start.30 = (f32[128,1152]{1,0:T(8,128)S(1)}, f32[128,1152]{1,0:T(8,128)S(1)}, u32[]{:S(2)}, u32[]{:S(2)}) collective-permute-start(f32[128,1152]{1,0:T(8,128)S(1)} %shard_map.86), channel_id=1, source_target_pairs={{0,6},{2,4},{4,2},{6,0},{8,14},{10,12},{12,10},{14,8},{16,22},{18,... | collective-permute-start | bytes 1769480 | tf_op jit(solution)/shard_map/ppermute | solution.py:30
  68.8 4.0 %collective-permute-done.22.refs_1_ = f32[256,128]{1,0:T(8,128)S(1)} collective-permute-done((f32[256,128]{1,0:T(8,128)}, f32[256,128]{1,0:T(8,128)S(1)}, u32[]{:S(2)}, u32[]{:S(2)}) %collective-permute-start.22) | collective-permute-done | bytes 131104 | tf_op jit(solution)/shard_map/ppermute | solution.py:25
  75.7 6.6 %collective-permute-done.24.refs_3_ = f32[256,128]{1,0:T(8,128)S(1)} collective-permute-done((f32[256,128]{1,0:T(8,128)}, f32[256,128]{1,0:T(8,128)S(1)}, u32[]{:S(2)}, u32[]{:S(2)}) %collective-permute-start.24) | collective-permute-done | bytes 131104 | tf_op jit(solution)/shard_map/ppermute | solution.py:25
  85.0 8.2 %collective-permute-done.27.refs_3_ = f32[256,128]{1,0:T(8,128)S(1)} collective-permute-done((f32[256,128]{1,0:T(8,128)S(1)}, f32[256,128]{1,0:T(8,128)S(1)}, u32[]{:S(2)}, u32[]{:S(2)}) %collective-permute-start.27) | collective-permute-done | bytes 131104 | tf_op jit(solution)/shard_map/ppermute | solution.py:25
  93.3 4.0 %collective-permute-start.39 = (f32[128,1152]{1,0:T(8,128)S(1)}, f32[128,1152]{1,0:T(8,128)S(1)}, u32[]{:S(2)}, u32[]{:S(2)}) collective-permute-start(f32[128,1152]{1,0:T(8,128)S(1)} %shard_map.92.refs_2_), channel_id=1, source_target_pairs={{0,8},{2,10},{8,16},{10,18},{12,4},{14,6},{16,24},{18,26},{20,12},... | collective-permute-start | bytes 1769480 | tf_op jit(solution)/shard_map/ppermute | solution.py:36
  97.3 2.7 %collective-permute-start.31 = (f32[4,256,128]{2,1,0:T(8,128)S(1)}, f32[4,256,128]{2,1,0:T(8,128)S(1)}, u32[]{:S(2)}, u32[]{:S(2)}) collective-permute-start(f32[4,256,128]{2,1,0:T(8,128)S(1)} %shard_map.87.refs_2_.refs_1_.refs_4_), channel_id=1, source_target_pairs={{0,4},{2,6},{4,0},{6,2},{8,12},{10,14},{12,8},{14,10},{16,20},{18,... | collective-permute-start | bytes 1572872 | tf_op jit(solution)/shard_map/ppermute | solution.py:25
  100.0 11.6 %collective-permute-done.31.refs_3_.refs_5_ = f32[4,256,128]{2,1,0:T(8,128)S(1)} collective-permute-done((f32[4,256,128]{2,1,0:T(8,128)S(1)}, f32[4,256,128]{2,1,0:T(8,128)S(1)}, u32[]{:S(2)}, u32[]{:S(2)}) %collective-permute-start.31) | collective-permute-done | bytes 524320 | tf_op jit(solution)/shard_map/ppermute | solution.py:25
  125.9 3.7 %collective-permute-start.40 = (f32[256,256]{1,0:T(8,128)S(1)}, f32[256,256]{1,0:T(8,128)S(1)}, u32[]{:S(2)}, u32[]{:S(2)}) collective-permute-start(f32[256,256]{1,0:T(8,128)S(1)} %get-tuple-element.79), channel_id=1, source_target_pairs={{0,2},{2,0},{4,6},{6,4},{8,10},{10,8},{12,14},{14,12},{16,18},{18,... | collective-permute-start | bytes 786440 | tf_op jit(solution)/shard_map/ppermute | solution.py:25
  132.8 6.9 %collective-permute-done.41.refs_1_ = f32[256,256]{1,0:T(8,128)S(1)} collective-permute-done((f32[256,256]{1,0:T(8,128)S(1)}, f32[256,256]{1,0:T(8,128)S(1)}, u32[]{:S(2)}, u32[]{:S(2)}) %collective-permute-start.41) | collective-permute-done | bytes 262176 | tf_op jit(solution)/shard_map/ppermute | solution.py:43
  159.8 6.7 %collective-permute-done.52.refs_1_ = f32[4,256,128]{2,1,0:T(8,128)S(1)} collective-permute-done((f32[4,256,128]{2,1,0:T(8,128)S(1)}, f32[4,256,128]{2,1,0:T(8,128)S(1)}, u32[]{:S(2)}, u32[]{:S(2)}) %collective-permute-start.52) | collective-permute-done | bytes 524320 | tf_op jit(solution)/shard_map/ppermute | solution.py:25
  175.0 6.5 %collective-permute-done.55.refs_3_ = f32[256,128]{1,0:T(8,128)S(1)} collective-permute-done((f32[256,128]{1,0:T(8,128)}, f32[256,128]{1,0:T(8,128)S(1)}, u32[]{:S(2)}, u32[]{:S(2)}) %collective-permute-start.55) | collective-permute-done | bytes 131104 | tf_op jit(solution)/shard_map/ppermute | solution.py:25
  181.7 2.5 %collective-permute-start.56 = (f32[256,128]{1,0:T(8,128)S(1)}, f32[256,128]{1,0:T(8,128)S(1)}, u32[]{:S(2)}, u32[]{:S(2)}) collective-permute-start(f32[256,128]{1,0:T(8,128)S(1)} %shard_map.104.refs_0_), channel_id=1, source_target_pairs={{0,8},{2,10},{4,12},{6,14},{8,0},{10,2},{12,4},{14,6},{16,24},{18,... | collective-permute-start | bytes 393224 | tf_op jit(solution)/shard_map/ppermute | solution.py:25
  184.2 10.1 %collective-permute-start.72 = (f32[256,1024]{1,0:T(8,128)S(1)}, f32[256,1024]{1,0:T(8,128)S(1)}, u32[]{:S(2)}, u32[]{:S(2)}) collective-permute-start(f32[256,1024]{1,0:T(8,128)S(1)} %get-tuple-element.80.refs_2_.refs_10_.refs_4_.refs_7_.refs_6_.refs_13_), channel_id=1, source_target_pairs={{0,2},{2,0},{4,6},{6,4},{8,10},{10,8},{12,14},{14,12},{16,18},{18,... | collective-permute-start | bytes 3145736 | tf_op jit(solution)/shard_map/ppermute | solution.py:25
  198.1 4.8 %collective-permute-start.73 = (f32[4,256,128]{2,1,0:T(8,128)S(1)}, f32[4,256,128]{2,1,0:T(8,128)S(1)}, u32[]{:S(2)}, u32[]{:S(2)}) collective-permute-start(f32[4,256,128]{2,1,0:T(8,128)S(1)} %shard_map.106.refs_2_.refs_1_.refs_12_), channel_id=1, source_target_pairs={{0,2},{2,0},{4,6},{6,4},{8,10},{10,8},{12,14},{14,12},{16,18},{18,... | collective-permute-start | bytes 1572872 | tf_op jit(solution)/shard_map/ppermute | solution.py:25
  204.1 5.0 %collective-permute-start.74 = (f32[4,256,128]{2,1,0:T(8,128)S(1)}, f32[4,256,128]{2,1,0:T(8,128)S(1)}, u32[]{:S(2)}, u32[]{:S(2)}) collective-permute-start(f32[4,256,128]{2,1,0:T(8,128)S(1)} %collective-permute-done.61.refs_3_.refs_13_), channel_id=1, source_target_pairs={{0,2},{2,0},{4,6},{6,4},{8,10},{10,8},{12,14},{14,12},{16,18},{18,... | collective-permute-start | bytes 1572872 | tf_op jit(solution)/shard_map/ppermute | solution.py:25
  221.4 2.2 collective-permute-start.67
  225.3 3.0 %shard_map.112 = (f32[4,256,1024]{2,1,0:T(8,128)S(1)}, f32[4,256,1024]{2,1,0:T(8,128)S(1)}) custom-call(s32[3]{0:T(128)S(1)} %pad_add_fusion.refs_0_, f32[128,1152]{1,0:T(8,128)S(1)} %shard_map.84.refs_1_, f32[128,1152]{1,0:T(8,128)S(1)} %shard_map.92.refs_2_, f32[128,1152]{1,0:T(8,128)S(1)} %shard_map.101.refs_3_, f32[128,1152]{1,0:T(8,128)S(1)} %shard_map.105.refs_4_, ...), custom_call_target="tpu_custom_call" | custom-call | tf_op jit(solution)/shard_map/pallas_call | solution.py:128
  228.4 12.5 %shard_map.113 = (f32[256,2048]{1,0:T(8,128)}, f32[256,1024]{1,0:T(8,128)S(1)}, f32[2,1024,256]{2,1,0:T(8,128)}) custom-call(s32[3]{0:T(128)S(1)} %pad_add_fusion.refs_0_, f32[8,128]{1,0:T(8,128)S(1)} %shard_map.110.refs_1_, f32[2,256,1024]{2,1,0:T(8,128)S(1)} %bitcast.7, f32[2,256,1024]{2,1,0:T(8,128)S(1)} %bitcast.8, ...), custom_call_target="tpu_custom_call" | custom-call | tf_op jit(solution)/shard_map/pallas_call | solution.py:128
  242.5 2.3 collective-permute-done.75
  (183 shorter events, 112.3 us)
Async XLA Ops:
  23.6 24.2 %collective-permute-start.20 = (f32[128,1152]{1,0:T(8,128)S(1)}, f32[128,1152]{1,0:T(8,128)S(1)}, u32[]{:S(2)}, u32[]{:S(2)}) collective-permute-start(f32[128,1152]{1,0:T(8,128)S(1)} %shard_map.80), channel_id=1, source_target_pairs={{0,4},{2,6},{4,0},{6,2},{8,12},{10,14},{12,8},{14,10},{16,20},{18,... | collective-permute-start | bytes 1769480 | tf_op jit(solution)/shard_map/ppermute | solution.py:30
  49.3 10.0 %collective-permute-start.21 = (f32[4,256,128]{2,1,0:T(8,128)S(1)}, f32[4,256,128]{2,1,0:T(8,128)S(1)}, u32[]{:S(2)}, u32[]{:S(2)}) collective-permute-start(f32[4,256,128]{2,1,0:T(8,128)S(1)} %get-tuple-element.69.refs_1_), channel_id=1, source_target_pairs={{0,4},{2,6},{4,0},{6,2},{8,12},{10,14},{12,8},{14,10},{16,20},{18,... | collective-permute-start | bytes 1572872 | tf_op jit(solution)/shard_map/ppermute | solution.py:25
  50.4 33.3 %collective-permute-start.28 = (f32[128,1152]{1,0:T(8,128)S(1)}, f32[128,1152]{1,0:T(8,128)S(1)}, u32[]{:S(2)}, u32[]{:S(2)}) collective-permute-start(f32[128,1152]{1,0:T(8,128)S(1)} %shard_map.84.refs_1_), channel_id=1, source_target_pairs={{0,8},{2,10},{8,16},{10,18},{12,4},{14,6},{16,24},{18,26},{20,12},... | collective-permute-start | bytes 1769480 | tf_op jit(solution)/shard_map/ppermute | solution.py:36
  59.3 33.9 %collective-permute-start.29 = (f32[128,1152]{1,0:T(8,128)S(1)}, f32[128,1152]{1,0:T(8,128)S(1)}, u32[]{:S(2)}, u32[]{:S(2)}) collective-permute-start(f32[128,1152]{1,0:T(8,128)S(1)} %shard_map.85), channel_id=1, source_target_pairs={{0,4},{2,6},{4,0},{6,2},{8,12},{10,14},{12,8},{14,10},{16,20},{18,... | collective-permute-start | bytes 1769480 | tf_op jit(solution)/shard_map/ppermute | solution.py:30
  60.3 33.0 %collective-permute-start.30 = (f32[128,1152]{1,0:T(8,128)S(1)}, f32[128,1152]{1,0:T(8,128)S(1)}, u32[]{:S(2)}, u32[]{:S(2)}) collective-permute-start(f32[128,1152]{1,0:T(8,128)S(1)} %shard_map.86), channel_id=1, source_target_pairs={{0,6},{2,4},{4,2},{6,0},{8,14},{10,12},{12,10},{14,8},{16,22},{18,... | collective-permute-start | bytes 1769480 | tf_op jit(solution)/shard_map/ppermute | solution.py:30
  82.3 10.9 %collective-permute-start.27 = (f32[256,128]{1,0:T(8,128)S(1)}, f32[256,128]{1,0:T(8,128)S(1)}, u32[]{:S(2)}, u32[]{:S(2)}) collective-permute-start(f32[256,128]{1,0:T(8,128)S(1)} %shard_map.83.refs_0_), channel_id=1, source_target_pairs={{0,24},{2,26},{4,28},{6,30},{8,16},{10,18},{12,20},{14,22},{16,8},... | collective-permute-start | bytes 393224 | tf_op jit(solution)/shard_map/ppermute | solution.py:25
  82.4 10.9 %collective-permute-start.26 = (f32[256,128]{1,0:T(8,128)S(1)}, f32[256,128]{1,0:T(8,128)S(1)}, u32[]{:S(2)}, u32[]{:S(2)}) collective-permute-start(f32[256,128]{1,0:T(8,128)S(1)} %shard_map.83.refs_0_), channel_id=1, source_target_pairs={{0,16},{2,18},{4,20},{6,22},{8,24},{10,26},{12,28},{14,30},{16,0},... | collective-permute-start | bytes 393224 | tf_op jit(solution)/shard_map/ppermute | solution.py:25
  83.7 9.6 %collective-permute-start.25 = (f32[256,128]{1,0:T(8,128)S(1)}, f32[256,128]{1,0:T(8,128)S(1)}, u32[]{:S(2)}, u32[]{:S(2)}) collective-permute-start(f32[256,128]{1,0:T(8,128)S(1)} %shard_map.83.refs_0_), channel_id=1, source_target_pairs={{0,8},{2,10},{4,12},{6,14},{8,0},{10,2},{12,4},{14,6},{16,24},{18,... | collective-permute-start | bytes 393224 | tf_op jit(solution)/shard_map/ppermute | solution.py:25
  93.3 30.9 %collective-permute-start.39 = (f32[128,1152]{1,0:T(8,128)S(1)}, f32[128,1152]{1,0:T(8,128)S(1)}, u32[]{:S(2)}, u32[]{:S(2)}) collective-permute-start(f32[128,1152]{1,0:T(8,128)S(1)} %shard_map.92.refs_2_), channel_id=1, source_target_pairs={{0,8},{2,10},{8,16},{10,18},{12,4},{14,6},{16,24},{18,26},{20,12},... | collective-permute-start | bytes 1769480 | tf_op jit(solution)/shard_map/ppermute | solution.py:36
  97.3 14.3 %collective-permute-start.31 = (f32[4,256,128]{2,1,0:T(8,128)S(1)}, f32[4,256,128]{2,1,0:T(8,128)S(1)}, u32[]{:S(2)}, u32[]{:S(2)}) collective-permute-start(f32[4,256,128]{2,1,0:T(8,128)S(1)} %shard_map.87.refs_2_.refs_1_.refs_4_), channel_id=1, source_target_pairs={{0,4},{2,6},{4,0},{6,2},{8,12},{10,14},{12,8},{14,10},{16,20},{18,... | collective-permute-start | bytes 1572872 | tf_op jit(solution)/shard_map/ppermute | solution.py:25
  129.5 25.0 %collective-permute-start.50 = (f32[128,1152]{1,0:T(8,128)S(1)}, f32[128,1152]{1,0:T(8,128)S(1)}, u32[]{:S(2)}, u32[]{:S(2)}) collective-permute-start(f32[128,1152]{1,0:T(8,128)S(1)} %shard_map.100), channel_id=1, source_target_pairs={{0,6},{2,4},{4,2},{6,0},{8,14},{10,12},{12,10},{14,8},{16,22},{18,... | collective-permute-start | bytes 1769480 | tf_op jit(solution)/shard_map/ppermute | solution.py:30
  130.3 24.2 %collective-permute-start.51 = (f32[128,1152]{1,0:T(8,128)S(1)}, f32[128,1152]{1,0:T(8,128)S(1)}, u32[]{:S(2)}, u32[]{:S(2)}) collective-permute-start(f32[128,1152]{1,0:T(8,128)S(1)} %shard_map.101.refs_3_), channel_id=1, source_target_pairs={{0,8},{2,10},{8,16},{10,18},{12,4},{14,6},{16,24},{18,26},{20,12},... | collective-permute-start | bytes 1769480 | tf_op jit(solution)/shard_map/ppermute | solution.py:36
  156.2 10.3 %collective-permute-start.52 = (f32[4,256,128]{2,1,0:T(8,128)S(1)}, f32[4,256,128]{2,1,0:T(8,128)S(1)}, u32[]{:S(2)}, u32[]{:S(2)}) collective-permute-start(f32[4,256,128]{2,1,0:T(8,128)S(1)} %get-tuple-element.87.refs_1_), channel_id=1, source_target_pairs={{0,4},{2,6},{4,0},{6,2},{8,12},{10,14},{12,8},{14,10},{16,20},{18,... | collective-permute-start | bytes 1572872 | tf_op jit(solution)/shard_map/ppermute | solution.py:25
  157.8 26.4 %collective-permute-start.59 = (f32[128,1152]{1,0:T(8,128)S(1)}, f32[128,1152]{1,0:T(8,128)S(1)}, u32[]{:S(2)}, u32[]{:S(2)}) collective-permute-start(f32[128,1152]{1,0:T(8,128)S(1)} %shard_map.105.refs_4_), channel_id=1, source_target_pairs={{0,8},{2,10},{8,16},{10,18},{12,4},{14,6},{16,24},{18,26},{20,12},... | collective-permute-start | bytes 1769480 | tf_op jit(solution)/shard_map/ppermute | solution.py:36
  170.6 10.8 %collective-permute-start.55 = (f32[256,128]{1,0:T(8,128)}, f32[256,128]{1,0:T(8,128)S(1)}, u32[]{:S(2)}, u32[]{:S(2)}) collective-permute-start(f32[256,128]{1,0:T(8,128)} %get-tuple-element.92), channel_id=1, source_target_pairs={{0,24},{2,26},{4,28},{6,30},{8,16},{10,18},{12,20},{14,22},{16,8},... | collective-permute-start | bytes 393224 | tf_op jit(solution)/shard_map/ppermute | solution.py:25
  170.9 23.4 %collective-permute-start.60 = (f32[256,256]{1,0:T(8,128)}, f32[256,256]{1,0:T(8,128)S(1)}, u32[]{:S(2)}, u32[]{:S(2)}) collective-permute-start(f32[256,256]{1,0:T(8,128)} %get-tuple-element.93), channel_id=1, source_target_pairs={{0,4},{2,6},{4,0},{6,2},{8,12},{10,14},{12,8},{14,10},{16,20},{18,... | collective-permute-start | bytes 786440 | tf_op jit(solution)/shard_map/ppermute | solution.py:30
  181.5 12.8 %collective-permute-start.58 = (f32[256,128]{1,0:T(8,128)S(1)}, f32[256,128]{1,0:T(8,128)S(1)}, u32[]{:S(2)}, u32[]{:S(2)}) collective-permute-start(f32[256,128]{1,0:T(8,128)S(1)} %shard_map.104.refs_0_), channel_id=1, source_target_pairs={{0,24},{2,26},{4,28},{6,30},{8,16},{10,18},{12,20},{14,22},{16,8},... | collective-permute-start | bytes 393224 | tf_op jit(solution)/shard_map/ppermute | solution.py:25
  181.6 12.7 %collective-permute-start.57 = (f32[256,128]{1,0:T(8,128)S(1)}, f32[256,128]{1,0:T(8,128)S(1)}, u32[]{:S(2)}, u32[]{:S(2)}) collective-permute-start(f32[256,128]{1,0:T(8,128)S(1)} %shard_map.104.refs_0_), channel_id=1, source_target_pairs={{0,16},{2,18},{4,20},{6,22},{8,24},{10,26},{12,28},{14,30},{16,0},... | collective-permute-start | bytes 393224 | tf_op jit(solution)/shard_map/ppermute | solution.py:25
  181.7 12.7 %collective-permute-start.56 = (f32[256,128]{1,0:T(8,128)S(1)}, f32[256,128]{1,0:T(8,128)S(1)}, u32[]{:S(2)}, u32[]{:S(2)}) collective-permute-start(f32[256,128]{1,0:T(8,128)S(1)} %shard_map.104.refs_0_), channel_id=1, source_target_pairs={{0,8},{2,10},{4,12},{6,14},{8,0},{10,2},{12,4},{14,6},{16,24},{18,... | collective-permute-start | bytes 393224 | tf_op jit(solution)/shard_map/ppermute | solution.py:25
  184.2 44.2 %collective-permute-start.72 = (f32[256,1024]{1,0:T(8,128)S(1)}, f32[256,1024]{1,0:T(8,128)S(1)}, u32[]{:S(2)}, u32[]{:S(2)}) collective-permute-start(f32[256,1024]{1,0:T(8,128)S(1)} %get-tuple-element.80.refs_2_.refs_10_.refs_4_.refs_7_.refs_6_.refs_13_), channel_id=1, source_target_pairs={{0,2},{2,0},{4,6},{6,4},{8,10},{10,8},{12,14},{14,12},{16,18},{18,... | collective-permute-start | bytes 3145736 | tf_op jit(solution)/shard_map/ppermute | solution.py:25
  194.4 9.7 %collective-permute-start.61 = (f32[4,256,128]{2,1,0:T(8,128)S(1)}, f32[4,256,128]{2,1,0:T(8,128)S(1)}, u32[]{:S(2)}, u32[]{:S(2)}) collective-permute-start(f32[4,256,128]{2,1,0:T(8,128)S(1)} %shard_map.106.refs_2_.refs_1_.refs_12_), channel_id=1, source_target_pairs={{0,4},{2,6},{4,0},{6,2},{8,12},{10,14},{12,8},{14,10},{16,20},{18,... | collective-permute-start | bytes 1572872 | tf_op jit(solution)/shard_map/ppermute | solution.py:25
  196.2 16.7 %collective-permute-start.70 = (f32[256,256]{1,0:T(8,128)S(1)}, f32[256,256]{1,0:T(8,128)S(1)}, u32[]{:S(2)}, u32[]{:S(2)}) collective-permute-start(f32[256,256]{1,0:T(8,128)S(1)} %shard_map.111.refs_9_.refs_6_), channel_id=1, source_target_pairs={{0,8},{2,10},{8,16},{10,18},{12,4},{14,6},{16,24},{18,26},{20,12},... | collective-permute-start | bytes 786440 | tf_op jit(solution)/shard_map/ppermute | solution.py:36
  198.1 30.3 %collective-permute-start.73 = (f32[4,256,128]{2,1,0:T(8,128)S(1)}, f32[4,256,128]{2,1,0:T(8,128)S(1)}, u32[]{:S(2)}, u32[]{:S(2)}) collective-permute-start(f32[4,256,128]{2,1,0:T(8,128)S(1)} %shard_map.106.refs_2_.refs_1_.refs_12_), channel_id=1, source_target_pairs={{0,2},{2,0},{4,6},{6,4},{8,10},{10,8},{12,14},{14,12},{16,18},{18,... | collective-permute-start | bytes 1572872 | tf_op jit(solution)/shard_map/ppermute | solution.py:25
  204.1 24.3 %collective-permute-start.74 = (f32[4,256,128]{2,1,0:T(8,128)S(1)}, f32[4,256,128]{2,1,0:T(8,128)S(1)}, u32[]{:S(2)}, u32[]{:S(2)}) collective-permute-start(f32[4,256,128]{2,1,0:T(8,128)S(1)} %collective-permute-done.61.refs_3_.refs_13_), channel_id=1, source_target_pairs={{0,2},{2,0},{4,6},{6,4},{8,10},{10,8},{12,14},{14,12},{16,18},{18,... | collective-permute-start | bytes 1572872 | tf_op jit(solution)/shard_map/ppermute | solution.py:25
  (55 other events, 221.7 us)

commit v5 on v4

--- a/solution.py
+++ b/solution.py
@@ -45,12 +45,14 @@
     return block
 
 
-def everywhere(sums):
+def everywhere(sums, late=False):
     count = lax.axis_size("col")
     devices = lax.axis_size("pix") * count
     bits = [count << k for k in range(1, (devices // count).bit_length() - 1)]
     bits = [bits[0]] + [1 << k for k in range(count.bit_length() - 1)] + bits[1:]
     stages = [[count]] + [bits[k : k + 2] for k in range(0, len(bits), 2)]
+    if late:
+        stages = stages[:1] + stages[:0:-1]
     for stage in stages:
         moves = [0]
         for bit in stage:
@@ -206,8 +208,9 @@
     return [pl.multiple_of((chip ^ (2 * step + b)) * LANES, LANES) for b in range(2)]
 
 
-def own_kernel(place, obs_ref, mask_ref, v_ref, u_ref, low_ref, high_ref, vt_ref, res_ref, weight_ref, sum_ref):
-    pack_strip(obs_ref, mask_ref, (low_ref, high_ref))
+def own_kernel(place, obs_ref, mask_ref, v_ref, u_ref, *refs):
+    vt_ref, res_ref, weight_ref, sum_ref = refs[-4:]
+    pack_strip(obs_ref, mask_ref, refs[:-4])
     u = left_parts(u_ref[...], 1)
     spread = 0.0
     for step, cols in enumerate(tiles(vt_ref)):
@@ -234,8 +237,9 @@
         start += piece.shape[0]
 
 
-def other_kernel(place, low_piece, high_piece, u_ref, vt_ref, own_res, own_weight, own_sum,
-                 res_ref, weight_ref, sums_ref):
+def other_kernel(place, *refs):
+    pieces = refs[:-8]
+    u_ref, vt_ref, own_res, own_weight, own_sum, res_ref, weight_ref, sums_ref = refs[-8:]
     pixels = own_res.shape[0]
     res_ref[:pixels] = own_res[...]
     weight_ref[:pixels] = own_weight[...]
@@ -243,7 +247,7 @@
     spread = own_sum[...]
     for step, cols in enumerate(tiles(vt_ref)):
         low_rank = product(u, right_parts(vt_ref[:, cols], 0))
-        for rows, res, weight in residual_of_pieces((low_piece, high_piece), place[1], step, low_rank):
+        for rows, res, weight in residual_of_pieces(pieces, place[1], step, low_rank):
             below = slice(pixels + rows.start, pixels + rows.stop)
             weight_ref[below, cols] = weight
             res_ref[below, cols] = res
@@ -350,9 +354,9 @@
 
 
 def rim_kernel(place, *refs):
-    packs = [refs[2 * k : 2 * k + 2] for k in range(4)]
-    factors = refs[8:12]
-    vt_ref, res_ref, weight_ref, u_parts = refs[12:]
+    packs = [refs[3 * k : 3 * k + 3] for k in range(4)]
+    factors = refs[12:16]
+    vt_ref, res_ref, weight_ref, u_parts = refs[16:]
     pixels = factors[0].shape[0]
     split_factor(factors, u_parts)
     for step, cols in enumerate(tiles(vt_ref)):
@@ -378,9 +382,8 @@
         refs[-1][k] = ref[...]
 
 
-def flux_of(diff, inverse):
-    ratio = diff * inverse
-    below = 1.0 + ratio * ratio
+def flux_of(diff):
+    below = 1.0 + diff * diff
     guess = pl.reciprocal(below, approx=True)
     return diff * (guess * (2.0 - below * guess))
 
@@ -389,7 +392,7 @@
 SPAN = 64
 
 
-def smooth_rows(source, target, inverse, keep_north, keep_south, north_edge, south_edge):
+def smooth_rows(source, target, keep_north, keep_south, north_edge, south_edge):
     count = source.shape[0]
     for start in range(0, WIDTH, SPAN):
         row = lax.broadcasted_iota(jnp.int32, (SPAN + 2 * PAD, LANES), 0) + (start - PAD)
@@ -400,13 +403,13 @@
         here = source[0, around]
         for k in range(count - 1):
             after = source[k + 1, around]
-            cross = flux_of(after[middle] - here[middle], inverse)
+            cross = flux_of(after[middle] - here[middle])
             if k == north_edge:
                 cross = cross * keep_north
             if k == south_edge:
                 cross = cross * keep_south
             if k > 0:
-                east = flux_of(pltpu.roll(here, SPAN + 2 * PAD - 1, 0) - here, inverse)
+                east = flux_of(pltpu.roll(here, SPAN + 2 * PAD - 1, 0) - here)
                 east = jnp.where(inside, east, 0.0)
                 west = pltpu.roll(east, 1, 0)
                 along = east[middle] - west[middle]
@@ -435,7 +438,7 @@
     rim_shift[...] = moved.reshape(rim_shift.shape)
 
     def cut(res):
-        return res - jnp.clip(res, -level, level)
+        return (res - jnp.clip(res, -level, level)) * inverse
 
     south = 2 * (chip % 2)
     beyond_own = jnp.where(core == 0, 2 - south, south)
@@ -464,18 +467,17 @@
 
         def to_cloud(strip, start, value):
             ref = other_ref if strip else own_ref
-            ref[start : start + SPAN, there] = value
-
-        smooth_rows(layer, to_once, inverse, keep_own, keep_other, 1, 3)
-        smooth_rows(once, to_cloud, inverse, keep_own, keep_other, 0, 2)
+            ref[start : start + SPAN, there] = level * value
+
+        smooth_rows(layer, to_once, keep_own, keep_other, 1, 3)
+        smooth_rows(once, to_cloud, keep_own, keep_other, 0, 2)
 
 
 def summed_over_chips(even, odd, held, beside):
     chips = lax.axis_size("pix") // 2
     count, rank, lanes = even.shape
     from_odd = along_pix(odd, 2)
-    shapes = [shaped(rank, lanes)] + [pltpu.HBM((rank, lanes), f32)] * (count - 1)
-    shapes += [pltpu.HBM(x.shape, f32) for x in held]
+    shapes = [shaped(rank, lanes)] * count + [shaped(*x.shape) for x in held]
     kept = call(
         add_kernel, [VMEM] * (2 + len(held)), [VMEM] * len(shapes), shapes, [], even, from_odd, *held, beside=beside,
     )
@@ -514,45 +516,52 @@
     strip = pltpu.VMEM((pixels, half), f32)
     factor_scratch = [pltpu.VMEM((both, 3 * rank), bf16)]
 
-    pieces = [pltpu.VMEM((pixels // 2, half + dates), f32)] * 2
+    unit = pixels // 32
+    own_rows, other_rows = [13 * unit, 13 * unit, 6 * unit], [7 * unit, 12 * unit, 13 * unit]
+
+    def pieces(rows):
+        return [pltpu.VMEM((n, half + dates), f32) for n in rows]
 
     half_in = [pl.BlockSpec((pixels, half), lambda t, s: (0, s[0])), pl.BlockSpec((pixels, dates), lambda t, s: (0, s[0]))]
     other_pieces = call(
-        pack_kernel, half_in, [VMEM] * 2, pieces, [], in_hbm(observed), in_hbm(valid_mask),
+        pack_kernel, half_in, [VMEM] * 3, pieces(other_rows), [], in_hbm(observed), in_hbm(valid_mask),
         grid=(1,), place=jnp.reshape(1 - core, (1,)).astype(jnp.int32),
     )
     received = [along_pix(piece, 1) for piece in other_pieces]
     own_u, other_u = pix_factor, along_pix(pix_factor, 1)
     *own_pieces, vt, own_res, own_weight, own_sum = call(
-        own_kernel, half_in + [pl.BlockSpec((half, rank), lambda t, s: (s[0], 0)), VMEM], [VMEM] * 6,
-        pieces + [vt_shape, strip, strip, shaped(8, wide)], [],
+        own_kernel, half_in + [pl.BlockSpec((half, rank), lambda t, s: (s[0], 0)), VMEM], [VMEM] * 7,
+        pieces(own_rows) + [vt_shape, strip, strip, shaped(8, wide)], [],
         in_hbm(observed), in_hbm(valid_mask), in_hbm(col_factor), own_u, grid=(1,), place=place,
     )
+    near_own, near_other, far_own, far_other = [None] * 3, [None] * 3, [None] * 3, [None] * 3
+    near_own[0] = to_near(own_pieces[0], 0)
     residual, weight, sums = call(
-        other_kernel, [SMEM] + [VMEM] * 7, [VMEM] * 3, [local, local, sums_shape], [],
+        other_kernel, [SMEM] + [VMEM] * 8, [VMEM] * 3, [local, local, sums_shape], [],
         place, *received, other_u, in_vmem(vt), in_vmem(own_res), in_vmem(own_weight), own_sum,
     )
-    level_sums = everywhere(sums)
-
-    near_own, near_other, far_own, far_other = [None, None], [None, None], [None, None], [None, None]
+    level_sums = everywhere(sums, late=True)
+
     for iteration in range(ITERS):
         first = iteration == 0
         if first:
-            near_own[0] = to_near(held_until(own_pieces[0], level_sums), 0)
-            passed = [near_own[0]]
+            near_own[1] = to_near(held_until(own_pieces[1], level_sums), 0)
+            near_own[0] = held_until(near_own[0], level_sums)
+            far_own[0] = to_far(near_own[0])
+            passed = [near_own[1], far_own[0]]
             own_part, other_part = call(
                 functools.partial(first_grad_kernel, total), [VMEM] * 3, [VMEM] * 2, [pix_shape] * 2, [],
-                level_sums, in_vmem(residual), in_vmem(vt),
+                level_sums, in_vmem(residual), in_vmem(vt), after=near_own[:1],
             )
         else:
-            near_other[1] = to_near(held_until(other_pieces[1], level_sums), 1)
-            near_other[0] = held_until(near_other[0], level_sums)
-            far_other[0] = to_far(near_other[0])
-            passed = [near_other[1], far_other[0]]
+            near_other[2] = to_near(held_until(other_pieces[2], level_sums), 1)
+            near_other[1] = held_until(near_other[1], level_sums)
+            far_other[1] = to_far(near_other[1])
+            passed = [near_other[2], far_other[1]]
             residual, vt, own_part, other_part = call(
                 functools.partial(next_grad_kernel, total), [VMEM] * 6, [VMEM] * 4,
                 [local, vt_shape, pix_shape, pix_shape], [],
-                level_sums, in_vmem(residual), in_vmem(shift), in_vmem(vt), even, odd, after=far_own[1:],
+                level_sums, in_vmem(residual), in_vmem(shift), in_vmem(vt), even, odd, after=[far_own[2], far_other[0]],
             )
         own_grad = summed_over_col(plus(own_part, along_pix(other_part, 1)))
         other_grad = along_pix(own_grad, 1)
@@ -570,26 +579,29 @@
         )
         alive = [residual, vt, weight, own_u, other_u]
         if first:
-            near_own[0] = held_until(near_own[0], odd)
-            far_own[0] = to_far(near_own[0])
+            near_own[1] = held_until(near_own[1], odd)
+            far_own[1] = to_far(near_own[1])
             parts, moved, _ = summed_over_chips(even, odd, [], alive)
-            near_own[1] = to_near(held_until(own_pieces[1], moved), 0)
+            near_own[2] = to_near(held_until(own_pieces[2], moved), 0)
             near_other[0] = to_near(held_until(other_pieces[0], moved), 1)
-            passed = [far_own[0], near_own[1], near_other[0]]
+            near_other[1] = to_near(held_until(other_pieces[1], moved), 1)
+            passed = [far_own[1], near_own[2], near_other[0], near_other[1]]
         else:
-            near_other[1] = held_until(near_other[1], odd)
-            far_other[1] = to_far(near_other[1])
+            near_other[2] = held_until(near_other[2], odd)
+            far_other[2] = to_far(near_other[2])
             parts, moved, sent = summed_over_chips(even, odd, [own_u], alive)
             near_u = to_near(sent[0], 0)
             other_vt = along_pix(vt, 1)
-            passed = [far_other[1], near_u]
+            passed = [far_other[2], near_u]
         (even,) = call(
             stack_kernel, [VMEM] * steps, [VMEM], [grad_shape], [], *parts, after=passed, beside=alive,
         )
         odd = along_pix(even, 2)
         if first:
-            near_own[1] = held_until(near_own[1], even)
-            far_own[1] = to_far(near_own[1])
+            near_own[2] = held_until(near_own[2], even)
+            near_other[0] = held_until(near_other[0], even)
+            far_own[2] = to_far(near_own[2])
+            far_other[0] = to_far(near_other[0])
         else:
             near_u = held_until(near_u, even)
             far_u = to_far(near_u)
@@ -604,7 +616,7 @@
     rim_scratch = [pltpu.VMEM((2 * both, 3 * rank), bf16)]
     rim_shape = pltpu.VMEM((4, pixels, half), f32)
     rim_res, rim_weight = call(
-        rim_kernel, [SMEM] + [VMEM] * 13, [VMEM] * 2, [rim_shape] * 2, rim_scratch,
+        rim_kernel, [SMEM] + [VMEM] * 17, [VMEM] * 2, [rim_shape] * 2, rim_scratch,
         place, *near_own, *near_other, *far_own, *far_other, *factors, in_vmem(vt), after=[sums],
     )
     grads = [even, odd, along_pix(even, 1), along_pix(odd, 1)]

time: 247 us -> 239 us (0.968)
  waiting for transfers between devices: 96.7 us -> 77.1 us
  starting transfers between devices: 112 us -> 124 us
    ppermute x29 -> x30, waiting for transfers between devices: 61.3 us -> 47.1 us  [along_pix(): return lax.ppermute(block, 'pix', [(i, i ^ distance) for i in range(count)])]
    ppermute x5 -> x7, starting transfers between devices: 12 us -> 21.6 us  [to_far(): lax.ppermute(block, 'pix', [(a, b) for a, b in route if 0 <= b < count])]
    ppermute x2, waiting for transfers between devices: 14.2 us -> 6 us  [summed_over_col(): lax.ppermute(block, 'col', [(i, i ^ step) for i in range(count)])]
    ppermute x5 -> x7, waiting for transfers between devices: 0.01 us -> 3.43 us  [to_near(): lax.ppermute(block, 'pix', [(i, i ^ 2 ^ crossed) for i in range(count)])]
    ppermute x5 -> x7, starting transfers between devices: 9.46 us -> 11.3 us  [to_near(): lax.ppermute(block, 'pix', [(i, i ^ 2 ^ crossed) for i in range(count)])]
    ppermute x29 -> x30, starting transfers between devices: 54.2 us -> 53.5 us  [along_pix(): return lax.ppermute(block, 'pix', [(i, i ^ distance) for i in range(count)])]
  transfers between devices with their start and end apart: 76 -> 81, of which waited for: 42 -> 47; matrix products, arithmetic and copies ran while one was open for 0% -> 0% of each run, Pallas kernels for 5% -> 5%
where the time goes in v5:
time: 239 us; the launch traced here: 237 us
  starting transfers between devices  124 us (52%)
  waiting for transfers between devices  77.1 us (32%)
  Pallas kernels  32.4 us (14%)
    ppermute x30, starting transfers between devices, along_pix(): return lax.ppermute(block, 'pix', [(i, i ^ distance) for i in range(count)])  53.5 us
    ppermute x30, waiting for transfers between devices, along_pix(): return lax.ppermute(block, 'pix', [(i, i ^ distance) for i in range(count)])  47.1 us
    ppermute x35, starting transfers between devices, everywhere(): lax.ppermute(sums, ('pix', 'col'), [(i, i ^ move) for i in range(devices)])  37.4 us
    pallas_call x38, Pallas kernels, call(): pl.pallas_call(body, grid_spec=pltpu.PrefetchScalarGridSpec(num_scalar_pr...  32.4 us
    ppermute x7, starting transfers between devices, to_far(): lax.ppermute(block, 'pix', [(a, b) for a, b in route if 0 <= b < count])  21.6 us
    ppermute x35, waiting for transfers between devices, everywhere(): lax.ppermute(sums, ('pix', 'col'), [(i, i ^ move) for i in range(devices)])  20.6 us
    ppermute x7, starting transfers between devices, to_near(): lax.ppermute(block, 'pix', [(i, i ^ 2 ^ crossed) for i in range(count)])  11.3 us
    ppermute x2, waiting for transfers between devices, summed_over_col(): lax.ppermute(block, 'col', [(i, i ^ step) for i in range(count)])  6 us
  transfers between devices with their start and end apart: 81, of which 47 were waited for; matrix products, arithmetic and copies ran while one was open for 0% of the time, Pallas kernels for 5%

profile of v5, /device:TPU:13, one launch (start us, length us, event | category | flops | bytes accessed | tf_op | source)
XLA Modules:
  0.0 236.7 jit_solution(11595663312689504369)
XLA Ops:
  2.8 3.1 %shard_map.68 = (f32[104,1152]{1,0:T(8,128)S(1)}, f32[104,1152]{1,0:T(8,128)S(1)}, f32[48,1152]{1,0:T(8,128)S(1)}, f32[256,1024]{1,0:T(8,128)S(1)}, f32[256,1024...) custom-call(s32[3]{0:T(128)S(1)} %pad_add_fusion.refs_0_, f32[256,2048]{1,0:T(8,128)} %refs_1_.3, ...), custom_call_target="tpu_custom_call" | custom-call | tf_op jit(solution)/shard_map/pallas_call | solution.py:130
  22.5 3.5 %collective-permute-start.12 = (f32[256,256]{1,0:T(8,128)S(1)}, f32[256,256]{1,0:T(8,128)S(1)}, u32[]{:S(2)}, u32[]{:S(2)}) collective-permute-start(f32[256,256]{1,0:T(8,128)S(1)} %get-tuple-element.65), channel_id=1, source_target_pairs={{0,2},{2,0},{4,6},{6,4},{8,10},{10,8},{12,14},{14,12},{16,18},{18,... | collective-permute-start | bytes 786440 | tf_op jit(solution)/shard_map/ppermute | solution.py:25
  28.7 4.3 %collective-permute-start.23 = (f32[104,1152]{1,0:T(8,128)S(1)}, f32[104,1152]{1,0:T(8,128)S(1)}, u32[]{:S(2)}, u32[]{:S(2)}) collective-permute-start(f32[104,1152]{1,0:T(8,128)S(1)} %shard_map.73.refs_3_.refs_1_), channel_id=1, source_target_pairs={{0,8},{2,10},{8,16},{10,18},{12,4},{14,6},{16,24},{18,26},{20,12},... | collective-permute-start | bytes 1437704 | tf_op jit(solution)/shard_map/ppermute | solution.py:36
  55.1 7.3 %collective-permute-done.24.refs_1_ = f32[4,256,128]{2,1,0:T(8,128)S(1)} collective-permute-done((f32[4,256,128]{2,1,0:T(8,128)S(1)}, f32[4,256,128]{2,1,0:T(8,128)S(1)}, u32[]{:S(2)}, u32[]{:S(2)}) %collective-permute-start.24) | collective-permute-done | bytes 524320 | tf_op jit(solution)/shard_map/ppermute | solution.py:25
  62.4 4.8 %collective-permute-start.34 = (f32[96,1152]{1,0:T(8,128)S(1)}, f32[96,1152]{1,0:T(8,128)S(1)}, u32[]{:S(2)}, u32[]{:S(2)}) collective-permute-start(f32[96,1152]{1,0:T(8,128)S(1)} %shard_map.88), channel_id=1, source_target_pairs={{0,6},{2,4},{4,2},{6,0},{8,14},{10,12},{12,10},{14,8},{16,22},{18,... | collective-permute-start | bytes 1327112 | tf_op jit(solution)/shard_map/ppermute | solution.py:30
  69.8 2.9 %collective-permute-done.25.refs_1_ = f32[256,128]{1,0:T(8,128)S(1)} collective-permute-done((f32[256,128]{1,0:T(8,128)S(1)}, f32[256,128]{1,0:T(8,128)S(1)}, u32[]{:S(2)}, u32[]{:S(2)}) %collective-permute-start.25) | collective-permute-done | bytes 131104 | tf_op jit(solution)/shard_map/ppermute | solution.py:25
  76.2 6.0 %collective-permute-done.27.refs_3_ = f32[256,128]{1,0:T(8,128)S(1)} collective-permute-done((f32[256,128]{1,0:T(8,128)S(1)}, f32[256,128]{1,0:T(8,128)S(1)}, u32[]{:S(2)}, u32[]{:S(2)}) %collective-permute-start.27) | collective-permute-done | bytes 131104 | tf_op jit(solution)/shard_map/ppermute | solution.py:25
  84.9 2.9 %collective-permute-done.33.refs_6_.refs_0_ = f32[56,1152]{1,0:T(8,128)S(1)} collective-permute-done((f32[56,1152]{1,0:T(8,128)S(1)}, f32[56,1152]{1,0:T(8,128)S(1)}, u32[]{:S(2)}, u32[]{:S(2)}) %collective-permute-start.33) | collective-permute-done | bytes 258080 | tf_op jit(solution)/shard_map/ppermute | solution.py:30
  87.8 4.3 %collective-permute-done.30.refs_3_ = f32[256,128]{1,0:T(8,128)S(1)} collective-permute-done((f32[256,128]{1,0:T(8,128)S(1)}, f32[256,128]{1,0:T(8,128)S(1)}, u32[]{:S(2)}, u32[]{:S(2)}) %collective-permute-start.30) | collective-permute-done | bytes 131104 | tf_op jit(solution)/shard_map/ppermute | solution.py:25
  95.0 2.8 %collective-permute-start.44 = (f32[56,1152]{1,0:T(8,128)S(1)}, f32[56,1152]{1,0:T(8,128)S(1)}, u32[]{:S(2)}, u32[]{:S(2)}) collective-permute-start(f32[56,1152]{1,0:T(8,128)S(1)} %shard_map.95.refs_4_), channel_id=1, source_target_pairs={{0,8},{2,10},{8,16},{10,18},{12,4},{14,6},{16,24},{18,26},{20,12},... | collective-permute-start | bytes 774152 | tf_op jit(solution)/shard_map/ppermute | solution.py:36
  97.7 4.4 %collective-permute-start.43 = (f32[48,1152]{1,0:T(8,128)S(1)}, f32[48,1152]{1,0:T(8,128)S(1)}, u32[]{:S(2)}, u32[]{:S(2)}) collective-permute-start(f32[48,1152]{1,0:T(8,128)S(1)} %shard_map.94.refs_3_), channel_id=1, source_target_pairs={{0,8},{2,10},{8,16},{10,18},{12,4},{14,6},{16,24},{18,26},{20,12},... | collective-permute-start | bytes 663560 | tf_op jit(solution)/shard_map/ppermute | solution.py:36
  102.2 3.7 %collective-permute-done.35.refs_3_.refs_5_ = f32[4,256,128]{2,1,0:T(8,128)S(1)} collective-permute-done((f32[4,256,128]{2,1,0:T(8,128)S(1)}, f32[4,256,128]{2,1,0:T(8,128)S(1)}, u32[]{:S(2)}, u32[]{:S(2)}) %collective-permute-start.35) | collective-permute-done | bytes 524320 | tf_op jit(solution)/shard_map/ppermute | solution.py:25
  116.0 4.0 %collective-permute-start.41 = (f32[8,128]{1,0:T(8,128)S(1)}, f32[8,128]{1,0:T(8,128)S(1)}, u32[]{:S(2)}, u32[]{:S(2)}) collective-permute-start(f32[8,128]{1,0:T(8,128)S(1)} %shard_map.92.refs_0_), channel_id=1, source_target_pairs={{0,16},{1,17},{2,18},{3,19},{4,20},{5,21},{6,22},{7,23},{8,24},{9,... | collective-permute-start | bytes 12296 | tf_op jit(solution)/shard_map/ppermute | solution.py:61
  123.9 3.8 %collective-permute-start.45 = (f32[256,256]{1,0:T(8,128)S(1)}, f32[256,256]{1,0:T(8,128)S(1)}, u32[]{:S(2)}, u32[]{:S(2)}) collective-permute-start(f32[256,256]{1,0:T(8,128)S(1)} %get-tuple-element.83), channel_id=1, source_target_pairs={{0,2},{2,0},{4,6},{6,4},{8,10},{10,8},{12,14},{14,12},{16,18},{18,... | collective-permute-start | bytes 786440 | tf_op jit(solution)/shard_map/ppermute | solution.py:25
  132.3 4.2 %collective-permute-done.46.refs_1_ = f32[256,256]{1,0:T(8,128)S(1)} collective-permute-done((f32[256,256]{1,0:T(8,128)S(1)}, f32[256,256]{1,0:T(8,128)S(1)}, u32[]{:S(2)}, u32[]{:S(2)}) %collective-permute-start.46) | collective-permute-done | bytes 262176 | tf_op jit(solution)/shard_map/ppermute | solution.py:43
  152.8 2.8 %collective-permute-start.64 = (f32[104,1152]{1,0:T(8,128)S(1)}, f32[104,1152]{1,0:T(8,128)S(1)}, u32[]{:S(2)}, u32[]{:S(2)}) collective-permute-start(f32[104,1152]{1,0:T(8,128)S(1)} %shard_map.108.refs_6_), channel_id=1, source_target_pairs={{0,8},{2,10},{8,16},{10,18},{12,4},{14,6},{16,24},{18,26},{20,12},... | collective-permute-start | bytes 1437704 | tf_op jit(solution)/shard_map/ppermute | solution.py:36
  155.5 5.4 %collective-permute-done.57.refs_1_ = f32[4,256,128]{2,1,0:T(8,128)S(1)} collective-permute-done((f32[4,256,128]{2,1,0:T(8,128)S(1)}, f32[4,256,128]{2,1,0:T(8,128)S(1)}, u32[]{:S(2)}, u32[]{:S(2)}) %collective-permute-start.57) | collective-permute-done | bytes 524320 | tf_op jit(solution)/shard_map/ppermute | solution.py:25
  168.1 4.4 %collective-permute-done.60.refs_3_ = f32[256,128]{1,0:T(8,128)S(1)} collective-permute-done((f32[256,128]{1,0:T(8,128)S(1)}, f32[256,128]{1,0:T(8,128)S(1)}, u32[]{:S(2)}, u32[]{:S(2)}) %collective-permute-start.60) | collective-permute-done | bytes 131104 | tf_op jit(solution)/shard_map/ppermute | solution.py:25
  172.5 4.9 %collective-permute-start.63 = (f32[256,128]{1,0:T(8,128)S(1)}, f32[256,128]{1,0:T(8,128)S(1)}, u32[]{:S(2)}, u32[]{:S(2)}) collective-permute-start(f32[256,128]{1,0:T(8,128)S(1)} %shard_map.107.refs_0_), channel_id=1, source_target_pairs={{0,24},{2,26},{4,28},{6,30},{8,16},{10,18},{12,20},{14,22},{16,8},... | collective-permute-start | bytes 393224 | tf_op jit(solution)/shard_map/ppermute | solution.py:25
  178.7 6.9 %collective-permute-start.77 = (f32[256,1024]{1,0:T(8,128)S(1)}, f32[256,1024]{1,0:T(8,128)S(1)}, u32[]{:S(2)}, u32[]{:S(2)}) collective-permute-start(f32[256,1024]{1,0:T(8,128)S(1)} %get-tuple-element.84.refs_2_.refs_10_.refs_4_.refs_7_.refs_6_.refs_17_), channel_id=1, source_target_pairs={{0,2},{2,0},{4,6},{6,4},{8,10},{10,8},{12,14},{14,12},{16,18},{18,... | collective-permute-start | bytes 3145736 | tf_op jit(solution)/shard_map/ppermute | solution.py:25
  190.6 5.0 %collective-permute-start.78 = (f32[4,256,128]{2,1,0:T(8,128)S(1)}, f32[4,256,128]{2,1,0:T(8,128)S(1)}, u32[]{:S(2)}, u32[]{:S(2)}) collective-permute-start(f32[4,256,128]{2,1,0:T(8,128)S(1)} %shard_map.109.refs_2_.refs_1_.refs_12_), channel_id=1, source_target_pairs={{0,2},{2,0},{4,6},{6,4},{8,10},{10,8},{12,14},{14,12},{16,18},{18,... | collective-permute-start | bytes 1572872 | tf_op jit(solution)/shard_map/ppermute | solution.py:25
  195.8 5.0 %collective-permute-start.79 = (f32[4,256,128]{2,1,0:T(8,128)S(1)}, f32[4,256,128]{2,1,0:T(8,128)S(1)}, u32[]{:S(2)}, u32[]{:S(2)}) collective-permute-start(f32[4,256,128]{2,1,0:T(8,128)S(1)} %collective-permute-done.66.refs_3_.refs_13_), channel_id=1, source_target_pairs={{0,2},{2,0},{4,6},{6,4},{8,10},{10,8},{12,14},{14,12},{16,18},{18,... | collective-permute-start | bytes 1572872 | tf_op jit(solution)/shard_map/ppermute | solution.py:25
  216.5 3.1 %shard_map.115 = (f32[4,256,1024]{2,1,0:T(8,128)S(1)}, f32[4,256,1024]{2,1,0:T(8,128)S(1)}) custom-call(s32[3]{0:T(128)S(1)} %pad_add_fusion.refs_0_, f32[104,1152]{1,0:T(8,128)S(1)} %shard_map.73.refs_3_.refs_1_, f32[104,1152]{1,0:T(8,128)S(1)} %shard_map.85.refs_2_, f32[48,1152]{1,0:T(8,128)S(1)} %shard_map.94.refs_3_, f32[56,1152]{1,0:T(8,128)S(1)} %shard_map.95.refs_4_, ...), custom_call_target="tpu_custom_call" | custom-call | tf_op jit(solution)/shard_map/pallas_call | solution.py:130
  219.6 12.3 %shard_map.116 = (f32[256,2048]{1,0:T(8,128)}, f32[256,1024]{1,0:T(8,128)S(1)}, f32[2,1024,256]{2,1,0:T(8,128)}) custom-call(s32[3]{0:T(128)S(1)} %pad_add_fusion.refs_0_, f32[8,128]{1,0:T(8,128)S(1)} %shard_map.113.refs_1_, f32[2,256,1024]{2,1,0:T(8,128)S(1)} %bitcast.7, f32[2,256,1024]{2,1,0:T(8,128)S(1)} %bitcast.8, ...), custom_call_target="tpu_custom_call" | custom-call | tf_op jit(solution)/shard_map/pallas_call | solution.py:130
  (194 shorter events, 123.9 us)
Async XLA Ops:
  5.9 15.5 %collective-permute-start.11 = (f32[104,1152]{1,0:T(8,128)S(1)}, f32[104,1152]{1,0:T(8,128)S(1)}, u32[]{:S(2)}, u32[]{:S(2)}) collective-permute-start(f32[104,1152]{1,0:T(8,128)S(1)} %get-tuple-element.63), channel_id=1, source_target_pairs={{0,4},{2,6},{4,0},{6,2},{8,12},{10,14},{12,8},{14,10},{16,20},{18,... | collective-permute-start | bytes 1437704 | tf_op jit(solution)/shard_map/ppermute | solution.py:30
  27.3 23.7 %collective-permute-start.22 = (f32[104,1152]{1,0:T(8,128)S(1)}, f32[104,1152]{1,0:T(8,128)S(1)}, u32[]{:S(2)}, u32[]{:S(2)}) collective-permute-start(f32[104,1152]{1,0:T(8,128)S(1)} %shard_map.81), channel_id=1, source_target_pairs={{0,4},{2,6},{4,0},{6,2},{8,12},{10,14},{12,8},{14,10},{16,20},{18,... | collective-permute-start | bytes 1437704 | tf_op jit(solution)/shard_map/ppermute | solution.py:30
  28.7 22.3 %collective-permute-start.23 = (f32[104,1152]{1,0:T(8,128)S(1)}, f32[104,1152]{1,0:T(8,128)S(1)}, u32[]{:S(2)}, u32[]{:S(2)}) collective-permute-start(f32[104,1152]{1,0:T(8,128)S(1)} %shard_map.73.refs_3_.refs_1_), channel_id=1, source_target_pairs={{0,8},{2,10},{8,16},{10,18},{12,4},{14,6},{16,24},{18,26},{20,12},... | collective-permute-start | bytes 1437704 | tf_op jit(solution)/shard_map/ppermute | solution.py:36
  52.5 9.9 %collective-permute-start.24 = (f32[4,256,128]{2,1,0:T(8,128)S(1)}, f32[4,256,128]{2,1,0:T(8,128)S(1)}, u32[]{:S(2)}, u32[]{:S(2)}) collective-permute-start(f32[4,256,128]{2,1,0:T(8,128)S(1)} %get-tuple-element.73.refs_1_), channel_id=1, source_target_pairs={{0,4},{2,6},{4,0},{6,2},{8,12},{10,14},{12,8},{14,10},{16,20},{18,... | collective-permute-start | bytes 1572872 | tf_op jit(solution)/shard_map/ppermute | solution.py:25
  53.0 29.3 %collective-permute-start.31 = (f32[104,1152]{1,0:T(8,128)S(1)}, f32[104,1152]{1,0:T(8,128)S(1)}, u32[]{:S(2)}, u32[]{:S(2)}) collective-permute-start(f32[104,1152]{1,0:T(8,128)S(1)} %shard_map.85.refs_2_), channel_id=1, source_target_pairs={{0,8},{2,10},{8,16},{10,18},{12,4},{14,6},{16,24},{18,26},{20,12},... | collective-permute-start | bytes 1437704 | tf_op jit(solution)/shard_map/ppermute | solution.py:36
  62.4 30.7 %collective-permute-start.34 = (f32[96,1152]{1,0:T(8,128)S(1)}, f32[96,1152]{1,0:T(8,128)S(1)}, u32[]{:S(2)}, u32[]{:S(2)}) collective-permute-start(f32[96,1152]{1,0:T(8,128)S(1)} %shard_map.88), channel_id=1, source_target_pairs={{0,6},{2,4},{4,2},{6,0},{8,14},{10,12},{12,10},{14,8},{16,22},{18,... | collective-permute-start | bytes 1327112 | tf_op jit(solution)/shard_map/ppermute | solution.py:30
  68.8 14.7 %collective-permute-start.32 = (f32[48,1152]{1,0:T(8,128)S(1)}, f32[48,1152]{1,0:T(8,128)S(1)}, u32[]{:S(2)}, u32[]{:S(2)}) collective-permute-start(f32[48,1152]{1,0:T(8,128)S(1)} %shard_map.86), channel_id=1, source_target_pairs={{0,4},{2,6},{4,0},{6,2},{8,12},{10,14},{12,8},{14,10},{16,20},{18,... | collective-permute-start | bytes 663560 | tf_op jit(solution)/shard_map/ppermute | solution.py:30
  75.5 12.3 %collective-permute-start.33 = (f32[56,1152]{1,0:T(8,128)S(1)}, f32[56,1152]{1,0:T(8,128)S(1)}, u32[]{:S(2)}, u32[]{:S(2)}) collective-permute-start(f32[56,1152]{1,0:T(8,128)S(1)} %shard_map.87), channel_id=1, source_target_pairs={{0,6},{2,4},{4,2},{6,0},{8,14},{10,12},{12,10},{14,8},{16,22},{18,... | collective-permute-start | bytes 774152 | tf_op jit(solution)/shard_map/ppermute | solution.py:30
  82.2 9.9 %collective-permute-start.30 = (f32[256,128]{1,0:T(8,128)S(1)}, f32[256,128]{1,0:T(8,128)S(1)}, u32[]{:S(2)}, u32[]{:S(2)}) collective-permute-start(f32[256,128]{1,0:T(8,128)S(1)} %shard_map.84.refs_0_), channel_id=1, source_target_pairs={{0,24},{2,26},{4,28},{6,30},{8,16},{10,18},{12,20},{14,22},{16,8},... | collective-permute-start | bytes 393224 | tf_op jit(solution)/shard_map/ppermute | solution.py:25
  82.3 10.8 %collective-permute-start.29 = (f32[256,128]{1,0:T(8,128)S(1)}, f32[256,128]{1,0:T(8,128)S(1)}, u32[]{:S(2)}, u32[]{:S(2)}) collective-permute-start(f32[256,128]{1,0:T(8,128)S(1)} %shard_map.84.refs_0_), channel_id=1, source_target_pairs={{0,16},{2,18},{4,20},{6,22},{8,24},{10,26},{12,28},{14,30},{16,0},... | collective-permute-start | bytes 393224 | tf_op jit(solution)/shard_map/ppermute | solution.py:25
  93.1 12.8 %collective-permute-start.35 = (f32[4,256,128]{2,1,0:T(8,128)S(1)}, f32[4,256,128]{2,1,0:T(8,128)S(1)}, u32[]{:S(2)}, u32[]{:S(2)}) collective-permute-start(f32[4,256,128]{2,1,0:T(8,128)S(1)} %shard_map.89.refs_2_.refs_1_.refs_4_), channel_id=1, source_target_pairs={{0,4},{2,6},{4,0},{6,2},{8,12},{10,14},{12,8},{14,10},{16,20},{18,... | collective-permute-start | bytes 1572872 | tf_op jit(solution)/shard_map/ppermute | solution.py:25
  95.0 27.5 %collective-permute-start.44 = (f32[56,1152]{1,0:T(8,128)S(1)}, f32[56,1152]{1,0:T(8,128)S(1)}, u32[]{:S(2)}, u32[]{:S(2)}) collective-permute-start(f32[56,1152]{1,0:T(8,128)S(1)} %shard_map.95.refs_4_), channel_id=1, source_target_pairs={{0,8},{2,10},{8,16},{10,18},{12,4},{14,6},{16,24},{18,26},{20,12},... | collective-permute-start | bytes 774152 | tf_op jit(solution)/shard_map/ppermute | solution.py:36
  97.7 24.7 %collective-permute-start.43 = (f32[48,1152]{1,0:T(8,128)S(1)}, f32[48,1152]{1,0:T(8,128)S(1)}, u32[]{:S(2)}, u32[]{:S(2)}) collective-permute-start(f32[48,1152]{1,0:T(8,128)S(1)} %shard_map.94.refs_3_), channel_id=1, source_target_pairs={{0,8},{2,10},{8,16},{10,18},{12,4},{14,6},{16,24},{18,26},{20,12},... | collective-permute-start | bytes 663560 | tf_op jit(solution)/shard_map/ppermute | solution.py:36
  129.1 20.5 %collective-permute-start.55 = (f32[104,1152]{1,0:T(8,128)S(1)}, f32[104,1152]{1,0:T(8,128)S(1)}, u32[]{:S(2)}, u32[]{:S(2)}) collective-permute-start(f32[104,1152]{1,0:T(8,128)S(1)} %shard_map.103), channel_id=1, source_target_pairs={{0,6},{2,4},{4,2},{6,0},{8,14},{10,12},{12,10},{14,8},{16,22},{18,... | collective-permute-start | bytes 1437704 | tf_op jit(solution)/shard_map/ppermute | solution.py:30
  129.7 19.9 %collective-permute-start.56 = (f32[96,1152]{1,0:T(8,128)S(1)}, f32[96,1152]{1,0:T(8,128)S(1)}, u32[]{:S(2)}, u32[]{:S(2)}) collective-permute-start(f32[96,1152]{1,0:T(8,128)S(1)} %shard_map.104.refs_5_), channel_id=1, source_target_pairs={{0,8},{2,10},{8,16},{10,18},{12,4},{14,6},{16,24},{18,26},{20,12},... | collective-permute-start | bytes 1327112 | tf_op jit(solution)/shard_map/ppermute | solution.py:36
  151.2 9.7 %collective-permute-start.57 = (f32[4,256,128]{2,1,0:T(8,128)S(1)}, f32[4,256,128]{2,1,0:T(8,128)S(1)}, u32[]{:S(2)}, u32[]{:S(2)}) collective-permute-start(f32[4,256,128]{2,1,0:T(8,128)S(1)} %get-tuple-element.91.refs_1_), channel_id=1, source_target_pairs={{0,4},{2,6},{4,0},{6,2},{8,12},{10,14},{12,8},{14,10},{16,20},{18,... | collective-permute-start | bytes 1572872 | tf_op jit(solution)/shard_map/ppermute | solution.py:25
  152.8 25.9 %collective-permute-start.64 = (f32[104,1152]{1,0:T(8,128)S(1)}, f32[104,1152]{1,0:T(8,128)S(1)}, u32[]{:S(2)}, u32[]{:S(2)}) collective-permute-start(f32[104,1152]{1,0:T(8,128)S(1)} %shard_map.108.refs_6_), channel_id=1, source_target_pairs={{0,8},{2,10},{8,16},{10,18},{12,4},{14,6},{16,24},{18,26},{20,12},... | collective-permute-start | bytes 1437704 | tf_op jit(solution)/shard_map/ppermute | solution.py:36
  164.7 20.9 %collective-permute-start.65 = (f32[256,256]{1,0:T(8,128)S(1)}, f32[256,256]{1,0:T(8,128)S(1)}, u32[]{:S(2)}, u32[]{:S(2)}) collective-permute-start(f32[256,256]{1,0:T(8,128)S(1)} %get-tuple-element.97), channel_id=1, source_target_pairs={{0,4},{2,6},{4,0},{6,2},{8,12},{10,14},{12,8},{14,10},{16,20},{18,... | collective-permute-start | bytes 786440 | tf_op jit(solution)/shard_map/ppermute | solution.py:30
  172.5 13.1 %collective-permute-start.63 = (f32[256,128]{1,0:T(8,128)S(1)}, f32[256,128]{1,0:T(8,128)S(1)}, u32[]{:S(2)}, u32[]{:S(2)}) collective-permute-start(f32[256,128]{1,0:T(8,128)S(1)} %shard_map.107.refs_0_), channel_id=1, source_target_pairs={{0,24},{2,26},{4,28},{6,30},{8,16},{10,18},{12,20},{14,22},{16,8},... | collective-permute-start | bytes 393224 | tf_op jit(solution)/shard_map/ppermute | solution.py:25
  178.7 40.9 %collective-permute-start.77 = (f32[256,1024]{1,0:T(8,128)S(1)}, f32[256,1024]{1,0:T(8,128)S(1)}, u32[]{:S(2)}, u32[]{:S(2)}) collective-permute-start(f32[256,1024]{1,0:T(8,128)S(1)} %get-tuple-element.84.refs_2_.refs_10_.refs_4_.refs_7_.refs_6_.refs_17_), channel_id=1, source_target_pairs={{0,2},{2,0},{4,6},{6,4},{8,10},{10,8},{12,14},{14,12},{16,18},{18,... | collective-permute-start | bytes 3145736 | tf_op jit(solution)/shard_map/ppermute | solution.py:25
  185.7 10.2 %collective-permute-start.66 = (f32[4,256,128]{2,1,0:T(8,128)S(1)}, f32[4,256,128]{2,1,0:T(8,128)S(1)}, u32[]{:S(2)}, u32[]{:S(2)}) collective-permute-start(f32[4,256,128]{2,1,0:T(8,128)S(1)} %shard_map.109.refs_2_.refs_1_.refs_12_), channel_id=1, source_target_pairs={{0,4},{2,6},{4,0},{6,2},{8,12},{10,14},{12,8},{14,10},{16,20},{18,... | collective-permute-start | bytes 1572872 | tf_op jit(solution)/shard_map/ppermute | solution.py:25
  187.9 15.6 %collective-permute-start.75 = (f32[256,256]{1,0:T(8,128)S(1)}, f32[256,256]{1,0:T(8,128)S(1)}, u32[]{:S(2)}, u32[]{:S(2)}) collective-permute-start(f32[256,256]{1,0:T(8,128)S(1)} %shard_map.114.refs_13_.refs_6_), channel_id=1, source_target_pairs={{0,8},{2,10},{8,16},{10,18},{12,4},{14,6},{16,24},{18,26},{20,12},... | collective-permute-start | bytes 786440 | tf_op jit(solution)/shard_map/ppermute | solution.py:36
  190.6 29.0 %collective-permute-start.78 = (f32[4,256,128]{2,1,0:T(8,128)S(1)}, f32[4,256,128]{2,1,0:T(8,128)S(1)}, u32[]{:S(2)}, u32[]{:S(2)}) collective-permute-start(f32[4,256,128]{2,1,0:T(8,128)S(1)} %shard_map.109.refs_2_.refs_1_.refs_12_), channel_id=1, source_target_pairs={{0,2},{2,0},{4,6},{6,4},{8,10},{10,8},{12,14},{14,12},{16,18},{18,... | collective-permute-start | bytes 1572872 | tf_op jit(solution)/shard_map/ppermute | solution.py:25
  195.8 23.8 %collective-permute-start.79 = (f32[4,256,128]{2,1,0:T(8,128)S(1)}, f32[4,256,128]{2,1,0:T(8,128)S(1)}, u32[]{:S(2)}, u32[]{:S(2)}) collective-permute-start(f32[4,256,128]{2,1,0:T(8,128)S(1)} %collective-permute-done.66.refs_3_.refs_13_), channel_id=1, source_target_pairs={{0,2},{2,0},{4,6},{6,4},{8,10},{10,8},{12,14},{14,12},{16,18},{18,... | collective-permute-start | bytes 1572872 | tf_op jit(solution)/shard_map/ppermute | solution.py:25
  (59 other events, 234.4 us)

commit v6 on v5

--- a/solution.py
+++ b/solution.py
@@ -45,7 +45,7 @@
     return block
 
 
-def everywhere(sums, late=False):
+def everywhere(sums, late=False, beside=None):
     count = lax.axis_size("col")
     devices = lax.axis_size("pix") * count
     bits = [count << k for k in range(1, (devices // count).bit_length() - 1)]
@@ -60,8 +60,10 @@
         parts = [
             lax.ppermute(sums, ("pix", "col"), [(i, i ^ move) for i in range(devices)]) for move in moves[1:]
         ]
-        sums = plus(sums, *parts)
-    return sums
+        sums = plus(sums, *parts, after=extra[-1:] if beside and stage is stages[2] else ())
+        if beside and stage is stages[1]:
+            extra = beside(sums)
+    return (sums, extra) if beside else sums
 
 
 def halves(x):
@@ -149,8 +151,8 @@
     refs[-1][...] = total
 
 
-def plus(*arrays):
-    (total,) = call(plus_kernel, [VMEM] * len(arrays), [VMEM], [shaped(*arrays[0].shape)], [], *arrays)
+def plus(*arrays, after=()):
+    (total,) = call(plus_kernel, [VMEM] * len(arrays), [VMEM], [shaped(*arrays[0].shape)], [], *arrays, after=after)
     return total
 
 
@@ -282,13 +284,13 @@
     return step, before + 2.0 * step * cross + step * step * curve
 
 
-def next_grad_kernel(total, sums_ref, res_ref, shift_ref, vt_ref, even_ref, odd_ref,
+def next_grad_kernel(total, sums_ref, res_ref, shift_ref, vt_ref, step_ref,
                      res_out, vt_out, own_ref, other_ref):
     size, spread = column_sums(read_sums(sums_ref, 4))
     level = level_from(spread, total)
     grad = None
-    for k, cols in enumerate(tiles(res_ref)):
-        vt = vt_ref[:, cols] - size * jnp.concatenate([even_ref[k], odd_ref[k]], axis=1)
+    for cols in tiles(res_ref):
+        vt = vt_ref[:, cols] - size * step_ref[:, cols]
         vt_out[:, cols] = vt
         res = res_ref[:, cols] + size * shift_ref[:, cols]
         res_out[:, cols] = res
@@ -310,7 +312,7 @@
 
 
 def pix_step_kernel(total, first, level_sums, sums_ref, own_u, other_u, own_grad, other_grad, res_ref,
-                    change_ref, own_out, other_out, res_out, even_ref, odd_ref, ut_parts):
+                    change_ref, own_out, other_out, res_out, copy_ref, even_ref, odd_ref, ut_parts):
     pixels = own_grad.shape[0]
     top, curve = read_sums(sums_ref, 2)
     size = top / curve
@@ -323,6 +325,8 @@
     for part, (old, grad, out) in enumerate(strips):
         u = old[...] - size * grad[...]
         out[...] = u
+        if part == 0:
+            copy_ref[...] = u
         high, low = halves(u.T)
         for k, value in enumerate((high, high, low)):
             first_col = (2 * k + part) * pixels
@@ -337,11 +341,14 @@
         odd_ref[k] = grad[:, LANES:]
 
 
-def shift_kernel(chips, own_u, other_u, even_ref, odd_ref, weight_ref, res_ref, shift_ref, sums_ref, u_parts):
+def shift_kernel(chips, own_u, other_u, weight_ref, res_ref, *refs):
+    chunk_refs = refs[:GROUP]
+    shift_ref, grad_ref, sums_ref, u_parts = refs[GROUP:]
     split_factor((own_u, other_u), u_parts)
     top = curve = cross = spread = 0.0
     for k, cols in enumerate(tiles(res_ref)):
-        grad = jnp.concatenate([even_ref[k], odd_ref[k]], axis=1)
+        grad = jnp.concatenate([chunk_refs[2 * k][...], chunk_refs[2 * k + 1][...]], axis=1)
+        grad_ref[:, cols] = grad
         top = top + rows_folded(grad * grad)
         shift = weight_ref[:, cols] * product(u_parts[...], right_parts(grad, 0))
         shift_ref[:, cols] = shift
@@ -368,24 +375,14 @@
                 res_ref[part, rows, cols] = res
 
 
-def add_kernel(kept_ref, from_ref, *refs):
-    count = kept_ref.shape[0]
-    held = (len(refs) - count) // 2
-    for k, ref in enumerate(refs[held : held + count]):
+def add_kernel(kept_ref, from_ref, *out_refs):
+    for k, ref in enumerate(out_refs):
         ref[...] = kept_ref[k] + from_ref[k]
-    for source, target in zip(refs[:held], refs[held + count :]):
-        target[...] = source[...]
-
-
-def stack_kernel(*refs):
-    for k, ref in enumerate(refs[:-1]):
-        refs[-1][k] = ref[...]
 
 
 def flux_of(diff):
     below = 1.0 + diff * diff
-    guess = pl.reciprocal(below, approx=True)
-    return diff * (guess * (2.0 - below * guess))
+    return diff * pl.reciprocal(below, approx=True)
 
 
 PAD = 8
@@ -420,8 +417,8 @@
 
 def smooth_kernel(total, chips, place, sums_ref, res_ref, shift_ref, rim_ref, rim_weight, *refs):
     factors = refs[:4]
-    own_vt, other_vt, own_even, own_odd, other_even, other_odd = refs[4:10]
-    own_ref, other_ref, v_ref, u_parts, rim_shift, layer, once = refs[10:]
+    own_vt, other_vt, own_grad, other_grad = refs[4:8]
+    own_ref, other_ref, v_ref, u_parts, rim_shift, layer, once = refs[8:]
     step = pl.program_id(0)
     core, chip = place[0], place[2]
     pixels = own_ref.shape[0]
@@ -433,8 +430,8 @@
     size, spread = column_sums(read_sums(sums_ref, 4))
     level = level_from(spread, total)
     inverse = 1.0 / level
-    grad = jnp.concatenate([own_even[step], own_odd[step]], axis=1)
-    moved = product(u_parts[...], right_parts(grad, 0))
+    both_chunks = pl.ds(pl.multiple_of(step * 2 * LANES, 2 * LANES), 2 * LANES)
+    moved = product(u_parts[...], right_parts(own_grad[:, both_chunks], 0))
     rim_shift[...] = moved.reshape(rim_shift.shape)
 
     def cut(res):
@@ -448,13 +445,12 @@
     keep_own = jnp.where(core == 0, keep_north, keep_south)
     keep_other = jnp.where(core == 0, keep_south, keep_north)
     inner = slice(PAD, PAD + pixels)
-    pair = ((own_even, other_even), (own_odd, other_odd))
     for b in range(2):
         cols = pl.ds(pl.multiple_of((2 * step + b) * LANES, LANES), LANES)
         here = slice(b * LANES, (b + 1) * LANES)
         there = pl.ds(pl.multiple_of((chip % 2 ^ b) * LANES, LANES), LANES)
-        v_ref[core, there] = (own_vt[:, cols] - size * pair[b][0][step]).T
-        v_ref[1 - core, there] = (other_vt[:, cols] - size * pair[b][1][step]).T
+        v_ref[core, there] = (own_vt[:, cols] - size * own_grad[:, cols]).T
+        v_ref[1 - core, there] = (other_vt[:, cols] - size * other_grad[:, cols]).T
         for k in range(2):
             layer[2 + k, inner] = cut(res_ref[k, :, cols] + size * shift_ref[k, :, cols])
             for first, base in ((0, beyond_own), (4, beyond_other)):
@@ -473,21 +469,23 @@
         smooth_rows(once, to_cloud, keep_own, keep_other, 0, 2)
 
 
-def summed_over_chips(even, odd, held, beside):
+def summed_over_chips(even, odd, meanwhile):
     chips = lax.axis_size("pix") // 2
     count, rank, lanes = even.shape
     from_odd = along_pix(odd, 2)
-    shapes = [shaped(rank, lanes)] * count + [shaped(*x.shape) for x in held]
-    kept = call(
-        add_kernel, [VMEM] * (2 + len(held)), [VMEM] * len(shapes), shapes, [], even, from_odd, *held, beside=beside,
-    )
-    mine = plus(kept[0], *[along_pix(kept[k], 4 * k) for k in (1, 2, 3)])
+    kept = call(add_kernel, [VMEM] * 2, [VMEM] * count, [shaped(rank, lanes)] * count, [], even, from_odd)
+    before_sum, before_end = meanwhile(from_odd)
+    mine = plus(kept[0], *[along_pix(kept[k], 4 * k) for k in (1, 2, 3)], after=before_sum)
     distance = GROUP
     while distance < chips:
         mine = plus(mine, along_pix(mine, 2 * distance))
         distance *= 2
     parts = [mine] + [along_pix(mine, 4 * k) for k in (1, 2, 3)]
-    return parts, from_odd, kept[count:]
+    parts[3] = held_until(parts[3], *before_end)
+    summed = []
+    for part in parts:
+        summed += [part, along_pix(part, 2)]
+    return summed
 
 
 def per_device(observed, valid_mask, pix_factor, col_factor):
@@ -510,7 +508,7 @@
     steps = half // wide
     sums_shape = shaped(8, LANES)
     pix_shape = shaped(pixels, rank)
-    grad_shape = shaped(steps, rank, LANES)
+    half_shape = shaped(steps, rank, LANES)
     vt_shape = pltpu.VMEM((rank, half), f32)
     local = pltpu.VMEM((both, half), f32)
     strip = pltpu.VMEM((pixels, half), f32)
@@ -532,10 +530,10 @@
     *own_pieces, vt, own_res, own_weight, own_sum = call(
         own_kernel, half_in + [pl.BlockSpec((half, rank), lambda t, s: (s[0], 0)), VMEM], [VMEM] * 7,
         pieces(own_rows) + [vt_shape, strip, strip, shaped(8, wide)], [],
-        in_hbm(observed), in_hbm(valid_mask), in_hbm(col_factor), own_u, grid=(1,), place=place,
+        in_hbm(observed), in_hbm(valid_mask), in_hbm(col_factor), own_u, grid=(1,), place=place, after=[other_u],
     )
     near_own, near_other, far_own, far_other = [None] * 3, [None] * 3, [None] * 3, [None] * 3
-    near_own[0] = to_near(own_pieces[0], 0)
+    near_own[0] = to_near(held_until(own_pieces[0], *received), 0)
     residual, weight, sums = call(
         other_kernel, [SMEM] + [VMEM] * 8, [VMEM] * 3, [local, local, sums_shape], [],
         place, *received, other_u, in_vmem(vt), in_vmem(own_res), in_vmem(own_weight), own_sum,
@@ -559,9 +557,9 @@
             far_other[1] = to_far(near_other[1])
             passed = [near_other[2], far_other[1]]
             residual, vt, own_part, other_part = call(
-                functools.partial(next_grad_kernel, total), [VMEM] * 6, [VMEM] * 4,
+                functools.partial(next_grad_kernel, total), [VMEM] * 5, [VMEM] * 4,
                 [local, vt_shape, pix_shape, pix_shape], [],
-                level_sums, in_vmem(residual), in_vmem(shift), in_vmem(vt), even, odd, after=[far_own[2], far_other[0]],
+                level_sums, in_vmem(residual), in_vmem(shift), in_vmem(vt), in_vmem(grad), after=[far_own[2], far_other[0]],
             )
         own_grad = summed_over_col(plus(own_part, along_pix(other_part, 1)))
         other_grad = along_pix(own_grad, 1)
@@ -571,58 +569,70 @@
             beside=[residual],
         )
         pix_sums = everywhere(sums)
-        own_u, other_u, residual, even, odd = call(
-            functools.partial(pix_step_kernel, total, first), [VMEM] * 8, [VMEM] * 5,
-            [pix_shape, pix_shape, local, grad_shape, grad_shape], [pltpu.VMEM((rank, 3 * both), bf16)],
+        u_next, other_u, residual, own_u, even, odd = call(
+            functools.partial(pix_step_kernel, total, first), [VMEM] * 8, [VMEM] * 6,
+            [pix_shape, pix_shape, local, pix_shape, half_shape, half_shape], [pltpu.VMEM((rank, 3 * both), bf16)],
             level_sums, pix_sums, own_u, other_u, own_grad, other_grad, in_vmem(residual),
             in_vmem(change), after=passed, beside=[vt, weight],
         )
-        alive = [residual, vt, weight, own_u, other_u]
         if first:
             near_own[1] = held_until(near_own[1], odd)
             far_own[1] = to_far(near_own[1])
-            parts, moved, _ = summed_over_chips(even, odd, [], alive)
-            near_own[2] = to_near(held_until(own_pieces[2], moved), 0)
-            near_other[0] = to_near(held_until(other_pieces[0], moved), 1)
-            near_other[1] = to_near(held_until(other_pieces[1], moved), 1)
-            passed = [far_own[1], near_own[2], near_other[0], near_other[1]]
+
+            def meanwhile(moved):
+                near_own[2] = to_near(held_until(own_pieces[2], moved), 0)
+                near_other[0] = to_near(held_until(other_pieces[0], moved), 1)
+                near_other[1] = to_near(held_until(other_pieces[1], moved), 1)
+                return [], [far_own[1], near_own[2], near_other[0]]
+
         else:
             near_other[2] = held_until(near_other[2], odd)
             far_other[2] = to_far(near_other[2])
-            parts, moved, sent = summed_over_chips(even, odd, [own_u], alive)
-            near_u = to_near(sent[0], 0)
+            sent = []
+
+            def meanwhile(moved):
+                sent.append(held_until(own_u, moved))
+                sent.append(to_near(sent[0], 0))
+                return [], [far_other[2], sent[1]]
+
             other_vt = along_pix(vt, 1)
-            passed = [far_other[2], near_u]
-        (even,) = call(
-            stack_kernel, [VMEM] * steps, [VMEM], [grad_shape], [], *parts, after=passed, beside=alive,
-        )
-        odd = along_pix(even, 2)
+        summed = summed_over_chips(even, odd, meanwhile)
         if first:
-            near_own[2] = held_until(near_own[2], even)
-            near_other[0] = held_until(near_other[0], even)
+            near_own[2] = held_until(near_own[2], summed[6])
+            near_other[0] = held_until(near_other[0], summed[6])
             far_own[2] = to_far(near_own[2])
             far_other[0] = to_far(near_other[0])
+            passed = near_other[1:2]
         else:
-            near_u = held_until(near_u, even)
+            own_u = sent[0]
+            near_u = held_until(sent[1], summed[6])
             far_u = to_far(near_u)
-        shift, sums = call(
-            functools.partial(shift_kernel, chips), [VMEM] * 6, [VMEM] * 2,
-            [local, sums_shape], factor_scratch, own_u, other_u, even, odd, in_vmem(weight),
-            in_vmem(residual), beside=[vt],
+            passed = [far_u]
+        shift, grad, sums = call(
+            functools.partial(shift_kernel, chips), [VMEM] * (4 + GROUP), [VMEM] * 3,
+            [local, vt_shape, sums_shape], factor_scratch, own_u, other_u, in_vmem(weight), in_vmem(residual),
+            *summed, after=passed, beside=[vt],
         )
-        level_sums = everywhere(sums)
-
-    factors = [near_u, along_pix(near_u, 1), far_u, along_pix(far_u, 1)]
+        if first:
+            level_sums = everywhere(sums)
+
+    near_other_u = along_pix(near_u, 1)
     rim_scratch = [pltpu.VMEM((2 * both, 3 * rank), bf16)]
     rim_shape = pltpu.VMEM((4, pixels, half), f32)
-    rim_res, rim_weight = call(
-        rim_kernel, [SMEM] + [VMEM] * 17, [VMEM] * 2, [rim_shape] * 2, rim_scratch,
-        place, *near_own, *near_other, *far_own, *far_other, *factors, in_vmem(vt), after=[sums],
-    )
-    grads = [even, odd, along_pix(even, 1), along_pix(odd, 1)]
+
+    def rim(group_sums):
+        far = held_until(far_u, group_sums)
+        factors = [near_u, near_other_u, far, along_pix(far, 1)]
+        other_grad = along_pix(held_until(grad, group_sums), 1)
+        return factors, other_grad, *call(
+            rim_kernel, [SMEM] + [VMEM] * 17, [VMEM] * 2, [rim_shape] * 2, rim_scratch,
+            place, *near_own, *near_other, *far_own, *far_other, *factors, in_vmem(vt), after=[group_sums],
+        )
+
+    level_sums, (factors, other_grad, rim_res, rim_weight) = everywhere(sums, beside=rim)
     pair = lambda s, t: s[1] // 2 ^ t
     own_cloud, other_cloud, v = call(
-        functools.partial(smooth_kernel, total, chips), [VMEM] * 15,
+        functools.partial(smooth_kernel, total, chips), [VMEM] * 13,
         [
             pl.BlockSpec((pixels, wide), lambda t, s: (0, s[0] * steps + pair(s, t))),
             pl.BlockSpec((pixels, wide), lambda t, s: (0, pair(s, t))),
@@ -635,11 +645,12 @@
             pltpu.VMEM((4, pixels + 2 * PAD, LANES), f32),
         ],
         level_sums, in_vmem(residual.reshape(2, pixels, half)), in_vmem(shift.reshape(2, pixels, half)),
-        in_vmem(rim_res), in_vmem(rim_weight), *factors, in_vmem(vt), other_vt, *grads, grid=(steps,), place=place,
+        in_vmem(rim_res), in_vmem(rim_weight), *factors, in_vmem(vt), other_vt, in_vmem(grad),
+        other_grad, grid=(steps,), place=place,
     )
     from_other = along_pix(other_cloud, 1)
     cloud = lax.dynamic_update_slice(own_cloud, from_other, (0, (1 - core) * half))
-    return own_u, v.reshape(columns, rank), cloud
+    return u_next, v.reshape(columns, rank), cloud
 
 
 def solution(mesh):

time: 239 us -> 232 us (0.971)
  starting transfers between devices: 124 us -> 120 us
    ppermute x30 -> x35, starting transfers between devices: 53.5 us -> 42.1 us  [along_pix(): return lax.ppermute(block, 'pix', [(i, i ^ distance) for i in range(count)])]
    ppermute x35, starting transfers between devices: 37.4 us -> 42.9 us  [everywhere(): lax.ppermute(sums, ('pix', 'col'), [(i, i ^ move) for i in range(devices)])]
    ppermute x30 -> x35, waiting for transfers between devices: 47.1 us -> 52 us  [along_pix(): return lax.ppermute(block, 'pix', [(i, i ^ distance) for i in range(count)])]
    ppermute x7, waiting for transfers between devices: 3.43 us -> 0.02 us  [to_near(): lax.ppermute(block, 'pix', [(i, i ^ 2 ^ crossed) for i in range(count)])]
    ppermute x7, starting transfers between devices: 11.3 us -> 14.7 us  [to_near(): lax.ppermute(block, 'pix', [(i, i ^ 2 ^ crossed) for i in range(count)])]
    pallas_call x38 -> x36, Pallas kernels: 32.4 us -> 30.7 us  [call(): pl.pallas_call(body, grid_spec=pltpu.PrefetchScalarGridSpec(num_scalar_pr...]
  transfers between devices with their start and end apart: 81 -> 86, of which waited for: 47 -> 48; matrix products, arithmetic and copies ran while one was open for 0% -> 0% of each run, Pallas kernels for 5% -> 5%
where the time goes in v6:
time: 232 us; the launch traced here: 230 us
  starting transfers between devices  120 us (52%)
  waiting for transfers between devices  76.7 us (33%)
  Pallas kernels  30.8 us (13%)
    ppermute x35, waiting for transfers between devices, along_pix(): return lax.ppermute(block, 'pix', [(i, i ^ distance) for i in range(count)])  52 us
    ppermute x35, starting transfers between devices, everywhere(): lax.ppermute(sums, ('pix', 'col'), [(i, i ^ move) for i in range(devices)])  42.9 us
    ppermute x35, starting transfers between devices, along_pix(): return lax.ppermute(block, 'pix', [(i, i ^ distance) for i in range(count)])  42.1 us
    pallas_call x36, Pallas kernels, call(): pl.pallas_call(body, grid_spec=pltpu.PrefetchScalarGridSpec(num_scalar_pr...  30.7 us
    ppermute x35, waiting for transfers between devices, everywhere(): lax.ppermute(sums, ('pix', 'col'), [(i, i ^ move) for i in range(devices)])  20.5 us
    ppermute x7, starting transfers between devices, to_far(): lax.ppermute(block, 'pix', [(a, b) for a, b in route if 0 <= b < count])  20.4 us
    ppermute x7, starting transfers between devices, to_near(): lax.ppermute(block, 'pix', [(i, i ^ 2 ^ crossed) for i in range(count)])  14.7 us
  transfers between devices with their start and end apart: 86, of which 48 were waited for; matrix products, arithmetic and copies ran while one was open for 0% of the time, Pallas kernels for 5%

profile of v6, /device:TPU:13, one launch (start us, length us, event | category | flops | bytes accessed | tf_op | source)
XLA Modules:
  0.0 230.1 jit_solution(1931270949630132356)
XLA Ops:
  5.2 3.1 %shard_map.68 = (f32[104,1152]{1,0:T(8,128)S(1)}, f32[104,1152]{1,0:T(8,128)S(1)}, f32[48,1152]{1,0:T(8,128)S(1)}, f32[256,1024]{1,0:T(8,128)S(1)}, f32[256,1024...) custom-call(s32[3]{0:T(128)S(1)} %pad_add_fusion.refs_0_, f32[256,2048]{1,0:T(8,128)} %refs_1_.3, ...), custom_call_target="tpu_custom_call" | custom-call | tf_op jit(solution)/shard_map/pallas_call | solution.py:132
  22.7 3.5 %collective-permute-start.12 = (f32[256,256]{1,0:T(8,128)S(1)}, f32[256,256]{1,0:T(8,128)S(1)}, u32[]{:S(2)}, u32[]{:S(2)}) collective-permute-start(f32[256,256]{1,0:T(8,128)S(1)} %get-tuple-element.67), channel_id=1, source_target_pairs={{0,2},{2,0},{4,6},{6,4},{8,10},{10,8},{12,14},{14,12},{16,18},{18,... | collective-permute-start | bytes 786440 | tf_op jit(solution)/shard_map/ppermute | solution.py:25
  28.9 4.3 %collective-permute-start.23 = (f32[104,1152]{1,0:T(8,128)S(1)}, f32[104,1152]{1,0:T(8,128)S(1)}, u32[]{:S(2)}, u32[]{:S(2)}) collective-permute-start(f32[104,1152]{1,0:T(8,128)S(1)} %shard_map.74.refs_3_.refs_1_), channel_id=1, source_target_pairs={{0,8},{2,10},{8,16},{10,18},{12,4},{14,6},{16,24},{18,26},{20,12},... | collective-permute-start | bytes 1437704 | tf_op jit(solution)/shard_map/ppermute | solution.py:36
  44.8 2.4 %collective-permute-start.21 = (f32[8,128]{1,0:T(8,128)S(1)}, f32[8,128]{1,0:T(8,128)S(1)}, u32[]{:S(2)}, u32[]{:S(2)}) collective-permute-start(f32[8,128]{1,0:T(8,128)S(1)} %shard_map.80.refs_0_), channel_id=1, source_target_pairs={{0,24},{1,25},{2,26},{3,27},{4,28},{5,29},{6,30},{7,31},{8,16},{9,... | collective-permute-start | bytes 12296 | tf_op jit(solution)/shard_map/ppermute | solution.py:61
  55.4 7.3 %collective-permute-done.24.refs_1_ = f32[4,256,128]{2,1,0:T(8,128)S(1)} collective-permute-done((f32[4,256,128]{2,1,0:T(8,128)S(1)}, f32[4,256,128]{2,1,0:T(8,128)S(1)}, u32[]{:S(2)}, u32[]{:S(2)}) %collective-permute-start.24) | collective-permute-done | bytes 524320 | tf_op jit(solution)/shard_map/ppermute | solution.py:25
  66.0 2.4 %collective-permute-done.25.refs_1_ = f32[256,128]{1,0:T(8,128)S(1)} collective-permute-done((f32[256,128]{1,0:T(8,128)S(1)}, f32[256,128]{1,0:T(8,128)S(1)}, u32[]{:S(2)}, u32[]{:S(2)}) %collective-permute-start.25) | collective-permute-done | bytes 131104 | tf_op jit(solution)/shard_map/ppermute | solution.py:25
  68.4 4.2 %collective-permute-start.36 = (f32[56,1152]{1,0:T(8,128)S(1)}, f32[56,1152]{1,0:T(8,128)S(1)}, u32[]{:S(2)}, u32[]{:S(2)}) collective-permute-start(f32[56,1152]{1,0:T(8,128)S(1)} %shard_map.88), channel_id=1, source_target_pairs={{0,6},{2,4},{4,2},{6,0},{8,14},{10,12},{12,10},{14,8},{16,22},{18,... | collective-permute-start | bytes 774152 | tf_op jit(solution)/shard_map/ppermute | solution.py:30
  72.6 3.9 %collective-permute-start.38 = (f32[96,1152]{1,0:T(8,128)S(1)}, f32[96,1152]{1,0:T(8,128)S(1)}, u32[]{:S(2)}, u32[]{:S(2)}) collective-permute-start(f32[96,1152]{1,0:T(8,128)S(1)} %shard_map.90), channel_id=1, source_target_pairs={{0,6},{2,4},{4,2},{6,0},{8,14},{10,12},{12,10},{14,8},{16,22},{18,... | collective-permute-start | bytes 1327112 | tf_op jit(solution)/shard_map/ppermute | solution.py:30
  77.2 4.5 %collective-permute-start.33 = (f32[256,128]{1,0:T(8,128)S(1)}, f32[256,128]{1,0:T(8,128)S(1)}, u32[]{:S(2)}, u32[]{:S(2)}) collective-permute-start(f32[256,128]{1,0:T(8,128)S(1)} %shard_map.85.refs_4_), channel_id=1, source_target_pairs={{0,24},{2,26},{4,28},{6,30},{8,16},{10,18},{12,20},{14,22},{16,8},... | collective-permute-start | bytes 393224 | tf_op jit(solution)/shard_map/ppermute | solution.py:25
  82.4 5.8 %collective-permute-start.32 = (f32[256,128]{1,0:T(8,128)S(1)}, f32[256,128]{1,0:T(8,128)S(1)}, u32[]{:S(2)}, u32[]{:S(2)}) collective-permute-start(f32[256,128]{1,0:T(8,128)S(1)} %collective-permute-done.31.refs_8_), channel_id=1, source_target_pairs={{0,4},{2,6},{4,0},{6,2},{8,12},{10,14},{12,8},{14,10},{16,20},{18,... | collective-permute-start | bytes 393224 | tf_op jit(solution)/shard_map/ppermute | solution.py:25
  88.1 3.1 %collective-permute-done.33.refs_0_ = f32[256,128]{1,0:T(8,128)S(1)} collective-permute-done((f32[256,128]{1,0:T(8,128)S(1)}, f32[256,128]{1,0:T(8,128)S(1)}, u32[]{:S(2)}, u32[]{:S(2)}) %collective-permute-start.33) | collective-permute-done | bytes 131104 | tf_op jit(solution)/shard_map/ppermute | solution.py:25
  97.2 2.6 %collective-permute-done.30.refs_7_ = f32[256,128]{1,0:T(8,128)S(1)} collective-permute-done((f32[256,128]{1,0:T(8,128)S(1)}, f32[256,128]{1,0:T(8,128)S(1)}, u32[]{:S(2)}, u32[]{:S(2)}) %collective-permute-start.30) | collective-permute-done | bytes 131104 | tf_op jit(solution)/shard_map/ppermute | solution.py:25
  103.3 2.5 %collective-permute-start.39 = (f32[8,128]{1,0:T(8,128)S(1)}, f32[8,128]{1,0:T(8,128)S(1)}, u32[]{:S(2)}, u32[]{:S(2)}) collective-permute-start(f32[8,128]{1,0:T(8,128)S(1)} %get-tuple-element.82.refs_0_), channel_id=1, source_target_pairs={{0,2},{1,3},{2,0},{3,1},{4,6},{5,7},{6,4},{7,5},{8,10},{9,11},{10,... | collective-permute-start | bytes 12296 | tf_op jit(solution)/shard_map/ppermute | solution.py:61
  118.3 3.4 %collective-permute-start.48 = (f32[256,256]{1,0:T(8,128)S(1)}, f32[256,256]{1,0:T(8,128)S(1)}, u32[]{:S(2)}, u32[]{:S(2)}) collective-permute-start(f32[256,256]{1,0:T(8,128)S(1)} %get-tuple-element.86), channel_id=1, source_target_pairs={{0,2},{2,0},{4,6},{6,4},{8,10},{10,8},{12,14},{14,12},{16,18},{18,... | collective-permute-start | bytes 786440 | tf_op jit(solution)/shard_map/ppermute | solution.py:25
  125.0 3.1 %collective-permute-start.59 = (f32[96,1152]{1,0:T(8,128)S(1)}, f32[96,1152]{1,0:T(8,128)S(1)}, u32[]{:S(2)}, u32[]{:S(2)}) collective-permute-start(f32[96,1152]{1,0:T(8,128)S(1)} %shard_map.105.refs_5_), channel_id=1, source_target_pairs={{0,8},{2,10},{8,16},{10,18},{12,4},{14,6},{16,24},{18,26},{20,12},... | collective-permute-start | bytes 1327112 | tf_op jit(solution)/shard_map/ppermute | solution.py:36
  128.1 2.5 %collective-permute-done.49.refs_1_ = f32[256,256]{1,0:T(8,128)S(1)} collective-permute-done((f32[256,256]{1,0:T(8,128)S(1)}, f32[256,256]{1,0:T(8,128)S(1)}, u32[]{:S(2)}, u32[]{:S(2)}) %collective-permute-start.49) | collective-permute-done | bytes 262176 | tf_op jit(solution)/shard_map/ppermute | solution.py:43
  150.9 6.1 %collective-permute-done.60.refs_1_ = f32[4,256,128]{2,1,0:T(8,128)S(1)} collective-permute-done((f32[4,256,128]{2,1,0:T(8,128)S(1)}, f32[4,256,128]{2,1,0:T(8,128)S(1)}, u32[]{:S(2)}, u32[]{:S(2)}) %collective-permute-start.60) | collective-permute-done | bytes 524320 | tf_op jit(solution)/shard_map/ppermute | solution.py:25
  163.0 5.2 %collective-permute-done.63.refs_3_ = f32[256,128]{1,0:T(8,128)S(1)} collective-permute-done((f32[256,128]{1,0:T(8,128)S(1)}, f32[256,128]{1,0:T(8,128)S(1)}, u32[]{:S(2)}, u32[]{:S(2)}) %collective-permute-start.63) | collective-permute-done | bytes 131104 | tf_op jit(solution)/shard_map/ppermute | solution.py:25
  171.7 5.0 %collective-permute-done.69.refs_0_ = f32[256,128]{1,0:T(8,128)S(1)} collective-permute-done((f32[256,128]{1,0:T(8,128)S(1)}, f32[256,128]{1,0:T(8,128)S(1)}, u32[]{:S(2)}, u32[]{:S(2)}) %collective-permute-start.69) | collective-permute-done | bytes 131104 | tf_op jit(solution)/shard_map/ppermute | solution.py:25
  176.8 4.3 %collective-permute-start.73 = (f32[256,256]{1,0:T(8,128)S(1)}, f32[256,256]{1,0:T(8,128)S(1)}, u32[]{:S(2)}, u32[]{:S(2)}) collective-permute-start(f32[256,256]{1,0:T(8,128)S(1)} %shard_map.112.refs_13_.refs_6_), channel_id=1, source_target_pairs={{0,8},{2,10},{8,16},{10,18},{12,4},{14,6},{16,24},{18,26},{20,12},... | collective-permute-start | bytes 786440 | tf_op jit(solution)/shard_map/ppermute | solution.py:36
  190.6 11.0 %collective-permute-start.74 = (f32[8,128]{1,0:T(8,128)S(1)}, f32[8,128]{1,0:T(8,128)S(1)}, u32[]{:S(2)}, u32[]{:S(2)}) collective-permute-start(f32[8,128]{1,0:T(8,128)S(1)} %get-tuple-element.101.refs_0_), channel_id=1, source_target_pairs={{0,2},{1,3},{2,0},{3,1},{4,6},{5,7},{6,4},{7,5},{8,10},{9,11},{10,... | collective-permute-start | bytes 12296 | tf_op jit(solution)/shard_map/ppermute | solution.py:61
  212.1 3.1 %shard_map.117 = (f32[4,256,1024]{2,1,0:T(8,128)S(1)}, f32[4,256,1024]{2,1,0:T(8,128)S(1)}) custom-call(s32[3]{0:T(128)S(1)} %pad_add_fusion.refs_0_, f32[104,1152]{1,0:T(8,128)S(1)} %shard_map.74.refs_3_.refs_1_, f32[104,1152]{1,0:T(8,128)S(1)} %shard_map.86.refs_2_, f32[48,1152]{1,0:T(8,128)S(1)} %shard_map.95.refs_3_, f32[56,1152]{1,0:T(8,128)S(1)} %shard_map.96.refs_4_, ...), custom_call_target="tpu_custom_call" | custom-call | tf_op jit(solution)/shard_map/pallas_call | solution.py:132
  215.3 10.6 %shard_map.120 = (f32[256,2048]{1,0:T(8,128)}, f32[256,1024]{1,0:T(8,128)S(1)}, f32[2,1024,256]{2,1,0:T(8,128)}) custom-call(s32[3]{0:T(128)S(1)} %pad_add_fusion.refs_0_, f32[8,128]{1,0:T(8,128)S(1)} %shard_map.118.refs_1_, f32[2,256,1024]{2,1,0:T(8,128)S(1)} %bitcast.7, f32[2,256,1024]{2,1,0:T(8,128)S(1)} %bitcast.8, ...), custom_call_target="tpu_custom_call" | custom-call | tf_op jit(solution)/shard_map/pallas_call | solution.py:132
  226.8 2.3 collective-permute-done.85
  (207 shorter events, 122.7 us)
Async XLA Ops:
  8.4 13.2 %collective-permute-start.11 = (f32[104,1152]{1,0:T(8,128)S(1)}, f32[104,1152]{1,0:T(8,128)S(1)}, u32[]{:S(2)}, u32[]{:S(2)}) collective-permute-start(f32[104,1152]{1,0:T(8,128)S(1)} %shard_map.73), channel_id=1, source_target_pairs={{0,4},{2,6},{4,0},{6,2},{8,12},{10,14},{12,8},{14,10},{16,20},{18,... | collective-permute-start | bytes 1437704 | tf_op jit(solution)/shard_map/ppermute | solution.py:30
  27.5 23.8 %collective-permute-start.22 = (f32[104,1152]{1,0:T(8,128)S(1)}, f32[104,1152]{1,0:T(8,128)S(1)}, u32[]{:S(2)}, u32[]{:S(2)}) collective-permute-start(f32[104,1152]{1,0:T(8,128)S(1)} %shard_map.82), channel_id=1, source_target_pairs={{0,4},{2,6},{4,0},{6,2},{8,12},{10,14},{12,8},{14,10},{16,20},{18,... | collective-permute-start | bytes 1437704 | tf_op jit(solution)/shard_map/ppermute | solution.py:30
  28.9 22.3 %collective-permute-start.23 = (f32[104,1152]{1,0:T(8,128)S(1)}, f32[104,1152]{1,0:T(8,128)S(1)}, u32[]{:S(2)}, u32[]{:S(2)}) collective-permute-start(f32[104,1152]{1,0:T(8,128)S(1)} %shard_map.74.refs_3_.refs_1_), channel_id=1, source_target_pairs={{0,8},{2,10},{8,16},{10,18},{12,4},{14,6},{16,24},{18,26},{20,12},... | collective-permute-start | bytes 1437704 | tf_op jit(solution)/shard_map/ppermute | solution.py:36
  52.8 9.9 %collective-permute-start.24 = (f32[4,256,128]{2,1,0:T(8,128)S(1)}, f32[4,256,128]{2,1,0:T(8,128)S(1)}, u32[]{:S(2)}, u32[]{:S(2)}) collective-permute-start(f32[4,256,128]{2,1,0:T(8,128)S(1)} %get-tuple-element.76.refs_1_), channel_id=1, source_target_pairs={{0,4},{2,6},{4,0},{6,2},{8,12},{10,14},{12,8},{14,10},{16,20},{18,... | collective-permute-start | bytes 1572872 | tf_op jit(solution)/shard_map/ppermute | solution.py:25
  53.3 23.9 %collective-permute-start.34 = (f32[104,1152]{1,0:T(8,128)S(1)}, f32[104,1152]{1,0:T(8,128)S(1)}, u32[]{:S(2)}, u32[]{:S(2)}) collective-permute-start(f32[104,1152]{1,0:T(8,128)S(1)} %shard_map.86.refs_2_), channel_id=1, source_target_pairs={{0,8},{2,10},{8,16},{10,18},{12,4},{14,6},{16,24},{18,26},{20,12},... | collective-permute-start | bytes 1437704 | tf_op jit(solution)/shard_map/ppermute | solution.py:36
  64.2 17.6 %collective-permute-start.35 = (f32[48,1152]{1,0:T(8,128)S(1)}, f32[48,1152]{1,0:T(8,128)S(1)}, u32[]{:S(2)}, u32[]{:S(2)}) collective-permute-start(f32[48,1152]{1,0:T(8,128)S(1)} %shard_map.87), channel_id=1, source_target_pairs={{0,4},{2,6},{4,0},{6,2},{8,12},{10,14},{12,8},{14,10},{16,20},{18,... | collective-permute-start | bytes 663560 | tf_op jit(solution)/shard_map/ppermute | solution.py:30
  64.7 11.8 %collective-permute-start.27 = (f32[256,128]{1,0:T(8,128)S(1)}, f32[256,128]{1,0:T(8,128)S(1)}, u32[]{:S(2)}, u32[]{:S(2)}) collective-permute-start(f32[256,128]{1,0:T(8,128)S(1)} %get-tuple-element.80), channel_id=1, source_target_pairs={{0,24},{2,26},{4,28},{6,30},{8,16},{10,18},{12,20},{14,22},{16,8},... | collective-permute-start | bytes 393224 | tf_op jit(solution)/shard_map/ppermute | solution.py:25
  68.4 13.4 %collective-permute-start.36 = (f32[56,1152]{1,0:T(8,128)S(1)}, f32[56,1152]{1,0:T(8,128)S(1)}, u32[]{:S(2)}, u32[]{:S(2)}) collective-permute-start(f32[56,1152]{1,0:T(8,128)S(1)} %shard_map.88), channel_id=1, source_target_pairs={{0,6},{2,4},{4,2},{6,0},{8,14},{10,12},{12,10},{14,8},{16,22},{18,... | collective-permute-start | bytes 774152 | tf_op jit(solution)/shard_map/ppermute | solution.py:30
  72.6 29.4 %collective-permute-start.38 = (f32[96,1152]{1,0:T(8,128)S(1)}, f32[96,1152]{1,0:T(8,128)S(1)}, u32[]{:S(2)}, u32[]{:S(2)}) collective-permute-start(f32[96,1152]{1,0:T(8,128)S(1)} %shard_map.90), channel_id=1, source_target_pairs={{0,6},{2,4},{4,2},{6,0},{8,14},{10,12},{12,10},{14,8},{16,22},{18,... | collective-permute-start | bytes 1327112 | tf_op jit(solution)/shard_map/ppermute | solution.py:30
  77.2 14.0 %collective-permute-start.33 = (f32[256,128]{1,0:T(8,128)S(1)}, f32[256,128]{1,0:T(8,128)S(1)}, u32[]{:S(2)}, u32[]{:S(2)}) collective-permute-start(f32[256,128]{1,0:T(8,128)S(1)} %shard_map.85.refs_4_), channel_id=1, source_target_pairs={{0,24},{2,26},{4,28},{6,30},{8,16},{10,18},{12,20},{14,22},{16,8},... | collective-permute-start | bytes 393224 | tf_op jit(solution)/shard_map/ppermute | solution.py:25
  81.8 11.7 %collective-permute-start.29 = (f32[256,128]{1,0:T(8,128)S(1)}, f32[256,128]{1,0:T(8,128)S(1)}, u32[]{:S(2)}, u32[]{:S(2)}) collective-permute-start(f32[256,128]{1,0:T(8,128)S(1)} %shard_map.85.refs_4_), channel_id=1, source_target_pairs={{0,8},{2,10},{4,12},{6,14},{8,0},{10,2},{12,4},{14,6},{16,24},{18,... | collective-permute-start | bytes 393224 | tf_op jit(solution)/shard_map/ppermute | solution.py:25
  81.8 13.9 %collective-permute-start.28 = (f32[256,128]{1,0:T(8,128)S(1)}, f32[256,128]{1,0:T(8,128)S(1)}, u32[]{:S(2)}, u32[]{:S(2)}) collective-permute-start(f32[256,128]{1,0:T(8,128)S(1)} %shard_map.85.refs_4_), channel_id=1, source_target_pairs={{0,4},{2,6},{4,0},{6,2},{8,12},{10,14},{12,8},{14,10},{16,20},{18,... | collective-permute-start | bytes 393224 | tf_op jit(solution)/shard_map/ppermute | solution.py:25
  82.4 14.6 %collective-permute-start.32 = (f32[256,128]{1,0:T(8,128)S(1)}, f32[256,128]{1,0:T(8,128)S(1)}, u32[]{:S(2)}, u32[]{:S(2)}) collective-permute-start(f32[256,128]{1,0:T(8,128)S(1)} %collective-permute-done.31.refs_8_), channel_id=1, source_target_pairs={{0,4},{2,6},{4,0},{6,2},{8,12},{10,14},{12,8},{14,10},{16,20},{18,... | collective-permute-start | bytes 393224 | tf_op jit(solution)/shard_map/ppermute | solution.py:25
  91.2 25.6 %collective-permute-start.47 = (f32[56,1152]{1,0:T(8,128)S(1)}, f32[56,1152]{1,0:T(8,128)S(1)}, u32[]{:S(2)}, u32[]{:S(2)}) collective-permute-start(f32[56,1152]{1,0:T(8,128)S(1)} %shard_map.96.refs_4_), channel_id=1, source_target_pairs={{0,8},{2,10},{8,16},{10,18},{12,4},{14,6},{16,24},{18,26},{20,12},... | collective-permute-start | bytes 774152 | tf_op jit(solution)/shard_map/ppermute | solution.py:36
  93.5 23.3 %collective-permute-start.46 = (f32[48,1152]{1,0:T(8,128)S(1)}, f32[48,1152]{1,0:T(8,128)S(1)}, u32[]{:S(2)}, u32[]{:S(2)}) collective-permute-start(f32[48,1152]{1,0:T(8,128)S(1)} %shard_map.95.refs_3_), channel_id=1, source_target_pairs={{0,8},{2,10},{8,16},{10,18},{12,4},{14,6},{16,24},{18,26},{20,12},... | collective-permute-start | bytes 663560 | tf_op jit(solution)/shard_map/ppermute | solution.py:36
  123.1 22.6 %collective-permute-start.58 = (f32[104,1152]{1,0:T(8,128)S(1)}, f32[104,1152]{1,0:T(8,128)S(1)}, u32[]{:S(2)}, u32[]{:S(2)}) collective-permute-start(f32[104,1152]{1,0:T(8,128)S(1)} %shard_map.104), channel_id=1, source_target_pairs={{0,6},{2,4},{4,2},{6,0},{8,14},{10,12},{12,10},{14,8},{16,22},{18,... | collective-permute-start | bytes 1437704 | tf_op jit(solution)/shard_map/ppermute | solution.py:30
  125.0 20.7 %collective-permute-start.59 = (f32[96,1152]{1,0:T(8,128)S(1)}, f32[96,1152]{1,0:T(8,128)S(1)}, u32[]{:S(2)}, u32[]{:S(2)}) collective-permute-start(f32[96,1152]{1,0:T(8,128)S(1)} %shard_map.105.refs_5_), channel_id=1, source_target_pairs={{0,8},{2,10},{8,16},{10,18},{12,4},{14,6},{16,24},{18,26},{20,12},... | collective-permute-start | bytes 1327112 | tf_op jit(solution)/shard_map/ppermute | solution.py:36
  148.7 23.0 %collective-permute-start.70 = (f32[104,1152]{1,0:T(8,128)S(1)}, f32[104,1152]{1,0:T(8,128)S(1)}, u32[]{:S(2)}, u32[]{:S(2)}) collective-permute-start(f32[104,1152]{1,0:T(8,128)S(1)} %shard_map.110.refs_6_), channel_id=1, source_target_pairs={{0,8},{2,10},{8,16},{10,18},{12,4},{14,6},{16,24},{18,26},{20,12},... | collective-permute-start | bytes 1437704 | tf_op jit(solution)/shard_map/ppermute | solution.py:36
  159.8 17.0 %collective-permute-start.71 = (f32[256,256]{1,0:T(8,128)S(1)}, f32[256,256]{1,0:T(8,128)S(1)}, u32[]{:S(2)}, u32[]{:S(2)}) collective-permute-start(f32[256,256]{1,0:T(8,128)S(1)} %shard_map.107.refs_0_), channel_id=1, source_target_pairs={{0,4},{2,6},{4,0},{6,2},{8,12},{10,14},{12,8},{14,10},{16,20},{18,... | collective-permute-start | bytes 786440 | tf_op jit(solution)/shard_map/ppermute | solution.py:30
  170.5 10.7 %collective-permute-start.67 = (f32[256,128]{1,0:T(8,128)S(1)}, f32[256,128]{1,0:T(8,128)S(1)}, u32[]{:S(2)}, u32[]{:S(2)}) collective-permute-start(f32[256,128]{1,0:T(8,128)S(1)} %shard_map.109.refs_4_), channel_id=1, source_target_pairs={{0,16},{2,18},{4,20},{6,22},{8,24},{10,26},{12,28},{14,30},{16,0},... | collective-permute-start | bytes 393224 | tf_op jit(solution)/shard_map/ppermute | solution.py:25
  170.5 12.2 %collective-permute-start.65 = (f32[256,128]{1,0:T(8,128)S(1)}, f32[256,128]{1,0:T(8,128)S(1)}, u32[]{:S(2)}, u32[]{:S(2)}) collective-permute-start(f32[256,128]{1,0:T(8,128)S(1)} %shard_map.109.refs_4_), channel_id=1, source_target_pairs={{0,8},{2,10},{4,12},{6,14},{8,0},{10,2},{12,4},{14,6},{16,24},{18,... | collective-permute-start | bytes 393224 | tf_op jit(solution)/shard_map/ppermute | solution.py:25
  176.8 12.4 %collective-permute-start.73 = (f32[256,256]{1,0:T(8,128)S(1)}, f32[256,256]{1,0:T(8,128)S(1)}, u32[]{:S(2)}, u32[]{:S(2)}) collective-permute-start(f32[256,256]{1,0:T(8,128)S(1)} %shard_map.112.refs_13_.refs_6_), channel_id=1, source_target_pairs={{0,8},{2,10},{8,16},{10,18},{12,4},{14,6},{16,24},{18,26},{20,12},... | collective-permute-start | bytes 786440 | tf_op jit(solution)/shard_map/ppermute | solution.py:36
  190.6 11.9 %collective-permute-start.74 = (f32[8,128]{1,0:T(8,128)S(1)}, f32[8,128]{1,0:T(8,128)S(1)}, u32[]{:S(2)}, u32[]{:S(2)}) collective-permute-start(f32[8,128]{1,0:T(8,128)S(1)} %get-tuple-element.101.refs_0_), channel_id=1, source_target_pairs={{0,2},{1,3},{2,0},{3,1},{4,6},{5,7},{6,4},{7,5},{8,10},{9,11},{10,... | collective-permute-start | bytes 12296 | tf_op jit(solution)/shard_map/ppermute | solution.py:61
  205.1 10.1 %collective-permute-start.83 = (f32[256,1024]{1,0:T(8,128)S(1)}, f32[256,1024]{1,0:T(8,128)S(1)}, u32[]{:S(2)}, u32[]{:S(2)}) collective-permute-start(f32[256,1024]{1,0:T(8,128)S(1)} %get-tuple-element.87.refs_2_.refs_10_.refs_13_.refs_17_), channel_id=1, source_target_pairs={{0,2},{2,0},{4,6},{6,4},{8,10},{10,8},{12,14},{14,12},{16,18},{18,... | collective-permute-start | bytes 3145736 | tf_op jit(solution)/shard_map/ppermute | solution.py:25
  (63 other events, 262.9 us)

commit v7 on v6

--- a/solution.py
+++ b/solution.py
@@ -393,7 +393,7 @@
     count = source.shape[0]
     for start in range(0, WIDTH, SPAN):
         row = lax.broadcasted_iota(jnp.int32, (SPAN + 2 * PAD, LANES), 0) + (start - PAD)
-        inside = (row >= 0) & (row < WIDTH - 1)
+        edge = start == 0 or start + SPAN == WIDTH
         around = slice(start, start + SPAN + 2 * PAD)
         middle = slice(PAD, PAD + SPAN)
         before = None
@@ -407,7 +407,8 @@
                 cross = cross * keep_south
             if k > 0:
                 east = flux_of(pltpu.roll(here, SPAN + 2 * PAD - 1, 0) - here)
-                east = jnp.where(inside, east, 0.0)
+                if edge:
+                    east = jnp.where((row >= 0) & (row < WIDTH - 1), east, 0.0)
                 west = pltpu.roll(east, 1, 0)
                 along = east[middle] - west[middle]
                 target(k - 1, start, here[middle] + diffusion * ((cross - before) + along))
@@ -568,7 +569,7 @@
             [local, sums_shape], factor_scratch, own_grad, other_grad, in_vmem(vt), in_vmem(weight),
             beside=[residual],
         )
-        pix_sums = everywhere(sums)
+        pix_sums = everywhere(sums, late=True)
         u_next, other_u, residual, own_u, even, odd = call(
             functools.partial(pix_step_kernel, total, first), [VMEM] * 8, [VMEM] * 6,
             [pix_shape, pix_shape, local, pix_shape, half_shape, half_shape], [pltpu.VMEM((rank, 3 * both), bf16)],

time: 232 us -> 233 us (level)
    ppermute x35, waiting for transfers between devices: 52 us -> 54.6 us  [along_pix(): return lax.ppermute(block, 'pix', [(i, i ^ distance) for i in range(count)])]
where the time goes in v7:
time: 233 us; the launch traced here: 232 us
  starting transfers between devices  120 us (52%)
  waiting for transfers between devices  78.5 us (34%)
  Pallas kernels  30.8 us (13%)
    ppermute x35, waiting for transfers between devices, along_pix(): return lax.ppermute(block, 'pix', [(i, i ^ distance) for i in range(count)])  54.6 us
    ppermute x35, starting transfers between devices, everywhere(): lax.ppermute(sums, ('pix', 'col'), [(i, i ^ move) for i in range(devices)])  44.4 us
    ppermute x35, starting transfers between devices, along_pix(): return lax.ppermute(block, 'pix', [(i, i ^ distance) for i in range(count)])  40.8 us
    pallas_call x36, Pallas kernels, call(): pl.pallas_call(body, grid_spec=pltpu.PrefetchScalarGridSpec(num_scalar_pr...  30.7 us
    ppermute x7, starting transfers between devices, to_far(): lax.ppermute(block, 'pix', [(a, b) for a, b in route if 0 <= b < count])  20.8 us
    ppermute x35, waiting for transfers between devices, everywhere(): lax.ppermute(sums, ('pix', 'col'), [(i, i ^ move) for i in range(devices)])  19.8 us
    ppermute x7, starting transfers between devices, to_near(): lax.ppermute(block, 'pix', [(i, i ^ 2 ^ crossed) for i in range(count)])  13.8 us
  transfers between devices with their start and end apart: 86, of which 48 were waited for; matrix products, arithmetic and copies ran while one was open for 0% of the time, Pallas kernels for 5%

profile of v7, /device:TPU:13, one launch (start us, length us, event | category | flops | bytes accessed | tf_op | source)
XLA Modules:
  0.0 231.6 jit_solution(7052026079141771785)
XLA Ops:
  5.2 3.1 %shard_map.68 = (f32[104,1152]{1,0:T(8,128)S(1)}, f32[104,1152]{1,0:T(8,128)S(1)}, f32[48,1152]{1,0:T(8,128)S(1)}, f32[256,1024]{1,0:T(8,128)S(1)}, f32[256,1024...) custom-call(s32[3]{0:T(128)S(1)} %pad_add_fusion.refs_0_, f32[256,2048]{1,0:T(8,128)} %refs_1_.3, ...), custom_call_target="tpu_custom_call" | custom-call | tf_op jit(solution)/shard_map/pallas_call | solution.py:132
  22.7 3.5 %collective-permute-start.12 = (f32[256,256]{1,0:T(8,128)S(1)}, f32[256,256]{1,0:T(8,128)S(1)}, u32[]{:S(2)}, u32[]{:S(2)}) collective-permute-start(f32[256,256]{1,0:T(8,128)S(1)} %get-tuple-element.67), channel_id=1, source_target_pairs={{0,2},{2,0},{4,6},{6,4},{8,10},{10,8},{12,14},{14,12},{16,18},{18,... | collective-permute-start | bytes 786440 | tf_op jit(solution)/shard_map/ppermute | solution.py:25
  28.9 4.3 %collective-permute-start.23 = (f32[104,1152]{1,0:T(8,128)S(1)}, f32[104,1152]{1,0:T(8,128)S(1)}, u32[]{:S(2)}, u32[]{:S(2)}) collective-permute-start(f32[104,1152]{1,0:T(8,128)S(1)} %shard_map.74.refs_3_.refs_1_), channel_id=1, source_target_pairs={{0,8},{2,10},{8,16},{10,18},{12,4},{14,6},{16,24},{18,26},{20,12},... | collective-permute-start | bytes 1437704 | tf_op jit(solution)/shard_map/ppermute | solution.py:36
  39.8 2.4 %collective-permute-start.18 = (f32[8,128]{1,0:T(8,128)S(1)}, f32[8,128]{1,0:T(8,128)S(1)}, u32[]{:S(2)}, u32[]{:S(2)}) collective-permute-start(f32[8,128]{1,0:T(8,128)S(1)} %shard_map.79.refs_0_), channel_id=1, source_target_pairs={{0,24},{1,25},{2,26},{3,27},{4,28},{5,29},{6,30},{7,31},{8,16},{9,... | collective-permute-start | bytes 12296 | tf_op jit(solution)/shard_map/ppermute | solution.py:61
  55.3 7.7 %collective-permute-done.24.refs_1_ = f32[4,256,128]{2,1,0:T(8,128)S(1)} collective-permute-done((f32[4,256,128]{2,1,0:T(8,128)S(1)}, f32[4,256,128]{2,1,0:T(8,128)S(1)}, u32[]{:S(2)}, u32[]{:S(2)}) %collective-permute-start.24) | collective-permute-done | bytes 524320 | tf_op jit(solution)/shard_map/ppermute | solution.py:25
  66.0 2.7 %collective-permute-done.25.refs_1_ = f32[256,128]{1,0:T(8,128)S(1)} collective-permute-done((f32[256,128]{1,0:T(8,128)S(1)}, f32[256,128]{1,0:T(8,128)S(1)}, u32[]{:S(2)}, u32[]{:S(2)}) %collective-permute-start.25) | collective-permute-done | bytes 131104 | tf_op jit(solution)/shard_map/ppermute | solution.py:25
  68.7 4.6 %collective-permute-start.36 = (f32[56,1152]{1,0:T(8,128)S(1)}, f32[56,1152]{1,0:T(8,128)S(1)}, u32[]{:S(2)}, u32[]{:S(2)}) collective-permute-start(f32[56,1152]{1,0:T(8,128)S(1)} %shard_map.88), channel_id=1, source_target_pairs={{0,6},{2,4},{4,2},{6,0},{8,14},{10,12},{12,10},{14,8},{16,22},{18,... | collective-permute-start | bytes 774152 | tf_op jit(solution)/shard_map/ppermute | solution.py:30
  73.3 3.3 %collective-permute-start.38 = (f32[96,1152]{1,0:T(8,128)S(1)}, f32[96,1152]{1,0:T(8,128)S(1)}, u32[]{:S(2)}, u32[]{:S(2)}) collective-permute-start(f32[96,1152]{1,0:T(8,128)S(1)} %shard_map.90), channel_id=1, source_target_pairs={{0,6},{2,4},{4,2},{6,0},{8,14},{10,12},{12,10},{14,8},{16,22},{18,... | collective-permute-start | bytes 1327112 | tf_op jit(solution)/shard_map/ppermute | solution.py:30
  77.1 4.8 %collective-permute-start.33 = (f32[256,128]{1,0:T(8,128)S(1)}, f32[256,128]{1,0:T(8,128)S(1)}, u32[]{:S(2)}, u32[]{:S(2)}) collective-permute-start(f32[256,128]{1,0:T(8,128)S(1)} %shard_map.85.refs_4_), channel_id=1, source_target_pairs={{0,24},{2,26},{4,28},{6,30},{8,16},{10,18},{12,20},{14,22},{16,8},... | collective-permute-start | bytes 393224 | tf_op jit(solution)/shard_map/ppermute | solution.py:25
  82.3 5.2 %collective-permute-start.32 = (f32[256,128]{1,0:T(8,128)S(1)}, f32[256,128]{1,0:T(8,128)S(1)}, u32[]{:S(2)}, u32[]{:S(2)}) collective-permute-start(f32[256,128]{1,0:T(8,128)S(1)} %collective-permute-done.31.refs_8_), channel_id=1, source_target_pairs={{0,4},{2,6},{4,0},{6,2},{8,12},{10,14},{12,8},{14,10},{16,20},{18,... | collective-permute-start | bytes 393224 | tf_op jit(solution)/shard_map/ppermute | solution.py:25
  87.5 3.8 %collective-permute-done.33.refs_0_ = f32[256,128]{1,0:T(8,128)S(1)} collective-permute-done((f32[256,128]{1,0:T(8,128)S(1)}, f32[256,128]{1,0:T(8,128)S(1)}, u32[]{:S(2)}, u32[]{:S(2)}) %collective-permute-start.33) | collective-permute-done | bytes 131104 | tf_op jit(solution)/shard_map/ppermute | solution.py:25
  91.3 2.4 %collective-permute-start.47 = (f32[56,1152]{1,0:T(8,128)S(1)}, f32[56,1152]{1,0:T(8,128)S(1)}, u32[]{:S(2)}, u32[]{:S(2)}) collective-permute-start(f32[56,1152]{1,0:T(8,128)S(1)} %shard_map.96.refs_4_), channel_id=1, source_target_pairs={{0,8},{2,10},{8,16},{10,18},{12,4},{14,6},{16,24},{18,26},{20,12},... | collective-permute-start | bytes 774152 | tf_op jit(solution)/shard_map/ppermute | solution.py:36
  97.6 2.6 %collective-permute-done.30.refs_7_ = f32[256,128]{1,0:T(8,128)S(1)} collective-permute-done((f32[256,128]{1,0:T(8,128)S(1)}, f32[256,128]{1,0:T(8,128)S(1)}, u32[]{:S(2)}, u32[]{:S(2)}) %collective-permute-start.30) | collective-permute-done | bytes 131104 | tf_op jit(solution)/shard_map/ppermute | solution.py:25
  100.2 2.5 %collective-permute-done.37.refs_11_ = f32[256,128]{1,0:T(8,128)S(1)} collective-permute-done((f32[256,128]{1,0:T(8,128)S(1)}, f32[256,128]{1,0:T(8,128)S(1)}, u32[]{:S(2)}, u32[]{:S(2)}) %collective-permute-start.37) | collective-permute-done | bytes 131104 | tf_op jit(solution)/shard_map/ppermute | solution.py:25
  119.0 3.4 %collective-permute-start.48 = (f32[256,256]{1,0:T(8,128)S(1)}, f32[256,256]{1,0:T(8,128)S(1)}, u32[]{:S(2)}, u32[]{:S(2)}) collective-permute-start(f32[256,256]{1,0:T(8,128)S(1)} %get-tuple-element.86), channel_id=1, source_target_pairs={{0,2},{2,0},{4,6},{6,4},{8,10},{10,8},{12,14},{14,12},{16,18},{18,... | collective-permute-start | bytes 786440 | tf_op jit(solution)/shard_map/ppermute | solution.py:25
  125.4 3.6 %collective-permute-start.59 = (f32[96,1152]{1,0:T(8,128)S(1)}, f32[96,1152]{1,0:T(8,128)S(1)}, u32[]{:S(2)}, u32[]{:S(2)}) collective-permute-start(f32[96,1152]{1,0:T(8,128)S(1)} %shard_map.105.refs_5_), channel_id=1, source_target_pairs={{0,8},{2,10},{8,16},{10,18},{12,4},{14,6},{16,24},{18,26},{20,12},... | collective-permute-start | bytes 1327112 | tf_op jit(solution)/shard_map/ppermute | solution.py:36
  135.9 2.6 %collective-permute-start.54 = (f32[8,128]{1,0:T(8,128)S(1)}, f32[8,128]{1,0:T(8,128)S(1)}, u32[]{:S(2)}, u32[]{:S(2)}) collective-permute-start(f32[8,128]{1,0:T(8,128)S(1)} %shard_map.101.refs_0_), channel_id=1, source_target_pairs={{0,24},{1,25},{2,26},{3,27},{4,28},{5,29},{6,30},{7,31},{8,16},{9,... | collective-permute-start | bytes 12296 | tf_op jit(solution)/shard_map/ppermute | solution.py:61
  151.7 6.4 %collective-permute-done.60.refs_1_ = f32[4,256,128]{2,1,0:T(8,128)S(1)} collective-permute-done((f32[4,256,128]{2,1,0:T(8,128)S(1)}, f32[4,256,128]{2,1,0:T(8,128)S(1)}, u32[]{:S(2)}, u32[]{:S(2)}) %collective-permute-start.60) | collective-permute-done | bytes 524320 | tf_op jit(solution)/shard_map/ppermute | solution.py:25
  164.0 7.0 %collective-permute-done.63.refs_3_ = f32[256,128]{1,0:T(8,128)S(1)} collective-permute-done((f32[256,128]{1,0:T(8,128)S(1)}, f32[256,128]{1,0:T(8,128)S(1)}, u32[]{:S(2)}, u32[]{:S(2)}) %collective-permute-start.63) | collective-permute-done | bytes 131104 | tf_op jit(solution)/shard_map/ppermute | solution.py:25
  173.7 3.9 %collective-permute-done.69.refs_0_ = f32[256,128]{1,0:T(8,128)S(1)} collective-permute-done((f32[256,128]{1,0:T(8,128)S(1)}, f32[256,128]{1,0:T(8,128)S(1)}, u32[]{:S(2)}, u32[]{:S(2)}) %collective-permute-start.69) | collective-permute-done | bytes 131104 | tf_op jit(solution)/shard_map/ppermute | solution.py:25
  177.7 4.3 %collective-permute-start.73 = (f32[256,256]{1,0:T(8,128)S(1)}, f32[256,256]{1,0:T(8,128)S(1)}, u32[]{:S(2)}, u32[]{:S(2)}) collective-permute-start(f32[256,256]{1,0:T(8,128)S(1)} %shard_map.112.refs_13_.refs_6_), channel_id=1, source_target_pairs={{0,8},{2,10},{8,16},{10,18},{12,4},{14,6},{16,24},{18,26},{20,12},... | collective-permute-start | bytes 786440 | tf_op jit(solution)/shard_map/ppermute | solution.py:36
  191.5 11.6 %collective-permute-start.74 = (f32[8,128]{1,0:T(8,128)S(1)}, f32[8,128]{1,0:T(8,128)S(1)}, u32[]{:S(2)}, u32[]{:S(2)}) collective-permute-start(f32[8,128]{1,0:T(8,128)S(1)} %get-tuple-element.101.refs_0_), channel_id=1, source_target_pairs={{0,2},{1,3},{2,0},{3,1},{4,6},{5,7},{6,4},{7,5},{8,10},{9,11},{10,... | collective-permute-start | bytes 12296 | tf_op jit(solution)/shard_map/ppermute | solution.py:61
  213.6 3.1 %shard_map.117 = (f32[4,256,1024]{2,1,0:T(8,128)S(1)}, f32[4,256,1024]{2,1,0:T(8,128)S(1)}) custom-call(s32[3]{0:T(128)S(1)} %pad_add_fusion.refs_0_, f32[104,1152]{1,0:T(8,128)S(1)} %shard_map.74.refs_3_.refs_1_, f32[104,1152]{1,0:T(8,128)S(1)} %shard_map.86.refs_2_, f32[48,1152]{1,0:T(8,128)S(1)} %shard_map.95.refs_3_, f32[56,1152]{1,0:T(8,128)S(1)} %shard_map.96.refs_4_, ...), custom_call_target="tpu_custom_call" | custom-call | tf_op jit(solution)/shard_map/pallas_call | solution.py:132
  216.7 10.6 %shard_map.120 = (f32[256,2048]{1,0:T(8,128)}, f32[256,1024]{1,0:T(8,128)S(1)}, f32[2,1024,256]{2,1,0:T(8,128)}) custom-call(s32[3]{0:T(128)S(1)} %pad_add_fusion.refs_0_, f32[8,128]{1,0:T(8,128)S(1)} %shard_map.118.refs_1_, f32[2,256,1024]{2,1,0:T(8,128)S(1)} %bitcast.7, f32[2,256,1024]{2,1,0:T(8,128)S(1)} %bitcast.8, ...), custom_call_target="tpu_custom_call" | custom-call | tf_op jit(solution)/shard_map/pallas_call | solution.py:132
  (207 shorter events, 121.3 us)
Async XLA Ops:
  8.4 13.2 %collective-permute-start.11 = (f32[104,1152]{1,0:T(8,128)S(1)}, f32[104,1152]{1,0:T(8,128)S(1)}, u32[]{:S(2)}, u32[]{:S(2)}) collective-permute-start(f32[104,1152]{1,0:T(8,128)S(1)} %shard_map.73), channel_id=1, source_target_pairs={{0,4},{2,6},{4,0},{6,2},{8,12},{10,14},{12,8},{14,10},{16,20},{18,... | collective-permute-start | bytes 1437704 | tf_op jit(solution)/shard_map/ppermute | solution.py:30
  27.5 23.9 %collective-permute-start.22 = (f32[104,1152]{1,0:T(8,128)S(1)}, f32[104,1152]{1,0:T(8,128)S(1)}, u32[]{:S(2)}, u32[]{:S(2)}) collective-permute-start(f32[104,1152]{1,0:T(8,128)S(1)} %shard_map.82), channel_id=1, source_target_pairs={{0,4},{2,6},{4,0},{6,2},{8,12},{10,14},{12,8},{14,10},{16,20},{18,... | collective-permute-start | bytes 1437704 | tf_op jit(solution)/shard_map/ppermute | solution.py:30
  28.9 22.5 %collective-permute-start.23 = (f32[104,1152]{1,0:T(8,128)S(1)}, f32[104,1152]{1,0:T(8,128)S(1)}, u32[]{:S(2)}, u32[]{:S(2)}) collective-permute-start(f32[104,1152]{1,0:T(8,128)S(1)} %shard_map.74.refs_3_.refs_1_), channel_id=1, source_target_pairs={{0,8},{2,10},{8,16},{10,18},{12,4},{14,6},{16,24},{18,26},{20,12},... | collective-permute-start | bytes 1437704 | tf_op jit(solution)/shard_map/ppermute | solution.py:36
  53.3 23.9 %collective-permute-start.34 = (f32[104,1152]{1,0:T(8,128)S(1)}, f32[104,1152]{1,0:T(8,128)S(1)}, u32[]{:S(2)}, u32[]{:S(2)}) collective-permute-start(f32[104,1152]{1,0:T(8,128)S(1)} %shard_map.86.refs_2_), channel_id=1, source_target_pairs={{0,8},{2,10},{8,16},{10,18},{12,4},{14,6},{16,24},{18,26},{20,12},... | collective-permute-start | bytes 1437704 | tf_op jit(solution)/shard_map/ppermute | solution.py:36
  64.3 17.6 %collective-permute-start.35 = (f32[48,1152]{1,0:T(8,128)S(1)}, f32[48,1152]{1,0:T(8,128)S(1)}, u32[]{:S(2)}, u32[]{:S(2)}) collective-permute-start(f32[48,1152]{1,0:T(8,128)S(1)} %shard_map.87), channel_id=1, source_target_pairs={{0,4},{2,6},{4,0},{6,2},{8,12},{10,14},{12,8},{14,10},{16,20},{18,... | collective-permute-start | bytes 663560 | tf_op jit(solution)/shard_map/ppermute | solution.py:30
  64.5 12.0 %collective-permute-start.27 = (f32[256,128]{1,0:T(8,128)S(1)}, f32[256,128]{1,0:T(8,128)S(1)}, u32[]{:S(2)}, u32[]{:S(2)}) collective-permute-start(f32[256,128]{1,0:T(8,128)S(1)} %get-tuple-element.80), channel_id=1, source_target_pairs={{0,24},{2,26},{4,28},{6,30},{8,16},{10,18},{12,20},{14,22},{16,8},... | collective-permute-start | bytes 393224 | tf_op jit(solution)/shard_map/ppermute | solution.py:25
  68.7 13.3 %collective-permute-start.36 = (f32[56,1152]{1,0:T(8,128)S(1)}, f32[56,1152]{1,0:T(8,128)S(1)}, u32[]{:S(2)}, u32[]{:S(2)}) collective-permute-start(f32[56,1152]{1,0:T(8,128)S(1)} %shard_map.88), channel_id=1, source_target_pairs={{0,6},{2,4},{4,2},{6,0},{8,14},{10,12},{12,10},{14,8},{16,22},{18,... | collective-permute-start | bytes 774152 | tf_op jit(solution)/shard_map/ppermute | solution.py:30
  73.3 29.4 %collective-permute-start.38 = (f32[96,1152]{1,0:T(8,128)S(1)}, f32[96,1152]{1,0:T(8,128)S(1)}, u32[]{:S(2)}, u32[]{:S(2)}) collective-permute-start(f32[96,1152]{1,0:T(8,128)S(1)} %shard_map.90), channel_id=1, source_target_pairs={{0,6},{2,4},{4,2},{6,0},{8,14},{10,12},{12,10},{14,8},{16,22},{18,... | collective-permute-start | bytes 1327112 | tf_op jit(solution)/shard_map/ppermute | solution.py:30
  77.1 14.2 %collective-permute-start.33 = (f32[256,128]{1,0:T(8,128)S(1)}, f32[256,128]{1,0:T(8,128)S(1)}, u32[]{:S(2)}, u32[]{:S(2)}) collective-permute-start(f32[256,128]{1,0:T(8,128)S(1)} %shard_map.85.refs_4_), channel_id=1, source_target_pairs={{0,24},{2,26},{4,28},{6,30},{8,16},{10,18},{12,20},{14,22},{16,8},... | collective-permute-start | bytes 393224 | tf_op jit(solution)/shard_map/ppermute | solution.py:25
  81.9 11.8 %collective-permute-start.29 = (f32[256,128]{1,0:T(8,128)S(1)}, f32[256,128]{1,0:T(8,128)S(1)}, u32[]{:S(2)}, u32[]{:S(2)}) collective-permute-start(f32[256,128]{1,0:T(8,128)S(1)} %shard_map.85.refs_4_), channel_id=1, source_target_pairs={{0,8},{2,10},{4,12},{6,14},{8,0},{10,2},{12,4},{14,6},{16,24},{18,... | collective-permute-start | bytes 393224 | tf_op jit(solution)/shard_map/ppermute | solution.py:25
  81.9 13.9 %collective-permute-start.28 = (f32[256,128]{1,0:T(8,128)S(1)}, f32[256,128]{1,0:T(8,128)S(1)}, u32[]{:S(2)}, u32[]{:S(2)}) collective-permute-start(f32[256,128]{1,0:T(8,128)S(1)} %shard_map.85.refs_4_), channel_id=1, source_target_pairs={{0,4},{2,6},{4,0},{6,2},{8,12},{10,14},{12,8},{14,10},{16,20},{18,... | collective-permute-start | bytes 393224 | tf_op jit(solution)/shard_map/ppermute | solution.py:25
  82.3 15.2 %collective-permute-start.32 = (f32[256,128]{1,0:T(8,128)S(1)}, f32[256,128]{1,0:T(8,128)S(1)}, u32[]{:S(2)}, u32[]{:S(2)}) collective-permute-start(f32[256,128]{1,0:T(8,128)S(1)} %collective-permute-done.31.refs_8_), channel_id=1, source_target_pairs={{0,4},{2,6},{4,0},{6,2},{8,12},{10,14},{12,8},{14,10},{16,20},{18,... | collective-permute-start | bytes 393224 | tf_op jit(solution)/shard_map/ppermute | solution.py:25
  91.3 26.2 %collective-permute-start.47 = (f32[56,1152]{1,0:T(8,128)S(1)}, f32[56,1152]{1,0:T(8,128)S(1)}, u32[]{:S(2)}, u32[]{:S(2)}) collective-permute-start(f32[56,1152]{1,0:T(8,128)S(1)} %shard_map.96.refs_4_), channel_id=1, source_target_pairs={{0,8},{2,10},{8,16},{10,18},{12,4},{14,6},{16,24},{18,26},{20,12},... | collective-permute-start | bytes 774152 | tf_op jit(solution)/shard_map/ppermute | solution.py:36
  93.7 23.7 %collective-permute-start.46 = (f32[48,1152]{1,0:T(8,128)S(1)}, f32[48,1152]{1,0:T(8,128)S(1)}, u32[]{:S(2)}, u32[]{:S(2)}) collective-permute-start(f32[48,1152]{1,0:T(8,128)S(1)} %shard_map.95.refs_3_), channel_id=1, source_target_pairs={{0,8},{2,10},{8,16},{10,18},{12,4},{14,6},{16,24},{18,26},{20,12},... | collective-permute-start | bytes 663560 | tf_op jit(solution)/shard_map/ppermute | solution.py:36
  123.9 22.6 %collective-permute-start.58 = (f32[104,1152]{1,0:T(8,128)S(1)}, f32[104,1152]{1,0:T(8,128)S(1)}, u32[]{:S(2)}, u32[]{:S(2)}) collective-permute-start(f32[104,1152]{1,0:T(8,128)S(1)} %shard_map.104), channel_id=1, source_target_pairs={{0,6},{2,4},{4,2},{6,0},{8,14},{10,12},{12,10},{14,8},{16,22},{18,... | collective-permute-start | bytes 1437704 | tf_op jit(solution)/shard_map/ppermute | solution.py:30
  125.4 21.1 %collective-permute-start.59 = (f32[96,1152]{1,0:T(8,128)S(1)}, f32[96,1152]{1,0:T(8,128)S(1)}, u32[]{:S(2)}, u32[]{:S(2)}) collective-permute-start(f32[96,1152]{1,0:T(8,128)S(1)} %shard_map.105.refs_5_), channel_id=1, source_target_pairs={{0,8},{2,10},{8,16},{10,18},{12,4},{14,6},{16,24},{18,26},{20,12},... | collective-permute-start | bytes 1327112 | tf_op jit(solution)/shard_map/ppermute | solution.py:36
  149.6 24.1 %collective-permute-start.70 = (f32[104,1152]{1,0:T(8,128)S(1)}, f32[104,1152]{1,0:T(8,128)S(1)}, u32[]{:S(2)}, u32[]{:S(2)}) collective-permute-start(f32[104,1152]{1,0:T(8,128)S(1)} %shard_map.110.refs_6_), channel_id=1, source_target_pairs={{0,8},{2,10},{8,16},{10,18},{12,4},{14,6},{16,24},{18,26},{20,12},... | collective-permute-start | bytes 1437704 | tf_op jit(solution)/shard_map/ppermute | solution.py:36
  159.7 11.3 %collective-permute-start.63 = (f32[256,128]{1,0:T(8,128)S(1)}, f32[256,128]{1,0:T(8,128)S(1)}, u32[]{:S(2)}, u32[]{:S(2)}) collective-permute-start(f32[256,128]{1,0:T(8,128)S(1)} %get-tuple-element.100), channel_id=1, source_target_pairs={{0,24},{2,26},{4,28},{6,30},{8,16},{10,18},{12,20},{14,22},{16,8},... | collective-permute-start | bytes 393224 | tf_op jit(solution)/shard_map/ppermute | solution.py:25
  160.9 16.8 %collective-permute-start.71 = (f32[256,256]{1,0:T(8,128)S(1)}, f32[256,256]{1,0:T(8,128)S(1)}, u32[]{:S(2)}, u32[]{:S(2)}) collective-permute-start(f32[256,256]{1,0:T(8,128)S(1)} %shard_map.107.refs_0_), channel_id=1, source_target_pairs={{0,4},{2,6},{4,0},{6,2},{8,12},{10,14},{12,8},{14,10},{16,20},{18,... | collective-permute-start | bytes 786440 | tf_op jit(solution)/shard_map/ppermute | solution.py:30
  171.1 11.0 %collective-permute-start.67 = (f32[256,128]{1,0:T(8,128)S(1)}, f32[256,128]{1,0:T(8,128)S(1)}, u32[]{:S(2)}, u32[]{:S(2)}) collective-permute-start(f32[256,128]{1,0:T(8,128)S(1)} %shard_map.109.refs_4_), channel_id=1, source_target_pairs={{0,16},{2,18},{4,20},{6,22},{8,24},{10,26},{12,28},{14,30},{16,0},... | collective-permute-start | bytes 393224 | tf_op jit(solution)/shard_map/ppermute | solution.py:25
  171.4 12.1 %collective-permute-start.65 = (f32[256,128]{1,0:T(8,128)S(1)}, f32[256,128]{1,0:T(8,128)S(1)}, u32[]{:S(2)}, u32[]{:S(2)}) collective-permute-start(f32[256,128]{1,0:T(8,128)S(1)} %shard_map.109.refs_4_), channel_id=1, source_target_pairs={{0,8},{2,10},{4,12},{6,14},{8,0},{10,2},{12,4},{14,6},{16,24},{18,... | collective-permute-start | bytes 393224 | tf_op jit(solution)/shard_map/ppermute | solution.py:25
  177.7 12.4 %collective-permute-start.73 = (f32[256,256]{1,0:T(8,128)S(1)}, f32[256,256]{1,0:T(8,128)S(1)}, u32[]{:S(2)}, u32[]{:S(2)}) collective-permute-start(f32[256,256]{1,0:T(8,128)S(1)} %shard_map.112.refs_13_.refs_6_), channel_id=1, source_target_pairs={{0,8},{2,10},{8,16},{10,18},{12,4},{14,6},{16,24},{18,26},{20,12},... | collective-permute-start | bytes 786440 | tf_op jit(solution)/shard_map/ppermute | solution.py:36
  191.5 12.4 %collective-permute-start.74 = (f32[8,128]{1,0:T(8,128)S(1)}, f32[8,128]{1,0:T(8,128)S(1)}, u32[]{:S(2)}, u32[]{:S(2)}) collective-permute-start(f32[8,128]{1,0:T(8,128)S(1)} %get-tuple-element.101.refs_0_), channel_id=1, source_target_pairs={{0,2},{1,3},{2,0},{3,1},{4,6},{5,7},{6,4},{7,5},{8,10},{9,11},{10,... | collective-permute-start | bytes 12296 | tf_op jit(solution)/shard_map/ppermute | solution.py:61
  206.6 10.1 %collective-permute-start.83 = (f32[256,1024]{1,0:T(8,128)S(1)}, f32[256,1024]{1,0:T(8,128)S(1)}, u32[]{:S(2)}, u32[]{:S(2)}) collective-permute-start(f32[256,1024]{1,0:T(8,128)S(1)} %get-tuple-element.87.refs_2_.refs_10_.refs_13_.refs_17_), channel_id=1, source_target_pairs={{0,2},{2,0},{4,6},{6,4},{8,10},{10,8},{12,14},{14,12},{16,18},{18,... | collective-permute-start | bytes 3145736 | tf_op jit(solution)/shard_map/ppermute | solution.py:25
  (63 other events, 263.1 us)

commit v8 on v7

--- a/solution.py
+++ b/solution.py
@@ -569,7 +569,7 @@
             [local, sums_shape], factor_scratch, own_grad, other_grad, in_vmem(vt), in_vmem(weight),
             beside=[residual],
         )
-        pix_sums = everywhere(sums, late=True)
+        pix_sums = everywhere(sums)
         u_next, other_u, residual, own_u, even, odd = call(
             functools.partial(pix_step_kernel, total, first), [VMEM] * 8, [VMEM] * 6,
             [pix_shape, pix_shape, local, pix_shape, half_shape, half_shape], [pltpu.VMEM((rank, 3 * both), bf16)],

time: 233 us -> 232 us (level)
    ppermute x35, waiting for transfers between devices: 54.6 us -> 52 us  [along_pix(): return lax.ppermute(block, 'pix', [(i, i ^ distance) for i in range(count)])]
where the time goes in v8:
time: 232 us; the launch traced here: 230 us
  starting transfers between devices  120 us (52%)
  waiting for transfers between devices  76.7 us (33%)
  Pallas kernels  30.8 us (13%)
    ppermute x35, waiting for transfers between devices, along_pix(): return lax.ppermute(block, 'pix', [(i, i ^ distance) for i in range(count)])  52 us
    ppermute x35, starting transfers between devices, everywhere(): lax.ppermute(sums, ('pix', 'col'), [(i, i ^ move) for i in range(devices)])  42.9 us
    ppermute x35, starting transfers between devices, along_pix(): return lax.ppermute(block, 'pix', [(i, i ^ distance) for i in range(count)])  42.1 us
    pallas_call x36, Pallas kernels, call(): pl.pallas_call(body, grid_spec=pltpu.PrefetchScalarGridSpec(num_scalar_pr...  30.7 us
    ppermute x35, waiting for transfers between devices, everywhere(): lax.ppermute(sums, ('pix', 'col'), [(i, i ^ move) for i in range(devices)])  20.5 us
    ppermute x7, starting transfers between devices, to_far(): lax.ppermute(block, 'pix', [(a, b) for a, b in route if 0 <= b < count])  20.4 us
    ppermute x7, starting transfers between devices, to_near(): lax.ppermute(block, 'pix', [(i, i ^ 2 ^ crossed) for i in range(count)])  14.7 us
  transfers between devices with their start and end apart: 86, of which 48 were waited for; matrix products, arithmetic and copies ran while one was open for 0% of the time, Pallas kernels for 5%

profile of v8, /device:TPU:13, one launch (start us, length us, event | category | flops | bytes accessed | tf_op | source)
XLA Modules:
  0.0 230.1 jit_solution(1931270949630132356)
XLA Ops:
  5.2 3.1 %shard_map.68 = (f32[104,1152]{1,0:T(8,128)S(1)}, f32[104,1152]{1,0:T(8,128)S(1)}, f32[48,1152]{1,0:T(8,128)S(1)}, f32[256,1024]{1,0:T(8,128)S(1)}, f32[256,1024...) custom-call(s32[3]{0:T(128)S(1)} %pad_add_fusion.refs_0_, f32[256,2048]{1,0:T(8,128)} %refs_1_.3, ...), custom_call_target="tpu_custom_call" | custom-call | tf_op jit(solution)/shard_map/pallas_call | solution.py:132
  22.7 3.5 %collective-permute-start.12 = (f32[256,256]{1,0:T(8,128)S(1)}, f32[256,256]{1,0:T(8,128)S(1)}, u32[]{:S(2)}, u32[]{:S(2)}) collective-permute-start(f32[256,256]{1,0:T(8,128)S(1)} %get-tuple-element.67), channel_id=1, source_target_pairs={{0,2},{2,0},{4,6},{6,4},{8,10},{10,8},{12,14},{14,12},{16,18},{18,... | collective-permute-start | bytes 786440 | tf_op jit(solution)/shard_map/ppermute | solution.py:25
  28.9 4.3 %collective-permute-start.23 = (f32[104,1152]{1,0:T(8,128)S(1)}, f32[104,1152]{1,0:T(8,128)S(1)}, u32[]{:S(2)}, u32[]{:S(2)}) collective-permute-start(f32[104,1152]{1,0:T(8,128)S(1)} %shard_map.74.refs_3_.refs_1_), channel_id=1, source_target_pairs={{0,8},{2,10},{8,16},{10,18},{12,4},{14,6},{16,24},{18,26},{20,12},... | collective-permute-start | bytes 1437704 | tf_op jit(solution)/shard_map/ppermute | solution.py:36
  44.8 2.4 %collective-permute-start.21 = (f32[8,128]{1,0:T(8,128)S(1)}, f32[8,128]{1,0:T(8,128)S(1)}, u32[]{:S(2)}, u32[]{:S(2)}) collective-permute-start(f32[8,128]{1,0:T(8,128)S(1)} %shard_map.80.refs_0_), channel_id=1, source_target_pairs={{0,24},{1,25},{2,26},{3,27},{4,28},{5,29},{6,30},{7,31},{8,16},{9,... | collective-permute-start | bytes 12296 | tf_op jit(solution)/shard_map/ppermute | solution.py:61
  55.4 7.3 %collective-permute-done.24.refs_1_ = f32[4,256,128]{2,1,0:T(8,128)S(1)} collective-permute-done((f32[4,256,128]{2,1,0:T(8,128)S(1)}, f32[4,256,128]{2,1,0:T(8,128)S(1)}, u32[]{:S(2)}, u32[]{:S(2)}) %collective-permute-start.24) | collective-permute-done | bytes 524320 | tf_op jit(solution)/shard_map/ppermute | solution.py:25
  66.0 2.4 %collective-permute-done.25.refs_1_ = f32[256,128]{1,0:T(8,128)S(1)} collective-permute-done((f32[256,128]{1,0:T(8,128)S(1)}, f32[256,128]{1,0:T(8,128)S(1)}, u32[]{:S(2)}, u32[]{:S(2)}) %collective-permute-start.25) | collective-permute-done | bytes 131104 | tf_op jit(solution)/shard_map/ppermute | solution.py:25
  68.4 4.2 %collective-permute-start.36 = (f32[56,1152]{1,0:T(8,128)S(1)}, f32[56,1152]{1,0:T(8,128)S(1)}, u32[]{:S(2)}, u32[]{:S(2)}) collective-permute-start(f32[56,1152]{1,0:T(8,128)S(1)} %shard_map.88), channel_id=1, source_target_pairs={{0,6},{2,4},{4,2},{6,0},{8,14},{10,12},{12,10},{14,8},{16,22},{18,... | collective-permute-start | bytes 774152 | tf_op jit(solution)/shard_map/ppermute | solution.py:30
  72.6 3.9 %collective-permute-start.38 = (f32[96,1152]{1,0:T(8,128)S(1)}, f32[96,1152]{1,0:T(8,128)S(1)}, u32[]{:S(2)}, u32[]{:S(2)}) collective-permute-start(f32[96,1152]{1,0:T(8,128)S(1)} %shard_map.90), channel_id=1, source_target_pairs={{0,6},{2,4},{4,2},{6,0},{8,14},{10,12},{12,10},{14,8},{16,22},{18,... | collective-permute-start | bytes 1327112 | tf_op jit(solution)/shard_map/ppermute | solution.py:30
  77.2 4.5 %collective-permute-start.33 = (f32[256,128]{1,0:T(8,128)S(1)}, f32[256,128]{1,0:T(8,128)S(1)}, u32[]{:S(2)}, u32[]{:S(2)}) collective-permute-start(f32[256,128]{1,0:T(8,128)S(1)} %shard_map.85.refs_4_), channel_id=1, source_target_pairs={{0,24},{2,26},{4,28},{6,30},{8,16},{10,18},{12,20},{14,22},{16,8},... | collective-permute-start | bytes 393224 | tf_op jit(solution)/shard_map/ppermute | solution.py:25
  82.4 5.8 %collective-permute-start.32 = (f32[256,128]{1,0:T(8,128)S(1)}, f32[256,128]{1,0:T(8,128)S(1)}, u32[]{:S(2)}, u32[]{:S(2)}) collective-permute-start(f32[256,128]{1,0:T(8,128)S(1)} %collective-permute-done.31.refs_8_), channel_id=1, source_target_pairs={{0,4},{2,6},{4,0},{6,2},{8,12},{10,14},{12,8},{14,10},{16,20},{18,... | collective-permute-start | bytes 393224 | tf_op jit(solution)/shard_map/ppermute | solution.py:25
  88.1 3.1 %collective-permute-done.33.refs_0_ = f32[256,128]{1,0:T(8,128)S(1)} collective-permute-done((f32[256,128]{1,0:T(8,128)S(1)}, f32[256,128]{1,0:T(8,128)S(1)}, u32[]{:S(2)}, u32[]{:S(2)}) %collective-permute-start.33) | collective-permute-done | bytes 131104 | tf_op jit(solution)/shard_map/ppermute | solution.py:25
  97.2 2.6 %collective-permute-done.30.refs_7_ = f32[256,128]{1,0:T(8,128)S(1)} collective-permute-done((f32[256,128]{1,0:T(8,128)S(1)}, f32[256,128]{1,0:T(8,128)S(1)}, u32[]{:S(2)}, u32[]{:S(2)}) %collective-permute-start.30) | collective-permute-done | bytes 131104 | tf_op jit(solution)/shard_map/ppermute | solution.py:25
  103.3 2.5 %collective-permute-start.39 = (f32[8,128]{1,0:T(8,128)S(1)}, f32[8,128]{1,0:T(8,128)S(1)}, u32[]{:S(2)}, u32[]{:S(2)}) collective-permute-start(f32[8,128]{1,0:T(8,128)S(1)} %get-tuple-element.82.refs_0_), channel_id=1, source_target_pairs={{0,2},{1,3},{2,0},{3,1},{4,6},{5,7},{6,4},{7,5},{8,10},{9,11},{10,... | collective-permute-start | bytes 12296 | tf_op jit(solution)/shard_map/ppermute | solution.py:61
  118.3 3.4 %collective-permute-start.48 = (f32[256,256]{1,0:T(8,128)S(1)}, f32[256,256]{1,0:T(8,128)S(1)}, u32[]{:S(2)}, u32[]{:S(2)}) collective-permute-start(f32[256,256]{1,0:T(8,128)S(1)} %get-tuple-element.86), channel_id=1, source_target_pairs={{0,2},{2,0},{4,6},{6,4},{8,10},{10,8},{12,14},{14,12},{16,18},{18,... | collective-permute-start | bytes 786440 | tf_op jit(solution)/shard_map/ppermute | solution.py:25
  125.0 3.1 %collective-permute-start.59 = (f32[96,1152]{1,0:T(8,128)S(1)}, f32[96,1152]{1,0:T(8,128)S(1)}, u32[]{:S(2)}, u32[]{:S(2)}) collective-permute-start(f32[96,1152]{1,0:T(8,128)S(1)} %shard_map.105.refs_5_), channel_id=1, source_target_pairs={{0,8},{2,10},{8,16},{10,18},{12,4},{14,6},{16,24},{18,26},{20,12},... | collective-permute-start | bytes 1327112 | tf_op jit(solution)/shard_map/ppermute | solution.py:36
  128.1 2.5 %collective-permute-done.49.refs_1_ = f32[256,256]{1,0:T(8,128)S(1)} collective-permute-done((f32[256,256]{1,0:T(8,128)S(1)}, f32[256,256]{1,0:T(8,128)S(1)}, u32[]{:S(2)}, u32[]{:S(2)}) %collective-permute-start.49) | collective-permute-done | bytes 262176 | tf_op jit(solution)/shard_map/ppermute | solution.py:43
  150.9 6.1 %collective-permute-done.60.refs_1_ = f32[4,256,128]{2,1,0:T(8,128)S(1)} collective-permute-done((f32[4,256,128]{2,1,0:T(8,128)S(1)}, f32[4,256,128]{2,1,0:T(8,128)S(1)}, u32[]{:S(2)}, u32[]{:S(2)}) %collective-permute-start.60) | collective-permute-done | bytes 524320 | tf_op jit(solution)/shard_map/ppermute | solution.py:25
  163.0 5.2 %collective-permute-done.63.refs_3_ = f32[256,128]{1,0:T(8,128)S(1)} collective-permute-done((f32[256,128]{1,0:T(8,128)S(1)}, f32[256,128]{1,0:T(8,128)S(1)}, u32[]{:S(2)}, u32[]{:S(2)}) %collective-permute-start.63) | collective-permute-done | bytes 131104 | tf_op jit(solution)/shard_map/ppermute | solution.py:25
  171.7 5.0 %collective-permute-done.69.refs_0_ = f32[256,128]{1,0:T(8,128)S(1)} collective-permute-done((f32[256,128]{1,0:T(8,128)S(1)}, f32[256,128]{1,0:T(8,128)S(1)}, u32[]{:S(2)}, u32[]{:S(2)}) %collective-permute-start.69) | collective-permute-done | bytes 131104 | tf_op jit(solution)/shard_map/ppermute | solution.py:25
  176.8 4.3 %collective-permute-start.73 = (f32[256,256]{1,0:T(8,128)S(1)}, f32[256,256]{1,0:T(8,128)S(1)}, u32[]{:S(2)}, u32[]{:S(2)}) collective-permute-start(f32[256,256]{1,0:T(8,128)S(1)} %shard_map.112.refs_13_.refs_6_), channel_id=1, source_target_pairs={{0,8},{2,10},{8,16},{10,18},{12,4},{14,6},{16,24},{18,26},{20,12},... | collective-permute-start | bytes 786440 | tf_op jit(solution)/shard_map/ppermute | solution.py:36
  190.6 11.0 %collective-permute-start.74 = (f32[8,128]{1,0:T(8,128)S(1)}, f32[8,128]{1,0:T(8,128)S(1)}, u32[]{:S(2)}, u32[]{:S(2)}) collective-permute-start(f32[8,128]{1,0:T(8,128)S(1)} %get-tuple-element.101.refs_0_), channel_id=1, source_target_pairs={{0,2},{1,3},{2,0},{3,1},{4,6},{5,7},{6,4},{7,5},{8,10},{9,11},{10,... | collective-permute-start | bytes 12296 | tf_op jit(solution)/shard_map/ppermute | solution.py:61
  212.1 3.1 %shard_map.117 = (f32[4,256,1024]{2,1,0:T(8,128)S(1)}, f32[4,256,1024]{2,1,0:T(8,128)S(1)}) custom-call(s32[3]{0:T(128)S(1)} %pad_add_fusion.refs_0_, f32[104,1152]{1,0:T(8,128)S(1)} %shard_map.74.refs_3_.refs_1_, f32[104,1152]{1,0:T(8,128)S(1)} %shard_map.86.refs_2_, f32[48,1152]{1,0:T(8,128)S(1)} %shard_map.95.refs_3_, f32[56,1152]{1,0:T(8,128)S(1)} %shard_map.96.refs_4_, ...), custom_call_target="tpu_custom_call" | custom-call | tf_op jit(solution)/shard_map/pallas_call | solution.py:132
  215.3 10.6 %shard_map.120 = (f32[256,2048]{1,0:T(8,128)}, f32[256,1024]{1,0:T(8,128)S(1)}, f32[2,1024,256]{2,1,0:T(8,128)}) custom-call(s32[3]{0:T(128)S(1)} %pad_add_fusion.refs_0_, f32[8,128]{1,0:T(8,128)S(1)} %shard_map.118.refs_1_, f32[2,256,1024]{2,1,0:T(8,128)S(1)} %bitcast.7, f32[2,256,1024]{2,1,0:T(8,128)S(1)} %bitcast.8, ...), custom_call_target="tpu_custom_call" | custom-call | tf_op jit(solution)/shard_map/pallas_call | solution.py:132
  226.8 2.3 collective-permute-done.85
  (207 shorter events, 122.7 us)
Async XLA Ops:
  8.4 13.2 %collective-permute-start.11 = (f32[104,1152]{1,0:T(8,128)S(1)}, f32[104,1152]{1,0:T(8,128)S(1)}, u32[]{:S(2)}, u32[]{:S(2)}) collective-permute-start(f32[104,1152]{1,0:T(8,128)S(1)} %shard_map.73), channel_id=1, source_target_pairs={{0,4},{2,6},{4,0},{6,2},{8,12},{10,14},{12,8},{14,10},{16,20},{18,... | collective-permute-start | bytes 1437704 | tf_op jit(solution)/shard_map/ppermute | solution.py:30
  27.5 23.8 %collective-permute-start.22 = (f32[104,1152]{1,0:T(8,128)S(1)}, f32[104,1152]{1,0:T(8,128)S(1)}, u32[]{:S(2)}, u32[]{:S(2)}) collective-permute-start(f32[104,1152]{1,0:T(8,128)S(1)} %shard_map.82), channel_id=1, source_target_pairs={{0,4},{2,6},{4,0},{6,2},{8,12},{10,14},{12,8},{14,10},{16,20},{18,... | collective-permute-start | bytes 1437704 | tf_op jit(solution)/shard_map/ppermute | solution.py:30
  28.9 22.3 %collective-permute-start.23 = (f32[104,1152]{1,0:T(8,128)S(1)}, f32[104,1152]{1,0:T(8,128)S(1)}, u32[]{:S(2)}, u32[]{:S(2)}) collective-permute-start(f32[104,1152]{1,0:T(8,128)S(1)} %shard_map.74.refs_3_.refs_1_), channel_id=1, source_target_pairs={{0,8},{2,10},{8,16},{10,18},{12,4},{14,6},{16,24},{18,26},{20,12},... | collective-permute-start | bytes 1437704 | tf_op jit(solution)/shard_map/ppermute | solution.py:36
  52.8 9.9 %collective-permute-start.24 = (f32[4,256,128]{2,1,0:T(8,128)S(1)}, f32[4,256,128]{2,1,0:T(8,128)S(1)}, u32[]{:S(2)}, u32[]{:S(2)}) collective-permute-start(f32[4,256,128]{2,1,0:T(8,128)S(1)} %get-tuple-element.76.refs_1_), channel_id=1, source_target_pairs={{0,4},{2,6},{4,0},{6,2},{8,12},{10,14},{12,8},{14,10},{16,20},{18,... | collective-permute-start | bytes 1572872 | tf_op jit(solution)/shard_map/ppermute | solution.py:25
  53.3 23.9 %collective-permute-start.34 = (f32[104,1152]{1,0:T(8,128)S(1)}, f32[104,1152]{1,0:T(8,128)S(1)}, u32[]{:S(2)}, u32[]{:S(2)}) collective-permute-start(f32[104,1152]{1,0:T(8,128)S(1)} %shard_map.86.refs_2_), channel_id=1, source_target_pairs={{0,8},{2,10},{8,16},{10,18},{12,4},{14,6},{16,24},{18,26},{20,12},... | collective-permute-start | bytes 1437704 | tf_op jit(solution)/shard_map/ppermute | solution.py:36
  64.2 17.6 %collective-permute-start.35 = (f32[48,1152]{1,0:T(8,128)S(1)}, f32[48,1152]{1,0:T(8,128)S(1)}, u32[]{:S(2)}, u32[]{:S(2)}) collective-permute-start(f32[48,1152]{1,0:T(8,128)S(1)} %shard_map.87), channel_id=1, source_target_pairs={{0,4},{2,6},{4,0},{6,2},{8,12},{10,14},{12,8},{14,10},{16,20},{18,... | collective-permute-start | bytes 663560 | tf_op jit(solution)/shard_map/ppermute | solution.py:30
  64.7 11.8 %collective-permute-start.27 = (f32[256,128]{1,0:T(8,128)S(1)}, f32[256,128]{1,0:T(8,128)S(1)}, u32[]{:S(2)}, u32[]{:S(2)}) collective-permute-start(f32[256,128]{1,0:T(8,128)S(1)} %get-tuple-element.80), channel_id=1, source_target_pairs={{0,24},{2,26},{4,28},{6,30},{8,16},{10,18},{12,20},{14,22},{16,8},... | collective-permute-start | bytes 393224 | tf_op jit(solution)/shard_map/ppermute | solution.py:25
  68.4 13.4 %collective-permute-start.36 = (f32[56,1152]{1,0:T(8,128)S(1)}, f32[56,1152]{1,0:T(8,128)S(1)}, u32[]{:S(2)}, u32[]{:S(2)}) collective-permute-start(f32[56,1152]{1,0:T(8,128)S(1)} %shard_map.88), channel_id=1, source_target_pairs={{0,6},{2,4},{4,2},{6,0},{8,14},{10,12},{12,10},{14,8},{16,22},{18,... | collective-permute-start | bytes 774152 | tf_op jit(solution)/shard_map/ppermute | solution.py:30
  72.6 29.4 %collective-permute-start.38 = (f32[96,1152]{1,0:T(8,128)S(1)}, f32[96,1152]{1,0:T(8,128)S(1)}, u32[]{:S(2)}, u32[]{:S(2)}) collective-permute-start(f32[96,1152]{1,0:T(8,128)S(1)} %shard_map.90), channel_id=1, source_target_pairs={{0,6},{2,4},{4,2},{6,0},{8,14},{10,12},{12,10},{14,8},{16,22},{18,... | collective-permute-start | bytes 1327112 | tf_op jit(solution)/shard_map/ppermute | solution.py:30
  77.2 14.0 %collective-permute-start.33 = (f32[256,128]{1,0:T(8,128)S(1)}, f32[256,128]{1,0:T(8,128)S(1)}, u32[]{:S(2)}, u32[]{:S(2)}) collective-permute-start(f32[256,128]{1,0:T(8,128)S(1)} %shard_map.85.refs_4_), channel_id=1, source_target_pairs={{0,24},{2,26},{4,28},{6,30},{8,16},{10,18},{12,20},{14,22},{16,8},... | collective-permute-start | bytes 393224 | tf_op jit(solution)/shard_map/ppermute | solution.py:25
  81.8 11.7 %collective-permute-start.29 = (f32[256,128]{1,0:T(8,128)S(1)}, f32[256,128]{1,0:T(8,128)S(1)}, u32[]{:S(2)}, u32[]{:S(2)}) collective-permute-start(f32[256,128]{1,0:T(8,128)S(1)} %shard_map.85.refs_4_), channel_id=1, source_target_pairs={{0,8},{2,10},{4,12},{6,14},{8,0},{10,2},{12,4},{14,6},{16,24},{18,... | collective-permute-start | bytes 393224 | tf_op jit(solution)/shard_map/ppermute | solution.py:25
  81.8 13.9 %collective-permute-start.28 = (f32[256,128]{1,0:T(8,128)S(1)}, f32[256,128]{1,0:T(8,128)S(1)}, u32[]{:S(2)}, u32[]{:S(2)}) collective-permute-start(f32[256,128]{1,0:T(8,128)S(1)} %shard_map.85.refs_4_), channel_id=1, source_target_pairs={{0,4},{2,6},{4,0},{6,2},{8,12},{10,14},{12,8},{14,10},{16,20},{18,... | collective-permute-start | bytes 393224 | tf_op jit(solution)/shard_map/ppermute | solution.py:25
  82.4 14.6 %collective-permute-start.32 = (f32[256,128]{1,0:T(8,128)S(1)}, f32[256,128]{1,0:T(8,128)S(1)}, u32[]{:S(2)}, u32[]{:S(2)}) collective-permute-start(f32[256,128]{1,0:T(8,128)S(1)} %collective-permute-done.31.refs_8_), channel_id=1, source_target_pairs={{0,4},{2,6},{4,0},{6,2},{8,12},{10,14},{12,8},{14,10},{16,20},{18,... | collective-permute-start | bytes 393224 | tf_op jit(solution)/shard_map/ppermute | solution.py:25
  91.2 25.6 %collective-permute-start.47 = (f32[56,1152]{1,0:T(8,128)S(1)}, f32[56,1152]{1,0:T(8,128)S(1)}, u32[]{:S(2)}, u32[]{:S(2)}) collective-permute-start(f32[56,1152]{1,0:T(8,128)S(1)} %shard_map.96.refs_4_), channel_id=1, source_target_pairs={{0,8},{2,10},{8,16},{10,18},{12,4},{14,6},{16,24},{18,26},{20,12},... | collective-permute-start | bytes 774152 | tf_op jit(solution)/shard_map/ppermute | solution.py:36
  93.5 23.3 %collective-permute-start.46 = (f32[48,1152]{1,0:T(8,128)S(1)}, f32[48,1152]{1,0:T(8,128)S(1)}, u32[]{:S(2)}, u32[]{:S(2)}) collective-permute-start(f32[48,1152]{1,0:T(8,128)S(1)} %shard_map.95.refs_3_), channel_id=1, source_target_pairs={{0,8},{2,10},{8,16},{10,18},{12,4},{14,6},{16,24},{18,26},{20,12},... | collective-permute-start | bytes 663560 | tf_op jit(solution)/shard_map/ppermute | solution.py:36
  123.1 22.6 %collective-permute-start.58 = (f32[104,1152]{1,0:T(8,128)S(1)}, f32[104,1152]{1,0:T(8,128)S(1)}, u32[]{:S(2)}, u32[]{:S(2)}) collective-permute-start(f32[104,1152]{1,0:T(8,128)S(1)} %shard_map.104), channel_id=1, source_target_pairs={{0,6},{2,4},{4,2},{6,0},{8,14},{10,12},{12,10},{14,8},{16,22},{18,... | collective-permute-start | bytes 1437704 | tf_op jit(solution)/shard_map/ppermute | solution.py:30
  125.0 20.7 %collective-permute-start.59 = (f32[96,1152]{1,0:T(8,128)S(1)}, f32[96,1152]{1,0:T(8,128)S(1)}, u32[]{:S(2)}, u32[]{:S(2)}) collective-permute-start(f32[96,1152]{1,0:T(8,128)S(1)} %shard_map.105.refs_5_), channel_id=1, source_target_pairs={{0,8},{2,10},{8,16},{10,18},{12,4},{14,6},{16,24},{18,26},{20,12},... | collective-permute-start | bytes 1327112 | tf_op jit(solution)/shard_map/ppermute | solution.py:36
  148.7 23.0 %collective-permute-start.70 = (f32[104,1152]{1,0:T(8,128)S(1)}, f32[104,1152]{1,0:T(8,128)S(1)}, u32[]{:S(2)}, u32[]{:S(2)}) collective-permute-start(f32[104,1152]{1,0:T(8,128)S(1)} %shard_map.110.refs_6_), channel_id=1, source_target_pairs={{0,8},{2,10},{8,16},{10,18},{12,4},{14,6},{16,24},{18,26},{20,12},... | collective-permute-start | bytes 1437704 | tf_op jit(solution)/shard_map/ppermute | solution.py:36
  159.8 17.0 %collective-permute-start.71 = (f32[256,256]{1,0:T(8,128)S(1)}, f32[256,256]{1,0:T(8,128)S(1)}, u32[]{:S(2)}, u32[]{:S(2)}) collective-permute-start(f32[256,256]{1,0:T(8,128)S(1)} %shard_map.107.refs_0_), channel_id=1, source_target_pairs={{0,4},{2,6},{4,0},{6,2},{8,12},{10,14},{12,8},{14,10},{16,20},{18,... | collective-permute-start | bytes 786440 | tf_op jit(solution)/shard_map/ppermute | solution.py:30
  170.5 10.7 %collective-permute-start.67 = (f32[256,128]{1,0:T(8,128)S(1)}, f32[256,128]{1,0:T(8,128)S(1)}, u32[]{:S(2)}, u32[]{:S(2)}) collective-permute-start(f32[256,128]{1,0:T(8,128)S(1)} %shard_map.109.refs_4_), channel_id=1, source_target_pairs={{0,16},{2,18},{4,20},{6,22},{8,24},{10,26},{12,28},{14,30},{16,0},... | collective-permute-start | bytes 393224 | tf_op jit(solution)/shard_map/ppermute | solution.py:25
  170.5 12.2 %collective-permute-start.65 = (f32[256,128]{1,0:T(8,128)S(1)}, f32[256,128]{1,0:T(8,128)S(1)}, u32[]{:S(2)}, u32[]{:S(2)}) collective-permute-start(f32[256,128]{1,0:T(8,128)S(1)} %shard_map.109.refs_4_), channel_id=1, source_target_pairs={{0,8},{2,10},{4,12},{6,14},{8,0},{10,2},{12,4},{14,6},{16,24},{18,... | collective-permute-start | bytes 393224 | tf_op jit(solution)/shard_map/ppermute | solution.py:25
  176.8 12.4 %collective-permute-start.73 = (f32[256,256]{1,0:T(8,128)S(1)}, f32[256,256]{1,0:T(8,128)S(1)}, u32[]{:S(2)}, u32[]{:S(2)}) collective-permute-start(f32[256,256]{1,0:T(8,128)S(1)} %shard_map.112.refs_13_.refs_6_), channel_id=1, source_target_pairs={{0,8},{2,10},{8,16},{10,18},{12,4},{14,6},{16,24},{18,26},{20,12},... | collective-permute-start | bytes 786440 | tf_op jit(solution)/shard_map/ppermute | solution.py:36
  190.6 11.9 %collective-permute-start.74 = (f32[8,128]{1,0:T(8,128)S(1)}, f32[8,128]{1,0:T(8,128)S(1)}, u32[]{:S(2)}, u32[]{:S(2)}) collective-permute-start(f32[8,128]{1,0:T(8,128)S(1)} %get-tuple-element.101.refs_0_), channel_id=1, source_target_pairs={{0,2},{1,3},{2,0},{3,1},{4,6},{5,7},{6,4},{7,5},{8,10},{9,11},{10,... | collective-permute-start | bytes 12296 | tf_op jit(solution)/shard_map/ppermute | solution.py:61
  205.1 10.1 %collective-permute-start.83 = (f32[256,1024]{1,0:T(8,128)S(1)}, f32[256,1024]{1,0:T(8,128)S(1)}, u32[]{:S(2)}, u32[]{:S(2)}) collective-permute-start(f32[256,1024]{1,0:T(8,128)S(1)} %get-tuple-element.87.refs_2_.refs_10_.refs_13_.refs_17_), channel_id=1, source_target_pairs={{0,2},{2,0},{4,6},{6,4},{8,10},{10,8},{12,14},{14,12},{16,18},{18,... | collective-permute-start | bytes 3145736 | tf_op jit(solution)/shard_map/ppermute | solution.py:25
  (63 other events, 262.9 us)
